TPU v7x, 512 devices: a whole 4x4x16 slice. The times are simulated.
512 devices in a mesh: aux: 128 (over y, x_hi, z), pair: 4 (over x_lo, core).
Axes of the slice: x: 4 (x_hi: 2, x_lo: 2; x = x_hi * 2 + x_lo), y: 4, z: 16, core: 2. Of those that a mesh axis runs over, the one named last changes fastest.
Arguments:
- coeffs: bfloat16 [32768, 8192], P('aux', 'pair'), may hold values from -1 to 1
- occ_index: int32 [8192], P('pair'), may hold values from 0 to 1999
- vir_index: int32 [8192], P('pair'), may hold values from 0 to 19999
- eps_occ: float32 [2000], replicated, may hold values from -3 to -0.5
- eps_vir: float32 [20000], replicated, may hold values from 0.2 to 4
- frequencies: float32 [2], replicated, may hold values from 0.2 to 2
- offset: int32 [1], replicated, may hold values from 0 to 240
Outputs:
- polar: float32 [2048, 2, 32768], P('pair', None, 'aux')
All inputs are finite; a program needn't handle non-finite values.
Results may differ from a plain program's by a relative error of at most 0.0026.
Values may be sent and summed in bfloat16 or wider, within the bound.
No kernel may reach another device: no remote copies, remote signals or barrier semaphores. Data moves between devices by JAX's collectives and lax.ppermute only.
A program may use at most 64 MiB of HBM per device.

v0:
```python
import jax
import jax.numpy as jnp
from jax import lax
from jax.sharding import PartitionSpec as P

ROWS_DEV = 16


def on_device(coeffs, occ_index, vir_index, eps_occ, eps_vir, frequencies, offset):
    aux_local = coeffs.shape[0]
    energy_gap = jnp.take(eps_vir, vir_index) - jnp.take(eps_occ, occ_index)
    squares = frequencies * frequencies
    response = (
        2.0 * energy_gap[None, :] / (energy_gap[None, :] * energy_gap[None, :] + squares[:, None])
    )
    scaled = (coeffs[None, :, :].astype(jnp.float32) * response[:, None, :]).astype(jnp.bfloat16)
    scaled = scaled.reshape(2 * aux_local, coeffs.shape[1])
    local_rows = lax.dynamic_slice_in_dim(coeffs, offset[0], ROWS_DEV, 0)
    partial_window = lax.dot_general(
        lax.all_gather(local_rows[:, None, :], "aux", axis=1, tiled=True),
        scaled,
        (((2,), (1,)), ((), ())),
        preferred_element_type=jnp.float32,
    )
    partial_window = partial_window.reshape(
        partial_window.shape[0] * partial_window.shape[1], 2, aux_local
    )
    polar = lax.psum_scatter(partial_window, "pair", scatter_dimension=0, tiled=True)
    return polar


def solution(mesh):
    return jax.shard_map(
        on_device,
        mesh=mesh,
        in_specs=(P("aux", "pair"), P("pair"), P("pair"), P(), P(), P(), P()),
        out_specs=P("pair", None, "aux"),
        check_vma=False,
    )
```

profile of v0, /device:TPU:1, one launch (start us, length us, event | category | flops | bytes accessed | tf_op | source)
XLA Modules:
  0.0 340.4 jit_solution(14727506362813309454)
XLA Ops:
  6.5 0.0 copy-start
  6.5 0.0 all-gather.3.cloned.1.call-start
  7.2 1.6 constant_dynamic-slice_fusion
  8.8 0.0 all-gather.3.cloned.1.call-update
  8.8 0.0 reduce-scatter.2.cloned.1.call-start
  8.9 1.5 convert_element_type.9
  10.3 0.7 fusion.3
  11.0 0.0 copy-done
  11.0 0.0 copy-start.2
  11.0 0.0 copy-start.1
  11.0 11.8 %gather_fusion = f32[2048]{0:T(1024)S(1)} fusion(f32[20000]{0:T(1024)S(1)} %copy-done, s32[2048]{0:T(1024)S(1)} %fusion.3), kind=kCustom, calls=%fused_computation | custom fusion | bytes 24576 | tf_op jit(solution)/shard_map/jit(_take)/gather | solution.py:11
  22.8 0.0 copy-done.2
  22.9 0.0 copy-done.1
  22.9 0.0 copy-start.3
  22.9 0.0 copy-start.4
  22.9 11.8 %gather_fusion.1 = f32[2048]{0:T(1024)S(1)} fusion(f32[2000]{0:T(1024)S(1)} %copy-done.1, s32[2048]{0:T(1024)S(1)} %fusion.4), kind=kCustom, calls=%fused_computation.1 | custom fusion | bytes 24576 | tf_op jit(solution)/shard_map/jit(_take)/gather | solution.py:11
  34.7 0.0 copy-done.3
  34.7 0.0 copy-done.4
  34.7 0.1 add_divide_fusion
  34.8 221.7 %all-gather.3.cloned.1.call-done = bf16[16,262144]{1,0:T(8,128)(2,1)} async-done(((bf16[16,2048]{1,0:T(8,128)(2,1)}), bf16[16,262144]{1,0:T(8,128)(2,1)}) %all-gather.3.cloned.1.call-update) | async-done | bytes 8388624 | tf_op jit(solution)/shard_map/all_gather | solution.py:20
  256.6 8.0 %reshape.94 = bf16[2048,2048,1]{1,0,2:T(8,128)(2,1)} reshape(bf16[16,262144]{1,0:T(8,128)(2,1)} %all-gather.3.cloned.1.call-done) | data formatting | bytes 16777216 | tf_op jit(solution)/shard_map/dot_general | solution.py:19
  264.5 9.5 %fusion = f32[2048,2,256]{2,0,1:T(8,128)} fusion(bf16[2048,2048,1]{1,0,2:T(8,128)(2,1)} %reshape.94, f32[2,2048]{1,0:T(2,128)S(1)} %add_divide_fusion, f32[256,2048]{1,0:T(8,128)S(1)} %convert_element_type.9), kind=kOutput, calls=%fused_computation.3 | convolution fusion | flops 4297064448 | bytes 14696448 | tf_op jit(solution)/shard_map/dot_general | solution.py:19
  274.1 0.0 reduce-scatter.2.cloned.1.call-update
  274.1 56.5 %reduce-scatter.2.cloned.1.call-done = f32[512,2,256]{2,0,1:T(8,128)} async-done(((f32[2048,2,256]{2,0,1:T(8,128)}), f32[512,2,256]{2,0,1:T(8,128)}) %reduce-scatter.2.cloned.1.call-update) | async-done | bytes 1048592 | tf_op jit(solution)/shard_map/reduce_scatter | solution.py:28
  330.6 3.0 copy.9
  (4 shorter events, 0.0 us)
Async XLA Ops:
  6.5 4.5 %copy-start = (f32[20000]{0:T(1024)S(1)}, f32[20000]{0:T(1024)}, u32[]{:S(2)}) copy-start(f32[20000]{0:T(1024)} %param.11) | copy-start | bytes 240004
  6.5 250.0 %all-gather.3.cloned.1.call-start = ((), (), s32[]{:S(2)}) async-start(), calls=%async_computation.2 | async-start | bytes 8454144 | tf_op jit(solution)/shard_map/all_gather | solution.py:20
  8.8 321.8 %reduce-scatter.2.cloned.1.call-start = ((), (), s32[]{:S(2)}) async-start(), calls=%async_computation.1 | async-start | bytes 5242880 | tf_op jit(solution)/shard_map/reduce_scatter | solution.py:28
  11.0 11.8 %copy-start.2 = (s32[2048]{0:T(1024)S(1)}, s32[2048]{0:T(1024)}, u32[]{:S(2)}) copy-start(s32[2048]{0:T(1024)} %param.8) | copy-start | bytes 24580
  11.0 11.8 %copy-start.1 = (f32[2000]{0:T(1024)S(1)}, f32[2000]{0:T(1024)}, u32[]{:S(2)}) copy-start(f32[2000]{0:T(1024)} %param.10) | copy-start | bytes 24004
  22.9 11.8 %copy-start.3 = (s32[2048]{0:T(1024)S(1)}, s32[2048]{0:T(1024)}, u32[]{:S(2)}) copy-start(s32[2048]{0:T(1024)} %param.9) | copy-start | bytes 24580
  22.9 11.8 %copy-start.4 = (f32[2]{0:T(128)S(1)}, f32[2]{0:T(128)}, u32[]{:S(2)}) copy-start(f32[2]{0:T(128)} %param.12) | copy-start | bytes 28
Sparse Core Ops, SparseCore 0:
  11.8 244.7 all-gather.2
  274.2 56.3 reduce-scatter.1
where the time goes:
time: 341 us; the launch traced here: 340 us
  waiting for transfers between devices  278 us (82%)
  local copies, waits for them, and re-layouts  36.1 us (11%)
  between operations  14.2 us (4%)
  matrix products  9.53 us (3%)
    all_gather x1, waiting for transfers between devices, on_device(): lax.all_gather(local_rows[:, None, :], 'aux', axis=1, tiled=True)  222 us
    reduce_scatter x1, waiting for transfers between devices, on_device(): lax.psum_scatter(partial_window, 'pair', scatter_dimension=0, tiled=True)  56.5 us
    gather x2, local copies, waits for them, and re-layouts, on_device(): energy_gap = jnp.take(eps_vir, vir_index) - jnp.take(eps_occ, occ_index)  23.6 us
    dot_general x1, matrix products, on_device(): lax.dot_general(lax.all_gather(local_rows[:, None, :], 'aux', axis=1, til...  9.53 us
    dot_general x1, local copies, waits for them, and re-layouts, on_device(): lax.dot_general(lax.all_gather(local_rows[:, None, :], 'aux', axis=1, til...  7.96 us
  transfers between devices with their start and end apart: 2, of which 2 were waited for; matrix products, arithmetic and copies ran while one was open for 8% of the time, Pallas kernels for 0%

commit v1 on v0

v1 whole, which is shorter than its diff:
```python
import functools

import jax
import jax.numpy as jnp
from jax import lax
from jax.experimental import pallas as pl
from jax.experimental.pallas import tpu as pltpu
from jax.sharding import Mesh
from jax.sharding import PartitionSpec as P

ROWS_DEV = 16
LANES = 128


def lookup(table, index):
    rows = -(-table.shape[0] // LANES)
    rows += -rows % 8
    grid = jnp.pad(table, (0, rows * LANES - table.shape[0])).reshape(rows, LANES)
    high = (index // LANES)[:, None] == jnp.arange(rows, dtype=jnp.int32)[None, :]
    low = (index % LANES)[:, None] == jnp.arange(LANES, dtype=jnp.int32)[None, :]
    picked = lax.dot_general(
        high.astype(jnp.float32),
        grid,
        (((1,), (0,)), ((), ())),
        precision=lax.Precision.HIGHEST,
        preferred_element_type=jnp.float32,
    )
    return jnp.sum(jnp.where(low, picked, 0.0), axis=1)


def product_kernel(own_ref, partner_ref, scaled_ref, out_ref):
    scaled = scaled_ref[0]
    depth = scaled.shape[-1]
    for side, ref in enumerate((own_ref, partner_ref)):
        rows = ref[...].reshape(-1, depth)
        product = lax.dot_general(
            rows, scaled, (((1,), (1,)), ((), ())), preferred_element_type=jnp.float32
        )
        product = product.reshape(ref.shape[0], 2, ref.shape[1] // 2, product.shape[-1])
        out_ref[0, 0, side] = product[:, 0]
        out_ref[0, 1, side] = product[:, 1]


def products(own, partner, scaled):
    n_z, n_rows, depth = own.shape
    n_y, columns, _ = scaled.shape
    block = (1, 2, 2, n_z, n_rows // 2, columns)
    whole = pl.BlockSpec((n_z, n_rows, depth), lambda y: (0, 0, 0))
    return pl.pallas_call(
        product_kernel,
        grid=(n_y,),
        in_specs=[whole, whole, pl.BlockSpec((1, columns, depth), lambda y: (y, 0, 0))],
        out_specs=pl.BlockSpec(block, lambda y: (y, 0, 0, 0, 0, 0)),
        out_shape=jax.ShapeDtypeStruct((n_y,) + block[1:], jnp.float32),
        compiler_params=pltpu.CompilerParams(vmem_limit_bytes=40 * 1024 * 1024),
        cost_estimate=pl.CostEstimate(
            flops=4 * n_z * n_rows * depth * columns * n_y,
            bytes_accessed=2 * columns * n_y * depth,
            transcendentals=0,
        ),
    )(own, partner, scaled)


def on_device(n_y, n_z, coeffs, occ_index, vir_index, eps_occ, eps_vir, frequencies, offset):
    aux_local, depth = coeffs.shape
    core = lax.axis_index("core")
    x_hi = lax.axis_index("x_hi")

    coeffs_y = lax.all_gather(coeffs, "y", axis=0)

    local_rows = lax.dynamic_slice_in_dim(coeffs, offset[0], ROWS_DEV, 0)
    local_rows = local_rows.reshape(2, 2, ROWS_DEV // 4, depth)
    first, second = local_rows[:, 0], local_rows[:, 1]
    parts = [jnp.where(core == 0, second, first), jnp.where(core == 0, first, second)]

    own = []
    for part in parts:
        part = part.reshape(1, ROWS_DEV // 2, depth)
        part = jnp.broadcast_to(part, (n_z,) + part.shape[1:])
        own.append(lax.all_to_all(part, "z", 0, 0, tiled=True))
    partner = [lax.ppermute(part, "x_hi", [(0, 1), (1, 0)]) for part in own]

    occ_index, vir_index, _ = lax.optimization_barrier((occ_index, vir_index, own[1]))
    energy_gap = lookup(eps_vir, vir_index) - lookup(eps_occ, occ_index)
    squares = frequencies * frequencies
    response = (
        2.0 * energy_gap[None, :] / (energy_gap[None, :] * energy_gap[None, :] + squares[:, None])
    )
    scaled = (coeffs_y[:, None].astype(jnp.float32) * response[None, :, None, :]).astype(
        jnp.bfloat16
    )
    scaled = scaled.reshape(n_y, 2 * aux_local, depth)

    away = products(own[0], partner[0], scaled)
    arrived = lax.ppermute(away, "core", [(0, 1), (1, 0)])
    kept = products(own[1], partner[1], scaled)
    total = (kept + arrived).reshape(n_y * 2, 2 * n_z * ROWS_DEV // 4, 2 * aux_local)
    total = lax.all_to_all(total, ("y", "x_lo"), 0, 0, tiled=True)
    total = total.reshape(n_y, 2, 2, n_z, ROWS_DEV // 4, 2, aux_local)
    total = total[:, 0] + total[:, 1]
    total = jnp.where(x_hi == 0, total, total[:, ::-1])
    polar = jnp.transpose(total, (3, 0, 1, 2, 4, 5))
    return polar.reshape(-1, 2, aux_local)


def solution(mesh):
    n_y = 4
    n_z = mesh.shape["aux"] // (2 * n_y)
    split = Mesh(
        mesh.devices.reshape(n_y, 2, n_z, 2, 2), ("y", "x_hi", "z", "x_lo", "core")
    )
    aux, pair = ("y", "x_hi", "z"), ("x_lo", "core")
    return jax.shard_map(
        functools.partial(on_device, n_y, n_z),
        mesh=split,
        in_specs=(P(aux, pair), P(pair), P(pair), P(), P(), P(), P()),
        out_specs=P(pair, None, aux),
        check_vma=False,
    )
```

time: 341 us -> 184 us (0.54)
  waiting for transfers between devices: 278 us -> 86.8 us
  starting transfers between devices: 0.04 us -> 49 us
  local copies, waits for them, and re-layouts: 36.1 us -> 9.81 us
  Pallas kernels: 0 us -> 12 us
  other arithmetic: 2.27 us -> 9.01 us
  matrix products: 9.53 us -> 2.87 us
    all_gather x1, waiting for transfers between devices: 222 us -> 0.02 us  [on_device(): coeffs_y = lax.all_gather(coeffs, 'y', axis=0)]
    all_to_all x0 -> x3, waiting for transfers between devices: none -> 71.6 us  [the longest x2 45.6 us: on_device(): own.append(lax.all_to_all(part, 'z', 0, 0, tiled=True))]
    reduce_scatter x1 -> x0, waiting for transfers between devices: 56.5 us -> none  [on_device(): lax.psum_scatter(partial_window, 'pair', scatter_dimension=0, tiled=True)]
    all_to_all x0 -> x3, starting transfers between devices: none -> 32.6 us  [the longest x2 28.4 us: on_device(): own.append(lax.all_to_all(part, 'z', 0, 0, tiled=True))]
    gather x2 -> x0, local copies, waits for them, and re-layouts: 23.6 us -> none  [on_device(): energy_gap = jnp.take(eps_vir, vir_index) - jnp.take(eps_occ, occ_index)]
    ppermute x0 -> x3, starting transfers between devices: none -> 16.4 us  [the longest x1 9.34 us: on_device(): arrived = lax.ppermute(away, 'core', [(0, 1), (1, 0)])]
    ppermute x0 -> x3, waiting for transfers between devices: none -> 14.6 us  [the longest x2 14.6 us: on_device(): partner = [lax.ppermute(part, 'x_hi', [(0, 1), (1, 0)]) for part in own]]
    pallas_call x0 -> x2, Pallas kernels: none -> 12 us  [products(): pl.pallas_call(product_kernel, grid=(n_y,), in_specs=[whole, whole, pl.Bl...]
  transfers between devices with their start and end apart: 2 -> 7, of which waited for: 2 -> 4; matrix products, arithmetic and copies ran while one was open for 8% -> 7% of each run, Pallas kernels for 0% -> 3%
where the time goes in v1:
time: 184 us
  waiting for transfers between devices  86.8 us (47%)
  starting transfers between devices  49 us (27%)
  between operations  14.3 us (8%)
  Pallas kernels  12 us (7%)
  local copies, waits for them, and re-layouts  9.81 us (5%)
  other arithmetic  9.01 us (5%)
  matrix products  2.87 us (2%)
    all_to_all x2, waiting for transfers between devices, on_device(): own.append(lax.all_to_all(part, 'z', 0, 0, tiled=True))  45.6 us
    all_to_all x2, starting transfers between devices, on_device(): own.append(lax.all_to_all(part, 'z', 0, 0, tiled=True))  28.4 us
    all_to_all x1, waiting for transfers between devices, on_device(): total = lax.all_to_all(total, ('y', 'x_lo'), 0, 0, tiled=True)  25.9 us
    ppermute x2, waiting for transfers between devices, on_device(): partner = [lax.ppermute(part, 'x_hi', [(0, 1), (1, 0)]) for part in own]  14.6 us
    pallas_call x2, Pallas kernels, products(): pl.pallas_call(product_kernel, grid=(n_y,), in_specs=[whole, whole, pl.Bl...  12 us
    ppermute x1, starting transfers between devices, on_device(): arrived = lax.ppermute(away, 'core', [(0, 1), (1, 0)])  9.34 us
    ppermute x2, starting transfers between devices, on_device(): partner = [lax.ppermute(part, 'x_hi', [(0, 1), (1, 0)]) for part in own]  7.01 us
    all_to_all x1, starting transfers between devices, on_device(): total = lax.all_to_all(total, ('y', 'x_lo'), 0, 0, tiled=True)  4.22 us
  transfers between devices with their start and end apart: 7, of which 4 were waited for; matrix products, arithmetic and copies ran while one was open for 7% of the time, Pallas kernels for 3%

profile of v1, /device:TPU:1, one launch (start us, length us, event | category | flops | bytes accessed | tf_op | source)
XLA Modules:
  0.0 183.9 jit_solution(13192045839874808205)
XLA Ops:
  6.5 0.0 all-gather.3.cloned.1.call-start
  6.6 0.7 all-gather.3.cloned.1.call-update
  7.9 0.9 constant_dynamic-slice_fusion
  9.0 0.8 broadcast_in_dim.8
  9.8 15.7 %all-to-all-start = ((bf16[16,8,2048]{2,1,0:T(8,128)(2,1)}), bf16[16,8,2048]{2,1,0:T(8,128)(2,1)S(1)}, u32[]{:S(2)}, u32[]{:S(2)}) async-start(bf16[16,8,2048]{2,1,0:T(8,128)(2,1)} %broadcast_in_dim.8), calls=%async_computation | async-start | bytes 1048576 | tf_op jit(solution)/shard_map/all_to_all | solution.py:80
  25.6 22.8 %all-to-all-done.own_ref = bf16[16,8,2048]{2,1,0:T(8,128)(2,1)S(1)} async-done(((bf16[16,8,2048]{2,1,0:T(8,128)(2,1)}), bf16[16,8,2048]{2,1,0:T(8,128)(2,1)S(1)}, u32[]{:S(2)}, u32[]{:S(2)}) %all-to-all-start) | async-done | bytes 524320 | tf_op jit(solution)/shard_map/all_to_all | solution.py:80
  48.4 0.8 broadcast_in_dim.10
  49.2 12.7 %all-to-all-start.1 = ((bf16[16,8,2048]{2,1,0:T(8,128)(2,1)}), bf16[16,8,2048]{2,1,0:T(8,128)(2,1)S(1)}, u32[]{:S(2)}, u32[]{:S(2)}) async-start(bf16[16,8,2048]{2,1,0:T(8,128)(2,1)} %broadcast_in_dim.10), calls=%async_computation.1 | async-start | bytes 1048576 | tf_op jit(solution)/shard_map/all_to_all | solution.py:80
  61.9 22.8 %all-to-all-done.1.own_ref = bf16[16,8,2048]{2,1,0:T(8,128)(2,1)S(1)} async-done(((bf16[16,8,2048]{2,1,0:T(8,128)(2,1)}), bf16[16,8,2048]{2,1,0:T(8,128)(2,1)S(1)}, u32[]{:S(2)}, u32[]{:S(2)}) %all-to-all-start.1) | async-done | bytes 524320 | tf_op jit(solution)/shard_map/all_to_all | solution.py:80
  84.8 4.6 %collective-permute-start.1 = (bf16[16,8,2048]{2,1,0:T(8,128)(2,1)S(1)}, bf16[16,8,2048]{2,1,0:T(8,128)(2,1)S(1)}, u32[]{:S(2)}, u32[]{:S(2)}) collective-permute-start(bf16[16,8,2048]{2,1,0:T(8,128)(2,1)S(1)} %all-to-all-done.1.own_ref), channel_id=1, source_target_pairs={{0,64},{64,0},{1,65},{65,1},{2,66},{66,2},{3,67},{67,3},{4,68},{68... | collective-permute-start | bytes 1572872 | tf_op jit(solution)/shard_map/ppermute | solution.py:81
  89.5 1.2 fusion.1
  90.7 1.7 fusion.2
  92.4 0.1 add_divide_fusion
  92.5 0.0 all-gather.3.cloned.1.call-done
  92.5 3.2 %convert = f32[4,256,2048]{2,1,0:T(8,128)S(1)} convert(bf16[4,256,2048]{2,1,0:T(8,128)(2,1)} %bitcast.23) | non-fusion elementwise | flops 2097152 | bytes 12582912 | tf_op jit(solution)/shard_map/convert_element_type | solution.py:89
  95.8 0.5 mul.48
  96.3 3.0 %fusion.scaled_ref = bf16[4,512,2048]{2,1,0:T(8,128)(2,1)S(1)} fusion(f32[512,2048]{1,0:T(8,128)S(1)} %bitcast.22, f32[4,256,2048]{2,1,0:T(8,128)S(1)} %convert), kind=kLoop, calls=%fused_computation.1 | loop fusion | flops 8388608 | bytes 20971520 | tf_op jit(solution)/shard_map/convert_element_type | solution.py:89
  99.3 0.0 collective-permute-done.1.partner_ref
  99.3 6.0 %shard_map.74 = f32[4,2,2,16,4,512]{5,4,3,2,1,0:T(4,128)S(1)} custom-call(bf16[16,8,2048]{2,1,0:T(8,128)(2,1)S(1)} %all-to-all-done.1.own_ref, bf16[16,8,2048]{2,1,0:T(8,128)(2,1)S(1)} %collective-permute-done.1.partner_ref, bf16[4,512,2048]{2,1,0:T(8,128)(2,1)S(1)} %fusion.scaled_ref), custom_call_target="tpu_custom_call" | custom-call | flops 2147483648 | bytes 8388608 | tf_op jit(solution)/shard_map/pallas_call | solution.py:49
  105.3 9.3 %collective-permute-start.2 = (f32[4,2,2,16,4,512]{5,4,3,2,1,0:T(4,128)S(1)}, f32[4,2,2,16,4,512]{5,4,3,2,1,0:T(4,128)S(1)}, u32[]{:S(2)}, u32[]{:S(2)}) collective-permute-start(f32[4,2,2,16,4,512]{5,4,3,2,1,0:T(4,128)S(1)} %shard_map.74), channel_id=1, source_target_pairs={{0,1},{1,0},{2,3},{3,2},{4,5},{5,4},{6,7},{7,6},{8,9},{9,8},{10,11... | collective-permute-start | bytes 6291464 | tf_op jit(solution)/shard_map/ppermute | solution.py:95
  114.7 2.4 %collective-permute-start = (bf16[16,8,2048]{2,1,0:T(8,128)(2,1)S(1)}, bf16[16,8,2048]{2,1,0:T(8,128)(2,1)S(1)}, u32[]{:S(2)}, u32[]{:S(2)}) collective-permute-start(bf16[16,8,2048]{2,1,0:T(8,128)(2,1)S(1)} %all-to-all-done.own_ref), channel_id=1, source_target_pairs={{0,64},{64,0},{1,65},{65,1},{2,66},{66,2},{3,67},{67,3},{4,68},{68... | collective-permute-start | bytes 1572872 | tf_op jit(solution)/shard_map/ppermute | solution.py:81
  117.1 14.6 %collective-permute-done.partner_ref = bf16[16,8,2048]{2,1,0:T(8,128)(2,1)S(1)} collective-permute-done((bf16[16,8,2048]{2,1,0:T(8,128)(2,1)S(1)}, bf16[16,8,2048]{2,1,0:T(8,128)(2,1)S(1)}, u32[]{:S(2)}, u32[]{:S(2)}) %collective-permute-start) | collective-permute-done | bytes 524320 | tf_op jit(solution)/shard_map/ppermute | solution.py:81
  131.6 6.0 %shard_map.73 = f32[4,2,2,16,4,512]{5,4,3,2,1,0:T(4,128)S(1)} custom-call(bf16[16,8,2048]{2,1,0:T(8,128)(2,1)S(1)} %all-to-all-done.own_ref, bf16[16,8,2048]{2,1,0:T(8,128)(2,1)S(1)} %collective-permute-done.partner_ref, bf16[4,512,2048]{2,1,0:T(8,128)(2,1)S(1)} %fusion.scaled_ref), custom_call_target="tpu_custom_call" | custom-call | flops 2147483648 | bytes 8388608 | tf_op jit(solution)/shard_map/pallas_call | solution.py:49
  137.7 0.0 collective-permute-done.2
  137.7 0.6 add.51
  138.3 1.7 reshape.109
  140.0 4.2 %all-to-all-start.2 = ((f32[8,128,512]{2,1,0:T(8,128)}), f32[8,128,512]{2,1,0:T(8,128)S(1)}, u32[]{:S(2)}, u32[]{:S(2)}) async-start(f32[8,128,512]{2,1,0:T(8,128)} %reshape.109), calls=%async_computation.2 | async-start | bytes 4194304 | tf_op jit(solution)/shard_map/all_to_all | solution.py:98
  144.3 25.9 %all-to-all-done.2 = f32[8,128,512]{2,1,0:T(8,128)S(1)} async-done(((f32[8,128,512]{2,1,0:T(8,128)}), f32[8,128,512]{2,1,0:T(8,128)S(1)}, u32[]{:S(2)}, u32[]{:S(2)}) %all-to-all-start.2) | async-done | bytes 2097184 | tf_op jit(solution)/shard_map/all_to_all | solution.py:98
  170.2 2.4 %reshape.110 = f32[4,2,2,16,4,2,256]{6,5,4,3,2,1,0:T(2,128)} reshape(f32[8,128,512]{2,1,0:T(8,128)S(1)} %all-to-all-done.2) | data formatting | bytes 4194304 | tf_op jit(solution)/shard_map/reshape | solution.py:99
  172.5 2.5 %fusion.16 = (f32[4,1,2,16,4,2,256]{6,5,4,3,2,1,0:T(2,128)S(1)}, f32[4,1,2,16,4,2,256]{6,5,4,3,2,1,0:T(2,128)S(1)}) fusion(f32[4,2,2,16,4,2,256]{6,5,4,3,2,1,0:T(2,128)} %reshape.110), kind=kLoop, calls=%fused_computation.43 | loop fusion | bytes 4194304 | tf_op jit(solution)/shard_map/slice | solution.py:100
  175.1 0.6 fusion.3
  175.7 1.3 reverse_select_fusion
  (17 shorter events, 0.1 us)
Async XLA Ops:
  6.5 55.4 %copy-start.4 = (f32[2]{0:T(128)S(1)}, f32[2]{0:T(128)}, u32[]{:S(2)}) copy-start(f32[2]{0:T(128)} %param.12) | copy-start | bytes 28
  6.5 82.9 %copy-start = (s32[2048]{0:T(1024)S(1)}, s32[2048]{0:T(1024)}, u32[]{:S(2)}) copy-start(s32[2048]{0:T(1024)} %param.8) | copy-start | bytes 24580
  6.5 82.9 %copy-start.1 = (s32[2048]{0:T(1024)S(1)}, s32[2048]{0:T(1024)}, u32[]{:S(2)}) copy-start(s32[2048]{0:T(1024)} %param.9) | copy-start | bytes 24580
  6.5 82.9 %copy-start.3 = (f32[2000]{0:T(1024)S(1)}, f32[2000]{0:T(1024)}, u32[]{:S(2)}) copy-start(f32[2000]{0:T(1024)} %param.10) | copy-start | bytes 24004
  6.5 84.1 %copy-start.2 = (f32[20000]{0:T(1024)S(1)}, f32[20000]{0:T(1024)}, u32[]{:S(2)}) copy-start(f32[20000]{0:T(1024)} %param.11) | copy-start | bytes 240004
  6.5 85.9 %all-gather.3.cloned.1.call-start = ((), (), s32[]{:S(2)}) async-start(), calls=%async_computation.3 | async-start | bytes 5242880 | tf_op jit(solution)/shard_map/all_gather | solution.py:69
  9.8 38.6 %all-to-all-start = ((bf16[16,8,2048]{2,1,0:T(8,128)(2,1)}), bf16[16,8,2048]{2,1,0:T(8,128)(2,1)S(1)}, u32[]{:S(2)}, u32[]{:S(2)}) async-start(bf16[16,8,2048]{2,1,0:T(8,128)(2,1)} %broadcast_in_dim.8), calls=%async_computation | async-start | bytes 1048576 | tf_op jit(solution)/shard_map/all_to_all | solution.py:80
  49.2 35.5 %all-to-all-start.1 = ((bf16[16,8,2048]{2,1,0:T(8,128)(2,1)}), bf16[16,8,2048]{2,1,0:T(8,128)(2,1)S(1)}, u32[]{:S(2)}, u32[]{:S(2)}) async-start(bf16[16,8,2048]{2,1,0:T(8,128)(2,1)} %broadcast_in_dim.10), calls=%async_computation.1 | async-start | bytes 1048576 | tf_op jit(solution)/shard_map/all_to_all | solution.py:80
  84.8 14.5 %collective-permute-start.1 = (bf16[16,8,2048]{2,1,0:T(8,128)(2,1)S(1)}, bf16[16,8,2048]{2,1,0:T(8,128)(2,1)S(1)}, u32[]{:S(2)}, u32[]{:S(2)}) collective-permute-start(bf16[16,8,2048]{2,1,0:T(8,128)(2,1)S(1)} %all-to-all-done.1.own_ref), channel_id=1, source_target_pairs={{0,64},{64,0},{1,65},{65,1},{2,66},{66,2},{3,67},{67,3},{4,68},{68... | collective-permute-start | bytes 1572872 | tf_op jit(solution)/shard_map/ppermute | solution.py:81
  105.3 32.3 %collective-permute-start.2 = (f32[4,2,2,16,4,512]{5,4,3,2,1,0:T(4,128)S(1)}, f32[4,2,2,16,4,512]{5,4,3,2,1,0:T(4,128)S(1)}, u32[]{:S(2)}, u32[]{:S(2)}) collective-permute-start(f32[4,2,2,16,4,512]{5,4,3,2,1,0:T(4,128)S(1)} %shard_map.74), channel_id=1, source_target_pairs={{0,1},{1,0},{2,3},{3,2},{4,5},{5,4},{6,7},{7,6},{8,9},{9,8},{10,11... | collective-permute-start | bytes 6291464 | tf_op jit(solution)/shard_map/ppermute | solution.py:95
  114.7 16.9 %collective-permute-start = (bf16[16,8,2048]{2,1,0:T(8,128)(2,1)S(1)}, bf16[16,8,2048]{2,1,0:T(8,128)(2,1)S(1)}, u32[]{:S(2)}, u32[]{:S(2)}) collective-permute-start(bf16[16,8,2048]{2,1,0:T(8,128)(2,1)S(1)} %all-to-all-done.own_ref), channel_id=1, source_target_pairs={{0,64},{64,0},{1,65},{65,1},{2,66},{66,2},{3,67},{67,3},{4,68},{68... | collective-permute-start | bytes 1572872 | tf_op jit(solution)/shard_map/ppermute | solution.py:81
  140.0 30.2 %all-to-all-start.2 = ((f32[8,128,512]{2,1,0:T(8,128)}), f32[8,128,512]{2,1,0:T(8,128)S(1)}, u32[]{:S(2)}, u32[]{:S(2)}) async-start(f32[8,128,512]{2,1,0:T(8,128)} %reshape.109), calls=%async_computation.2 | async-start | bytes 4194304 | tf_op jit(solution)/shard_map/all_to_all | solution.py:98
Sparse Core Ops, SparseCore 0:
  9.5 61.2 all-gather.2

commit v2 on v1

v2 whole, which is shorter than its diff:
```python
import functools

import jax
import jax.numpy as jnp
from jax import lax
from jax.experimental import pallas as pl
from jax.experimental.pallas import tpu as pltpu
from jax.sharding import Mesh
from jax.sharding import PartitionSpec as P

ROWS_DEV = 16
LANES = 128
VMEM = 24 * 1024 * 1024


def lookup(table, index):
    rows = -(-table.shape[0] // LANES)
    rows += -rows % 8
    grid = jnp.pad(table, (0, rows * LANES - table.shape[0])).reshape(rows, LANES)
    high = (index // LANES)[:, None] == jnp.arange(rows, dtype=jnp.int32)[None, :]
    low = (index % LANES)[:, None] == jnp.arange(LANES, dtype=jnp.int32)[None, :]
    picked = lax.dot_general(
        high.astype(jnp.float32),
        grid,
        (((1,), (0,)), ((), ())),
        precision=lax.Precision.HIGHEST,
        preferred_element_type=jnp.float32,
    )
    return jnp.sum(jnp.where(low, picked, 0.0), axis=1)


def scale_kernel(coeffs_ref, response_ref, out_ref):
    coeffs = coeffs_ref[0].astype(jnp.float32)
    aux_local = coeffs.shape[0]
    for w in range(2):
        out_ref[0, w * aux_local : (w + 1) * aux_local] = (
            coeffs * response_ref[w : w + 1, :]
        ).astype(jnp.bfloat16)


def scale(coeffs, response):
    n_y, aux_local, depth = coeffs.shape
    return pl.pallas_call(
        scale_kernel,
        grid=(n_y,),
        in_specs=[
            pl.BlockSpec((1, aux_local, depth), lambda y: (y, 0, 0)),
            pl.BlockSpec(response.shape, lambda y: (0, 0)),
        ],
        out_specs=pl.BlockSpec((1, 2 * aux_local, depth), lambda y: (y, 0, 0)),
        out_shape=jax.ShapeDtypeStruct((n_y, 2 * aux_local, depth), jnp.bfloat16),
        compiler_params=pltpu.CompilerParams(vmem_limit_bytes=VMEM),
        cost_estimate=pl.CostEstimate(
            flops=2 * aux_local * n_y * depth,
            bytes_accessed=6 * aux_local * n_y * depth,
            transcendentals=0,
        ),
    )(coeffs, response)


def product_kernel(rows_ref, scaled_ref, away_ref, kept_ref):
    product = lax.dot_general(
        rows_ref[...],
        scaled_ref[0],
        (((1,), (1,)), ((), ())),
        preferred_element_type=jnp.float32,
    )
    half = product.shape[0] // 2
    away_ref[0] = product[:half]
    kept_ref[0] = product[half:]


def products(rows, scaled):
    n_rows, depth = rows.shape
    n_y, columns, _ = scaled.shape
    out = (n_y, n_rows // 2, columns)
    return pl.pallas_call(
        product_kernel,
        grid=(n_y,),
        in_specs=[
            pl.BlockSpec((n_rows, depth), lambda y: (0, 0)),
            pl.BlockSpec((1, columns, depth), lambda y: (y, 0, 0)),
        ],
        out_specs=[pl.BlockSpec((1,) + out[1:], lambda y: (y, 0, 0))] * 2,
        out_shape=[jax.ShapeDtypeStruct(out, jnp.float32)] * 2,
        compiler_params=pltpu.CompilerParams(vmem_limit_bytes=VMEM),
        cost_estimate=pl.CostEstimate(
            flops=2 * n_rows * depth * columns * n_y,
            bytes_accessed=2 * columns * n_y * depth,
            transcendentals=0,
        ),
    )(rows, scaled)


def total_kernel(x_hi_ref, own_ref, partner_ref, out_ref):
    own, partner = [ref[:, 0, 0] + ref[:, 1, 0] for ref in (own_ref, partner_ref)]
    swap = x_hi_ref[0] == 1
    sides = jnp.where(swap, partner, own), jnp.where(swap, own, partner)
    n_y, n_z, _ = own.shape
    for y in range(n_y):
        for side in range(2):
            base = (2 * y + side) * n_z * 4
            for w in range(2):
                for half in range(2):
                    at = (2 * w + half) * LANES
                    out_ref[pl.ds(base + 2 * half + w, n_z, stride=4), :] = sides[side][
                        y, :, at : at + LANES
                    ]


def total_over_x(x_hi, own, partner):
    n_y, n_x, n_i, n_z, columns = own.shape
    block = pl.BlockSpec((n_y, n_x, 1, n_z, columns), lambda i, x: (0, 0, i, 0, 0))
    n_rows = n_y * 2 * n_z
    out = pl.pallas_call(
        total_kernel,
        grid_spec=pltpu.PrefetchScalarGridSpec(
            num_scalar_prefetch=1,
            grid=(n_i,),
            in_specs=[block, block],
            out_specs=pl.BlockSpec((n_rows * 4, LANES), lambda i, x: (i, 0)),
        ),
        out_shape=jax.ShapeDtypeStruct((n_i * n_rows * 4, LANES), jnp.float32),
        compiler_params=pltpu.CompilerParams(vmem_limit_bytes=VMEM),
    )(x_hi, own, partner)
    out = out.reshape(n_i * n_rows, 2, 2, LANES)
    return jnp.transpose(out, (0, 2, 1, 3)).reshape(-1, 2, 2 * LANES)


def on_device(n_y, n_z, coeffs, occ_index, vir_index, eps_occ, eps_vir, frequencies, offset):
    aux_local, depth = coeffs.shape
    core = lax.axis_index("core")
    x_hi = lax.axis_index("x_hi").reshape(1).astype(jnp.int32)
    swap = [(0, 1), (1, 0)]

    coeffs_y = lax.all_gather(coeffs, "y", axis=0)

    rows = lax.dynamic_slice_in_dim(coeffs, offset[0], ROWS_DEV, 0)
    rows = rows.reshape(2, 2, ROWS_DEV // 4, depth)
    first, second = rows[:, 0], rows[:, 1]
    rows = jnp.where(core == 0, jnp.stack([second, first]), jnp.stack([first, second]))
    rows = rows.reshape(ROWS_DEV, depth)

    last = jnp.broadcast_to(rows[-1].reshape(1, 2, -1), (n_z, 2, depth // 2))
    last = lax.all_to_all(last, "z", 0, 0, tiled=True)
    gathered = lax.all_gather(rows[:-1], "z", axis=0)
    gathered, last = lax.optimization_barrier((gathered, last))
    own = jnp.concatenate(
        [jnp.transpose(gathered, (1, 0, 2)), last.reshape(1, n_z, depth)], axis=0
    ).reshape(-1, depth)
    partner = lax.ppermute(own, "x_hi", swap)

    occ_index, vir_index, _ = lax.optimization_barrier((occ_index, vir_index, gathered))
    energy_gap = lookup(eps_vir, vir_index) - lookup(eps_occ, occ_index)
    squares = frequencies * frequencies
    response = (
        2.0 * energy_gap[None, :] / (energy_gap[None, :] * energy_gap[None, :] + squares[:, None])
    )
    scaled = scale(coeffs_y, response)

    totals = []
    for side in (own, partner):
        away, kept = products(side, scaled)
        total = (kept + lax.ppermute(away, "core", swap)).reshape(n_y * 2, -1, 2 * aux_local)
        total = lax.all_to_all(total, ("y", "x_lo"), 0, 0, tiled=True)
        totals.append(total.reshape(n_y, 2, ROWS_DEV // 4, n_z, 2 * aux_local))
    return total_over_x(x_hi, *totals)


def solution(mesh):
    n_y = 4
    n_z = mesh.shape["aux"] // (2 * n_y)
    split = Mesh(
        mesh.devices.reshape(n_y, 2, n_z, 2, 2), ("y", "x_hi", "z", "x_lo", "core")
    )
    aux, pair = ("y", "x_hi", "z"), ("x_lo", "core")
    return jax.shard_map(
        functools.partial(on_device, n_y, n_z),
        mesh=split,
        in_specs=(P(aux, pair), P(pair), P(pair), P(), P(), P(), P()),
        out_specs=P(pair, None, aux),
        check_vma=False,
    )
```

time: 184 us -> 144 us (0.78)
  waiting for transfers between devices: 86.8 us -> 34.1 us
  blocking collectives: 0 us -> 32.4 us
  starting transfers between devices: 49 us -> 41 us
  other arithmetic: 9.01 us -> 3.53 us
  local copies, waits for them, and re-layouts: 9.81 us -> 4.57 us
  Pallas kernels: 12 us -> 9.78 us
    all_to_all x2 -> x1, waiting for transfers between devices: 45.6 us -> 0.01 us  [on_device(): last = lax.all_to_all(last, 'z', 0, 0, tiled=True)]
    all_gather x0 -> x1, blocking collectives: none -> 32.4 us  [on_device(): gathered = lax.all_gather(rows[:-1], 'z', axis=0)]
    ppermute x3, waiting for transfers between devices: 14.6 us -> 1.29 us  [the longest x1 1.29 us: on_device(): partner = lax.ppermute(own, 'x_hi', swap)]
    all_to_all x2 -> x1, starting transfers between devices: 28.4 us -> 15.7 us  [on_device(): last = lax.all_to_all(last, 'z', 0, 0, tiled=True)]
    convert_element_type x2 -> x0, other arithmetic: 6.28 us -> none  [the longest x1 3.24 us: on_device(): coeffs_y[:, None].astype(jnp.float32) * response[None, :, None, :]]
    all_to_all x1 -> x2, starting transfers between devices: 4.22 us -> 8.81 us  [on_device(): total = lax.all_to_all(total, ('y', 'x_lo'), 0, 0, tiled=True)]
    reshape x3 -> x2, local copies, waits for them, and re-layouts: 4.13 us -> 0.09 us  [the longest x1 0.05 us: on_device(): last.reshape(1, n_z, depth)]
    all_gather x1, waiting for transfers between devices: 0.02 us -> 3.44 us  [on_device(): coeffs_y = lax.all_gather(coeffs, 'y', axis=0)]
  transfers between devices with their start and end apart: 7 -> 7, of which waited for: 4 -> 4; matrix products, arithmetic and copies ran while one was open for 7% -> 6% of each run, Pallas kernels for 3% -> 6%
where the time goes in v2:
time: 144 us; the launch traced here: 143 us
  starting transfers between devices  41 us (28%)
  waiting for transfers between devices  34.1 us (24%)
  blocking collectives  32.4 us (22%)
  between operations  14.3 us (10%)
  Pallas kernels  9.78 us (7%)
  local copies, waits for them, and re-layouts  4.57 us (3%)
  other arithmetic  3.53 us (2%)
  matrix products  2.87 us (2%)
    all_gather x1, blocking collectives, on_device(): gathered = lax.all_gather(rows[:-1], 'z', axis=0)  32.4 us
    all_to_all x2, waiting for transfers between devices, on_device(): total = lax.all_to_all(total, ('y', 'x_lo'), 0, 0, tiled=True)  28.7 us
    all_to_all x1, starting transfers between devices, on_device(): last = lax.all_to_all(last, 'z', 0, 0, tiled=True)  15.7 us
    ppermute x2, starting transfers between devices, on_device(): lax.ppermute(away, 'core', swap)  11.8 us
    all_to_all x2, starting transfers between devices, on_device(): total = lax.all_to_all(total, ('y', 'x_lo'), 0, 0, tiled=True)  8.81 us
    pallas_call x2, Pallas kernels, products(): pl.pallas_call(product_kernel, grid=(n_y,), in_specs=[pl.BlockSpec((n_row...  6.68 us
    ppermute x1, starting transfers between devices, on_device(): partner = lax.ppermute(own, 'x_hi', swap)  4.65 us
    all_gather x1, waiting for transfers between devices, on_device(): coeffs_y = lax.all_gather(coeffs, 'y', axis=0)  3.44 us
  transfers between devices with their start and end apart: 7, of which 4 were waited for; matrix products, arithmetic and copies ran while one was open for 6% of the time, Pallas kernels for 6%

profile of v2, /device:TPU:1, one launch (start us, length us, event | category | flops | bytes accessed | tf_op | source)
XLA Modules:
  0.0 142.5 jit_solution(7200825655113964674)
XLA Ops:
  6.5 0.7 all-gather.5.cloned.1.call-update
  7.9 0.9 constant_dynamic-slice_fusion
  8.9 0.1 maximum_select_fusion
  9.0 0.7 broadcast_in_dim.10
  9.7 15.7 %all-to-all-start = ((bf16[16,2,1024]{2,1,0:T(2,128)(2,1)}), bf16[16,2,1024]{2,1,0:T(2,128)(2,1)S(1)}, u32[]{:S(2)}, u32[]{:S(2)}) async-start(bf16[16,2,1024]{2,1,0:T(2,128)(2,1)} %broadcast_in_dim.10), calls=%async_computation | async-start | bytes 131072 | tf_op jit(solution)/shard_map/all_to_all | solution.py:145
  25.5 0.7 mul.25
  26.2 32.4 %all-gather.2 = bf16[16,15,2048]{2,1,0:T(8,128)(2,1)S(1)} all-gather(bf16[1,15,2048]{2,1,0:T(8,128)(2,1)S(1)} %slice_bitcast_fusion), channel_id=2, replica_groups=mesh['y'=4,'x_hi'=2,'z'=16,'x_lo'=2,'core'=2] {'z'}, dimensions={0}, use_global_device_ids=true | all-gather | bytes 1044480 | tf_op jit(solution)/shard_map/all_gather | solution.py:146
  58.6 0.1 reshape.77
  58.7 0.0 copy-start.1
  58.7 0.0 copy-start.2
  58.7 0.3 pad_maximum_fusion
  59.0 0.0 copy-start.3
  59.0 0.6 copy.18
  59.6 4.7 %collective-permute-start.1 = (bf16[256,2048]{1,0:T(8,128)(2,1)S(1)}, bf16[256,2048]{1,0:T(8,128)(2,1)S(1)}, u32[]{:S(2)}, u32[]{:S(2)}) collective-permute-start(bf16[256,2048]{1,0:T(8,128)(2,1)S(1)} %bitcast.31), channel_id=1, source_target_pairs={{0,64},{64,0},{1,65},{65,1},{2,66},{66,2},{3,67},{67,3},{4,68},{68... | collective-permute-start | bytes 3145736 | tf_op jit(solution)/shard_map/ppermute | solution.py:151
  64.3 1.2 fusion
  65.5 1.7 %fusion.1 = f32[2048]{0:T(1024)S(1)} fusion(s32[2048]{0:T(1024)S(1)} %get-tuple-element.29, s32[2048]{0:T(1024)S(1)} %get-tuple-element.30, f32[20000]{0:T(1024)S(1)} %copy-done.3), kind=kOutput, calls=%fused_computation.4 | convolution fusion | flops 504428544 | bytes 104576 | tf_op jit(solution)/shard_map/dot_general | solution.py:22
  67.2 0.1 add_divide_fusion.response_ref
  67.3 3.4 %all-gather.5.cloned.1.call-done = bf16[1024,2048]{1,0:T(8,128)(2,1)} async-done(((bf16[256,2048]{1,0:T(8,128)(2,1)}), bf16[1024,2048]{1,0:T(8,128)(2,1)}) %all-gather.5.cloned.1.call-update) | async-done | bytes 4194320 | tf_op jit(solution)/shard_map/all_gather | solution.py:136
  70.8 2.2 %copy-done = bf16[1024,2048]{1,0:T(8,128)(2,1)S(1)} copy-done((bf16[1024,2048]{1,0:T(8,128)(2,1)S(1)}, bf16[1024,2048]{1,0:T(8,128)(2,1)}, u32[]{:S(2)}) %copy-start) | copy-done | bytes 4194328
  73.0 1.4 shard_map.73.scaled_ref
  74.4 3.0 %shard_map.74 = (f32[4,128,512]{2,1,0:T(8,128)S(1)}, f32[4,128,512]{2,1,0:T(8,128)S(1)}) custom-call(bf16[256,2048]{1,0:T(8,128)(2,1)S(1)} %bitcast.32, bf16[4,512,2048]{2,1,0:T(8,128)(2,1)S(1)} %shard_map.73.scaled_ref), custom_call_target="tpu_custom_call" | custom-call | flops 2147483648 | bytes 8388608 | tf_op jit(solution)/shard_map/pallas_call | solution.py:77
  77.4 3.9 %collective-permute-start = (f32[4,128,512]{2,1,0:T(8,128)S(1)}, f32[4,128,512]{2,1,0:T(8,128)S(1)}, u32[]{:S(2)}, u32[]{:S(2)}) collective-permute-start(f32[4,128,512]{2,1,0:T(8,128)S(1)} %get-tuple-element.18), channel_id=1, source_target_pairs={{0,1},{1,0},{2,3},{3,2},{4,5},{5,4},{6,7},{7,6},{8,9},{9,8},{10,11... | collective-permute-start | bytes 3145736 | tf_op jit(solution)/shard_map/ppermute | solution.py:164
  81.3 1.3 collective-permute-done.1.rows_ref
  82.6 3.7 %shard_map.75 = (f32[4,128,512]{2,1,0:T(8,128)}, f32[4,128,512]{2,1,0:T(8,128)S(1)}) custom-call(bf16[256,2048]{1,0:T(8,128)(2,1)S(1)} %collective-permute-done.1.rows_ref, bf16[4,512,2048]{2,1,0:T(8,128)(2,1)S(1)} %shard_map.73.scaled_ref), custom_call_target="tpu_custom_call" | custom-call | flops 2147483648 | bytes 8388608 | tf_op jit(solution)/shard_map/pallas_call | solution.py:77
  86.2 7.9 %collective-permute-start.2 = (f32[4,128,512]{2,1,0:T(8,128)}, f32[4,128,512]{2,1,0:T(8,128)S(1)}, u32[]{:S(2)}, u32[]{:S(2)}) collective-permute-start(f32[4,128,512]{2,1,0:T(8,128)} %get-tuple-element.20), channel_id=1, source_target_pairs={{0,1},{1,0},{2,3},{3,2},{4,5},{5,4},{6,7},{7,6},{8,9},{9,8},{10,11... | collective-permute-start | bytes 3145736 | tf_op jit(solution)/shard_map/ppermute | solution.py:164
  94.2 1.2 add.44
  95.3 5.3 %all-to-all-start.1 = ((f32[8,64,512]{2,1,0:T(8,128)}), f32[8,64,512]{2,1,0:T(8,128)S(1)}, u32[]{:S(2)}, u32[]{:S(2)}) async-start(f32[8,64,512]{2,1,0:T(8,128)} %bitcast.10), calls=%async_computation.1 | async-start | bytes 2097152 | tf_op jit(solution)/shard_map/all_to_all | solution.py:165
  100.6 1.2 add.45
  101.8 14.4 %all-to-all-done.1 = f32[8,64,512]{2,1,0:T(8,128)S(1)} async-done(((f32[8,64,512]{2,1,0:T(8,128)}), f32[8,64,512]{2,1,0:T(8,128)S(1)}, u32[]{:S(2)}, u32[]{:S(2)}) %all-to-all-start.1) | async-done | bytes 1048608 | tf_op jit(solution)/shard_map/all_to_all | solution.py:165
  116.2 3.6 %all-to-all-start.2 = ((f32[8,64,512]{2,1,0:T(8,128)}), f32[8,64,512]{2,1,0:T(8,128)S(1)}, u32[]{:S(2)}, u32[]{:S(2)}) async-start(f32[8,64,512]{2,1,0:T(8,128)} %bitcast.36), calls=%async_computation.2 | async-start | bytes 2097152 | tf_op jit(solution)/shard_map/all_to_all | solution.py:165
  119.8 14.3 %all-to-all-done.2 = f32[8,64,512]{2,1,0:T(8,128)S(1)} async-done(((f32[8,64,512]{2,1,0:T(8,128)}), f32[8,64,512]{2,1,0:T(8,128)S(1)}, u32[]{:S(2)}, u32[]{:S(2)}) %all-to-all-start.2) | async-done | bytes 1048608 | tf_op jit(solution)/shard_map/all_to_all | solution.py:165
  134.0 1.7 %shard_map.76 = f32[2048,128]{1,0:T(8,128)} custom-call(s32[1]{0:T(128)} %bitcast.x_hi_ref, f32[4,2,4,16,512]{4,3,2,1,0:T(8,128)S(1)} %bitcast.34, f32[4,2,4,16,512]{4,3,2,1,0:T(8,128)S(1)} %bitcast.35), custom_call_target="tpu_custom_call" | custom-call | tf_op jit(solution)/shard_map/pallas_call | solution.py:115
  (18 shorter events, 0.2 us)
Async XLA Ops:
  6.5 64.2 %all-gather.5.cloned.1.call-start = ((), (), s32[]{:S(2)}) async-start(), calls=%async_computation.3 | async-start | bytes 5242880 | tf_op jit(solution)/shard_map/all_gather | solution.py:136
  9.7 48.9 %all-to-all-start = ((bf16[16,2,1024]{2,1,0:T(2,128)(2,1)}), bf16[16,2,1024]{2,1,0:T(2,128)(2,1)S(1)}, u32[]{:S(2)}, u32[]{:S(2)}) async-start(bf16[16,2,1024]{2,1,0:T(2,128)(2,1)} %broadcast_in_dim.10), calls=%async_computation | async-start | bytes 131072 | tf_op jit(solution)/shard_map/all_to_all | solution.py:145
  58.7 5.6 %copy-start.1 = (s32[2048]{0:T(1024)S(1)}, s32[2048]{0:T(1024)}, u32[]{:S(2)}) copy-start(s32[2048]{0:T(1024)} %param.8) | copy-start | bytes 24580
  58.7 5.6 %copy-start.2 = (s32[2048]{0:T(1024)S(1)}, s32[2048]{0:T(1024)}, u32[]{:S(2)}) copy-start(s32[2048]{0:T(1024)} %param.9) | copy-start | bytes 24580
  58.7 5.6 %copy-start.4 = (f32[2000]{0:T(1024)S(1)}, f32[2000]{0:T(1024)}, u32[]{:S(2)}) copy-start(f32[2000]{0:T(1024)} %param.10) | copy-start | bytes 24004
  59.0 6.5 %copy-start.3 = (f32[20000]{0:T(1024)S(1)}, f32[20000]{0:T(1024)}, u32[]{:S(2)}) copy-start(f32[20000]{0:T(1024)} %param.11) | copy-start | bytes 240004
  59.6 23.0 %collective-permute-start.1 = (bf16[256,2048]{1,0:T(8,128)(2,1)S(1)}, bf16[256,2048]{1,0:T(8,128)(2,1)S(1)}, u32[]{:S(2)}, u32[]{:S(2)}) collective-permute-start(bf16[256,2048]{1,0:T(8,128)(2,1)S(1)} %bitcast.31), channel_id=1, source_target_pairs={{0,64},{64,0},{1,65},{65,1},{2,66},{66,2},{3,67},{67,3},{4,68},{68... | collective-permute-start | bytes 3145736 | tf_op jit(solution)/shard_map/ppermute | solution.py:151
  70.8 2.2 %copy-start = (bf16[1024,2048]{1,0:T(8,128)(2,1)S(1)}, bf16[1024,2048]{1,0:T(8,128)(2,1)}, u32[]{:S(2)}) copy-start(bf16[1024,2048]{1,0:T(8,128)(2,1)} %all-gather.5.cloned.1.call-done) | copy-start | bytes 12582916
  77.4 16.8 %collective-permute-start = (f32[4,128,512]{2,1,0:T(8,128)S(1)}, f32[4,128,512]{2,1,0:T(8,128)S(1)}, u32[]{:S(2)}, u32[]{:S(2)}) collective-permute-start(f32[4,128,512]{2,1,0:T(8,128)S(1)} %get-tuple-element.18), channel_id=1, source_target_pairs={{0,1},{1,0},{2,3},{3,2},{4,5},{5,4},{6,7},{7,6},{8,9},{9,8},{10,11... | collective-permute-start | bytes 3145736 | tf_op jit(solution)/shard_map/ppermute | solution.py:164
  86.2 14.4 %collective-permute-start.2 = (f32[4,128,512]{2,1,0:T(8,128)}, f32[4,128,512]{2,1,0:T(8,128)S(1)}, u32[]{:S(2)}, u32[]{:S(2)}) collective-permute-start(f32[4,128,512]{2,1,0:T(8,128)} %get-tuple-element.20), channel_id=1, source_target_pairs={{0,1},{1,0},{2,3},{3,2},{4,5},{5,4},{6,7},{7,6},{8,9},{9,8},{10,11... | collective-permute-start | bytes 3145736 | tf_op jit(solution)/shard_map/ppermute | solution.py:164
  95.3 20.8 %all-to-all-start.1 = ((f32[8,64,512]{2,1,0:T(8,128)}), f32[8,64,512]{2,1,0:T(8,128)S(1)}, u32[]{:S(2)}, u32[]{:S(2)}) async-start(f32[8,64,512]{2,1,0:T(8,128)} %bitcast.10), calls=%async_computation.1 | async-start | bytes 2097152 | tf_op jit(solution)/shard_map/all_to_all | solution.py:165
  116.2 17.8 %all-to-all-start.2 = ((f32[8,64,512]{2,1,0:T(8,128)}), f32[8,64,512]{2,1,0:T(8,128)S(1)}, u32[]{:S(2)}, u32[]{:S(2)}) async-start(f32[8,64,512]{2,1,0:T(8,128)} %bitcast.36), calls=%async_computation.2 | async-start | bytes 2097152 | tf_op jit(solution)/shard_map/all_to_all | solution.py:165
Sparse Core Ops, SparseCore 0:
  9.5 61.2 all-gather.4

commit v3 on v2

v3 whole, which is shorter than its diff:
```python
import functools

import jax
import jax.numpy as jnp
from jax import lax
from jax.experimental import pallas as pl
from jax.experimental.pallas import tpu as pltpu
from jax.sharding import Mesh
from jax.sharding import PartitionSpec as P

ROWS_DEV = 16
LANES = 128
VMEM = 24 * 1024 * 1024
SMALL = pl.CostEstimate(flops=1, bytes_accessed=1, transcendentals=0)


def lookup(table, index):
    rows = -(-table.shape[0] // LANES)
    rows += -rows % 8
    grid = jnp.pad(table, (0, rows * LANES - table.shape[0])).reshape(rows, LANES)
    high = (index // LANES)[:, None] == jnp.arange(rows, dtype=jnp.int32)[None, :]
    low = (index % LANES)[:, None] == jnp.arange(LANES, dtype=jnp.int32)[None, :]
    picked = lax.dot_general(
        high.astype(jnp.float32),
        grid,
        (((1,), (0,)), ((), ())),
        precision=lax.Precision.HIGHEST,
        preferred_element_type=jnp.float32,
    )
    return jnp.sum(jnp.where(low, picked, 0.0), axis=1)


def scale_kernel(y_ref, *refs):
    del y_ref
    *coeffs_refs, response_ref, out_ref = refs
    for step, coeffs_ref in enumerate(coeffs_refs):

        @pl.when(pl.program_id(0) == step)
        def _(coeffs_ref=coeffs_ref):
            coeffs = coeffs_ref[...].astype(jnp.float32)
            aux_local = coeffs.shape[0]
            for w in range(2):
                out_ref[0, w * aux_local : (w + 1) * aux_local] = (
                    coeffs * response_ref[w : w + 1, :]
                ).astype(jnp.bfloat16)


def scale(y, coeffs, response):
    n_y = len(coeffs)
    aux_local, depth = coeffs[0].shape
    return pl.pallas_call(
        scale_kernel,
        grid_spec=pltpu.PrefetchScalarGridSpec(
            num_scalar_prefetch=1,
            grid=(n_y,),
            in_specs=[
                *[pl.BlockSpec((aux_local, depth), lambda i, y: (0, 0))] * n_y,
                pl.BlockSpec(response.shape, lambda i, y: (0, 0)),
            ],
            out_specs=pl.BlockSpec(
                (1, 2 * aux_local, depth), lambda i, y: (lax.rem(i + y[0], n_y), 0, 0)
            ),
        ),
        out_shape=jax.ShapeDtypeStruct((n_y, 2 * aux_local, depth), jnp.bfloat16),
        compiler_params=pltpu.CompilerParams(vmem_limit_bytes=VMEM),
        cost_estimate=SMALL,
    )(y, *coeffs, response)


def product_kernel(n_away, *refs):
    *rows_refs, scaled_ref, away_ref, kept_ref = refs
    depth = scaled_ref.shape[-1]
    rows = [ref[...].reshape(-1, depth) for ref in rows_refs]
    product = lax.dot_general(
        rows[0] if len(rows) == 1 else jnp.concatenate(rows, axis=0),
        scaled_ref[0],
        (((1,), (1,)), ((), ())),
        preferred_element_type=jnp.float32,
    )
    away_ref[0] = product[:n_away]
    kept_ref[0] = product[n_away:]


def products(rows, scaled, n_away):
    n_y, columns, depth = scaled.shape
    n_kept = sum(part.shape[0] for part in rows) - n_away
    return pl.pallas_call(
        functools.partial(product_kernel, n_away),
        grid=(n_y,),
        in_specs=[
            *[pl.BlockSpec(part.shape, lambda y: (0, 0)) for part in rows],
            pl.BlockSpec((1, columns, depth), lambda y: (y, 0, 0)),
        ],
        out_specs=[pl.BlockSpec((1, n, columns), lambda y: (y, 0, 0)) for n in (n_away, n_kept)],
        out_shape=[jax.ShapeDtypeStruct((n_y, n, columns), jnp.float32) for n in (n_away, n_kept)],
        compiler_params=pltpu.CompilerParams(vmem_limit_bytes=VMEM),
        cost_estimate=SMALL,
    )(*rows, scaled)


def total_kernel(x_hi_ref, parts_ref, out_ref):
    parts = parts_ref[:, :, :, 0].astype(jnp.float32)
    total = parts[:, 0] + parts[:, 1]
    swap = x_hi_ref[0] == 1
    n_y, _, n_z, _ = total.shape
    for y in range(n_y):
        for side in range(2):
            rows = jnp.where(swap, total[y, 1 - side], total[y, side])
            base = (2 * y + side) * n_z * 4
            for w in range(2):
                for half in range(2):
                    at = (2 * w + half) * LANES
                    out_ref[pl.ds(base + 2 * half + w, n_z, stride=4), :] = rows[:, at : at + LANES]


def total_over_x(x_hi, parts):
    n_y, n_x, n_sides, n_i, n_z, columns = parts.shape
    n_rows = n_y * n_sides * n_z
    out = pl.pallas_call(
        total_kernel,
        grid_spec=pltpu.PrefetchScalarGridSpec(
            num_scalar_prefetch=1,
            grid=(n_i,),
            in_specs=[
                pl.BlockSpec(
                    (n_y, n_x, n_sides, 1, n_z, columns), lambda i, x: (0, 0, 0, i, 0, 0)
                )
            ],
            out_specs=pl.BlockSpec((n_rows * 4, LANES), lambda i, x: (i, 0)),
        ),
        out_shape=jax.ShapeDtypeStruct((n_i * n_rows * 4, LANES), jnp.float32),
        compiler_params=pltpu.CompilerParams(vmem_limit_bytes=VMEM),
    )(x_hi, parts)
    out = out.reshape(n_i * n_rows, 2, 2, LANES)
    return jnp.transpose(out, (0, 2, 1, 3)).reshape(-1, 2, 2 * LANES)


def on_device(n_y, n_z, coeffs, occ_index, vir_index, eps_occ, eps_vir, frequencies, offset):
    aux_local, depth = coeffs.shape
    core = lax.axis_index("core")
    x_hi = lax.axis_index("x_hi").reshape(1).astype(jnp.int32)
    y = lax.axis_index("y").reshape(1).astype(jnp.int32)
    swap = [(0, 1), (1, 0)]

    rows = lax.dynamic_slice_in_dim(coeffs, offset[0], ROWS_DEV, 0)
    rows = rows.reshape(2, 2, ROWS_DEV // 4, depth)
    first, second = rows[:, 0], rows[:, 1]
    rows = jnp.where(core == 0, jnp.stack([second, first]), jnp.stack([first, second]))
    rows = rows.reshape(ROWS_DEV, depth)

    shifts = [[(i, (i - shift) % n_y) for i in range(n_y)] for shift in range(n_y)]
    coeffs_y = [coeffs] + [lax.ppermute(coeffs, "y", shifts[shift]) for shift in range(1, n_y)]

    last = jnp.concatenate([rows[-1:], lax.ppermute(rows[-1:], "x_hi", swap)], axis=0)
    gathered = lax.all_gather(rows[:-1], "z", axis=0)
    last, gathered = lax.optimization_barrier((last, gathered))
    own = jnp.transpose(gathered, (1, 0, 2)).reshape(-1, depth)
    partner = lax.ppermute(own, "x_hi", swap)
    last = jnp.broadcast_to(last[None], (n_z, 2, depth))
    last = lax.all_to_all(last, "z", 0, 0, tiled=True)
    last = jnp.transpose(last, (1, 0, 2))

    occ_index, vir_index, _ = lax.optimization_barrier((occ_index, vir_index, gathered))
    energy_gap = lookup(eps_vir, vir_index) - lookup(eps_occ, occ_index)
    squares = frequencies * frequencies
    response = (
        2.0 * energy_gap[None, :] / (energy_gap[None, :] * energy_gap[None, :] + squares[:, None])
    )
    scaled = scale(y, coeffs_y, response)

    n_away = ROWS_DEV // 2 * n_z
    away, kept = products([own, last[0]], scaled, n_away)
    arrived = lax.ppermute(away, "core", swap)
    totals = [kept + arrived]
    away, kept = products([partner, last[1]], scaled, n_away)
    totals.append(kept + lax.ppermute(away, "core", swap))
    totals = jnp.stack([t.reshape(n_y * 2, -1, 2 * aux_local) for t in totals], axis=1)
    totals = lax.all_to_all(totals, ("y", "x_lo"), 0, 0, tiled=True)
    totals = totals.reshape(n_y, 2, 2, ROWS_DEV // 4, n_z, 2 * aux_local)
    return total_over_x(x_hi, totals)


def solution(mesh):
    n_y = 4
    n_z = mesh.shape["aux"] // (2 * n_y)
    split = Mesh(
        mesh.devices.reshape(n_y, 2, n_z, 2, 2), ("y", "x_hi", "z", "x_lo", "core")
    )
    aux, pair = ("y", "x_hi", "z"), ("x_lo", "core")
    return jax.shard_map(
        functools.partial(on_device, n_y, n_z),
        mesh=split,
        in_specs=(P(aux, pair), P(pair), P(pair), P(), P(), P(), P()),
        out_specs=P(pair, None, aux),
        check_vma=False,
    )
```

time: 144 us -> 134 us (0.931)
  between operations: 14.3 us -> 0.98 us
  blocking collectives: 32.4 us -> 38.1 us
  starting transfers between devices: 41 us -> 38.6 us
  Pallas kernels: 9.78 us -> 12 us
  local copies, waits for them, and re-layouts: 4.57 us -> 2.41 us
    ppermute x2 -> x6, starting transfers between devices: 11.8 us -> 26.3 us  [the longest x3 10.3 us: on_device(): lax.ppermute(coeffs, 'y', shifts[shift])]
    all_to_all x1, starting transfers between devices: 15.7 us -> 6.53 us  [on_device(): last = lax.all_to_all(last, 'z', 0, 0, tiled=True)]
    all_to_all x1, waiting for transfers between devices: 0.01 us -> 6.77 us  [on_device(): last = lax.all_to_all(last, 'z', 0, 0, tiled=True)]
    all_gather x1, blocking collectives: 32.4 us -> 38.1 us  [on_device(): gathered = lax.all_gather(rows[:-1], 'z', axis=0)]
    all_to_all x2 -> x1, starting transfers between devices: 8.81 us -> 3.6 us  [on_device(): totals = lax.all_to_all(totals, ('y', 'x_lo'), 0, 0, tiled=True)]
    all_gather x1 -> x0, waiting for transfers between devices: 3.44 us -> none  [on_device(): coeffs_y = lax.all_gather(coeffs, 'y', axis=0)]
    ppermute x1, starting transfers between devices: 4.65 us -> 2.14 us  [on_device(): partner = lax.ppermute(own, 'x_hi', swap)]
    pallas_call x3, Pallas kernels: 8.1 us -> 10.3 us  [the longest x2 7.23 us: products(): pl.pallas_call(functools.partial(product_kernel, n_away), grid=(n_y,), in...]
  transfers between devices with their start and end apart: 7 -> 9, of which waited for: 4 -> 3; matrix products, arithmetic and copies ran while one was open for 6% -> 5% of each run, Pallas kernels for 6% -> 8%
where the time goes in v3:
time: 134 us; the launch traced here: 133 us
  starting transfers between devices  38.6 us (29%)
  blocking collectives  38.1 us (28%)
  waiting for transfers between devices  35.5 us (26%)
  Pallas kernels  12 us (9%)
  other arithmetic  2.9 us (2%)
  matrix products  2.88 us (2%)
  local copies, waits for them, and re-layouts  2.41 us (2%)
    all_gather x1, blocking collectives, on_device(): gathered = lax.all_gather(rows[:-1], 'z', axis=0)  38.1 us
    all_to_all x1, waiting for transfers between devices, on_device(): totals = lax.all_to_all(totals, ('y', 'x_lo'), 0, 0, tiled=True)  26.7 us
    ppermute x3, starting transfers between devices, on_device(): lax.ppermute(coeffs, 'y', shifts[shift])  10.3 us
    ppermute x1, starting transfers between devices, on_device(): arrived = lax.ppermute(away, 'core', swap)  8.98 us
    pallas_call x2, Pallas kernels, products(): pl.pallas_call(functools.partial(product_kernel, n_away), grid=(n_y,), in...  7.23 us
    all_to_all x1, waiting for transfers between devices, on_device(): last = lax.all_to_all(last, 'z', 0, 0, tiled=True)  6.77 us
    all_to_all x1, starting transfers between devices, on_device(): last = lax.all_to_all(last, 'z', 0, 0, tiled=True)  6.53 us
    ppermute x1, starting transfers between devices, on_device(): lax.ppermute(rows[-1:], 'x_hi', swap)  4.65 us
  transfers between devices with their start and end apart: 9, of which 3 were waited for; matrix products, arithmetic and copies ran while one was open for 5% of the time, Pallas kernels for 8%

profile of v3, /device:TPU:1, one launch (start us, length us, event | category | flops | bytes accessed | tf_op | source)
XLA Modules:
  0.0 133.3 jit_solution(3839966774753279232)
XLA Ops:
  0.0 5.5 %collective-permute-start.1 = (bf16[256,2048]{1,0:T(8,128)(2,1)}, bf16[256,2048]{1,0:T(8,128)(2,1)S(1)}, u32[]{:S(2)}, u32[]{:S(2)}) collective-permute-start(bf16[256,2048]{1,0:T(8,128)(2,1)} %refs_0_.1), channel_id=1, source_target_pairs={{0,384},{128,0},{256,128},{384,256},{1,385},{129,1},{257,129},{385... | collective-permute-start | bytes 3145736 | tf_op jit(solution)/shard_map/ppermute | solution.py:152
  5.5 2.3 %collective-permute-start.2 = (bf16[256,2048]{1,0:T(8,128)(2,1)}, bf16[256,2048]{1,0:T(8,128)(2,1)}, u32[]{:S(2)}, u32[]{:S(2)}) collective-permute-start(bf16[256,2048]{1,0:T(8,128)(2,1)} %refs_0_.1), channel_id=1, source_target_pairs={{0,256},{128,384},{256,0},{384,128},{1,257},{129,385},{257,1},{385... | collective-permute-start | bytes 3145736 | tf_op jit(solution)/shard_map/ppermute | solution.py:152
  7.7 2.6 %collective-permute-start.3 = (bf16[256,2048]{1,0:T(8,128)(2,1)}, bf16[256,2048]{1,0:T(8,128)(2,1)}, u32[]{:S(2)}, u32[]{:S(2)}) collective-permute-start(bf16[256,2048]{1,0:T(8,128)(2,1)} %refs_0_.1), channel_id=1, source_target_pairs={{0,128},{128,256},{256,384},{384,0},{1,129},{129,257},{257,385},{3... | collective-permute-start | bytes 3145736 | tf_op jit(solution)/shard_map/ppermute | solution.py:152
  11.0 0.9 constant_dynamic-slice_fusion
  12.0 0.0 copy-start.1
  12.0 0.0 copy-start.2
  12.0 0.0 copy-start.4
  12.0 0.1 maximum_select_fusion
  12.1 4.7 %collective-permute-start = (bf16[1,2048]{1,0:T(2,128)(2,1)S(1)}, bf16[1,2048]{1,0:T(2,128)(2,1)S(1)}, u32[]{:S(2)}, u32[]{:S(2)}) collective-permute-start(bf16[1,2048]{1,0:T(2,128)(2,1)S(1)} %slice.27), channel_id=1, source_target_pairs={{0,64},{64,0},{1,65},{65,1},{2,66},{66,2},{3,67},{67,3},{4,68},{68... | collective-permute-start | bytes 12296 | tf_op jit(solution)/shard_map/ppermute | solution.py:154
  16.8 38.1 %all-gather.1 = bf16[16,15,2048]{2,1,0:T(8,128)(2,1)S(1)} all-gather(bf16[1,15,2048]{2,1,0:T(8,128)(2,1)S(1)} %slice_bitcast_fusion.2), channel_id=2, replica_groups=mesh['y'=4,'x_hi'=2,'z'=16,'x_lo'=2,'core'=2] {'z'}, dimensions={0}, use_global_device_ids=true | all-gather | bytes 1044480 | tf_op jit(solution)/shard_map/all_gather | solution.py:155
  54.9 0.7 mul.25
  55.6 0.6 copy.18
  56.2 0.0 copy-start
  56.2 0.7 broadcast_in_dim.6
  57.0 6.5 %all-to-all-start = ((bf16[16,2,2048]{2,1,0:T(2,128)(2,1)}), bf16[16,2,2048]{2,1,0:T(2,128)(2,1)S(1)}, u32[]{:S(2)}, u32[]{:S(2)}) async-start(bf16[16,2,2048]{2,1,0:T(2,128)(2,1)} %broadcast_in_dim.6), calls=%async_computation | async-start | bytes 262144 | tf_op jit(solution)/shard_map/all_to_all | solution.py:160
  63.5 2.1 %collective-permute-start.5 = (bf16[240,2048]{1,0:T(8,128)(2,1)S(1)}, bf16[240,2048]{1,0:T(8,128)(2,1)}, u32[]{:S(2)}, u32[]{:S(2)}) collective-permute-start(bf16[240,2048]{1,0:T(8,128)(2,1)S(1)} %bitcast.42), channel_id=1, source_target_pairs={{0,64},{64,0},{1,65},{65,1},{2,66},{66,2},{3,67},{67,3},{4,68},{68... | collective-permute-start | bytes 2949128 | tf_op jit(solution)/shard_map/ppermute | solution.py:158
  65.7 1.2 fusion
  66.9 1.7 %fusion.1 = f32[2048]{0:T(1024)S(1)} fusion(s32[2048]{0:T(1024)S(1)} %get-tuple-element.31, s32[2048]{0:T(1024)S(1)} %get-tuple-element.32, f32[20000]{0:T(1024)S(1)} %copy-done.3), kind=kOutput, calls=%fused_computation.5 | convolution fusion | flops 504428544 | bytes 104576 | tf_op jit(solution)/shard_map/dot_general | solution.py:23
  68.6 0.1 add_divide_fusion.refs_4_
  68.7 6.8 %all-to-all-done = bf16[16,2,2048]{2,1,0:T(2,128)(2,1)S(1)} async-done(((bf16[16,2,2048]{2,1,0:T(2,128)(2,1)}), bf16[16,2,2048]{2,1,0:T(2,128)(2,1)S(1)}, u32[]{:S(2)}, u32[]{:S(2)}) %all-to-all-start) | async-done | bytes 131104 | tf_op jit(solution)/shard_map/all_to_all | solution.py:160
  75.6 3.1 %shard_map.73.refs_2_ = bf16[4,512,2048]{2,1,0:T(8,128)(2,1)S(1)} custom-call(s32[1]{0:T(128)} %bitcast.9.y_ref, bf16[256,2048]{1,0:T(8,128)(2,1)S(1)} %copy-done, bf16[256,2048]{1,0:T(8,128)(2,1)S(1)} %collective-permute-done.1.refs_1_, bf16[256,2048]{1,0:T(8,128)(2,1)} %collective-permute-done.2.refs_2_, bf16[256,2048]{1,0:T(8,128)(2,1)} %collective-permute-done.3.refs_3_, ...), custom_call_target="tpu_custom_call" | custom-call | flops 1 | bytes 1 | tf_op jit(solution)/shard_map/pallas_call | solution.py:51
  78.7 3.0 %shard_map.74 = (f32[4,128,512]{2,1,0:T(8,128)S(1)}, f32[4,128,512]{2,1,0:T(8,128)S(1)}) custom-call(bf16[240,2048]{1,0:T(8,128)(2,1)S(1)} %bitcast.43, bf16[16,2048]{1,0:T(8,128)(2,1)S(1)} %get-tuple-element.21.refs_1_, bf16[4,512,2048]{2,1,0:T(8,128)(2,1)S(1)} %shard_map.73.refs_2_), custom_call_target="tpu_custom_call" | custom-call | flops 1 | bytes 1 | tf_op jit(solution)/shard_map/pallas_call | solution.py:87
  81.7 9.0 %collective-permute-start.4 = (f32[4,128,512]{2,1,0:T(8,128)S(1)}, f32[4,128,512]{2,1,0:T(8,128)S(1)}, u32[]{:S(2)}, u32[]{:S(2)}) collective-permute-start(f32[4,128,512]{2,1,0:T(8,128)S(1)} %get-tuple-element.18), channel_id=1, source_target_pairs={{0,1},{1,0},{2,3},{3,2},{4,5},{5,4},{6,7},{7,6},{8,9},{9,8},{10,11... | collective-permute-start | bytes 3145736 | tf_op jit(solution)/shard_map/ppermute | solution.py:173
  90.7 4.2 %shard_map.75 = (f32[4,128,512]{2,1,0:T(8,128)S(1)}, f32[4,128,512]{2,1,0:T(8,128)S(1)}) custom-call(bf16[240,2048]{1,0:T(8,128)(2,1)} %collective-permute-done.5.refs_0_, bf16[16,2048]{1,0:T(8,128)(2,1)S(1)} %get-tuple-element.22.refs_1_, bf16[4,512,2048]{2,1,0:T(8,128)(2,1)S(1)} %shard_map.73.refs_2_), custom_call_target="tpu_custom_call" | custom-call | flops 1 | bytes 1 | tf_op jit(solution)/shard_map/pallas_call | solution.py:87
  94.9 2.4 %collective-permute-start.6 = (f32[4,128,512]{2,1,0:T(8,128)S(1)}, f32[4,128,512]{2,1,0:T(8,128)S(1)}, u32[]{:S(2)}, u32[]{:S(2)}) collective-permute-start(f32[4,128,512]{2,1,0:T(8,128)S(1)} %get-tuple-element.20), channel_id=1, source_target_pairs={{0,1},{1,0},{2,3},{3,2},{4,5},{5,4},{6,7},{7,6},{8,9},{9,8},{10,11... | collective-permute-start | bytes 3145736 | tf_op jit(solution)/shard_map/ppermute | solution.py:176
  97.3 0.2 add.44
  97.5 2.0 %collective-permute-done.6 = f32[4,128,512]{2,1,0:T(8,128)S(1)} collective-permute-done((f32[4,128,512]{2,1,0:T(8,128)S(1)}, f32[4,128,512]{2,1,0:T(8,128)S(1)}, u32[]{:S(2)}, u32[]{:S(2)}) %collective-permute-start.6) | collective-permute-done | bytes 1048608 | tf_op jit(solution)/shard_map/ppermute | solution.py:176
  99.6 0.2 add.45
  99.8 1.6 %pad_maximum_fusion = f32[8,2,64,512]{3,2,1,0:T(8,128)} fusion(f32[8,1,64,512]{3,2,1,0:T(8,128)S(1)} %bitcast.46, f32[8,1,64,512]{3,2,1,0:T(8,128)S(1)} %bitcast.45), kind=kLoop, calls=%fused_computation.2 | loop fusion | flops 524288 | bytes 4194304 | tf_op jit(solution)/shard_map/stack | solution.py:177
  101.3 3.6 %all-to-all-start.1 = ((f32[8,2,64,512]{3,2,1,0:T(8,128)}), f32[8,2,64,512]{3,2,1,0:T(8,128)S(1)}, u32[]{:S(2)}, u32[]{:S(2)}) async-start(f32[8,2,64,512]{3,2,1,0:T(8,128)} %pad_maximum_fusion), calls=%async_computation.1 | async-start | bytes 4194304 | tf_op jit(solution)/shard_map/all_to_all | solution.py:178
  105.0 26.7 %all-to-all-done.1 = f32[8,2,64,512]{3,2,1,0:T(8,128)S(1)} async-done(((f32[8,2,64,512]{3,2,1,0:T(8,128)}), f32[8,2,64,512]{3,2,1,0:T(8,128)S(1)}, u32[]{:S(2)}, u32[]{:S(2)}) %all-to-all-start.1) | async-done | bytes 2097184 | tf_op jit(solution)/shard_map/all_to_all | solution.py:178
  131.6 1.7 %shard_map.76 = f32[2048,128]{1,0:T(8,128)} custom-call(s32[1]{0:T(128)} %bitcast.x_hi_ref, f32[4,2,2,4,16,512]{5,4,3,2,1,0:T(8,128)S(1)} %bitcast.41), custom_call_target="tpu_custom_call" | custom-call | tf_op jit(solution)/shard_map/pallas_call | solution.py:119
  (22 shorter events, 0.2 us)
Async XLA Ops:
  0.0 75.5 %collective-permute-start.1 = (bf16[256,2048]{1,0:T(8,128)(2,1)}, bf16[256,2048]{1,0:T(8,128)(2,1)S(1)}, u32[]{:S(2)}, u32[]{:S(2)}) collective-permute-start(bf16[256,2048]{1,0:T(8,128)(2,1)} %refs_0_.1), channel_id=1, source_target_pairs={{0,384},{128,0},{256,128},{384,256},{1,385},{129,1},{257,129},{385... | collective-permute-start | bytes 3145736 | tf_op jit(solution)/shard_map/ppermute | solution.py:152
  5.5 70.1 %collective-permute-start.2 = (bf16[256,2048]{1,0:T(8,128)(2,1)}, bf16[256,2048]{1,0:T(8,128)(2,1)}, u32[]{:S(2)}, u32[]{:S(2)}) collective-permute-start(bf16[256,2048]{1,0:T(8,128)(2,1)} %refs_0_.1), channel_id=1, source_target_pairs={{0,256},{128,384},{256,0},{384,128},{1,257},{129,385},{257,1},{385... | collective-permute-start | bytes 3145736 | tf_op jit(solution)/shard_map/ppermute | solution.py:152
  7.7 67.8 %collective-permute-start.3 = (bf16[256,2048]{1,0:T(8,128)(2,1)}, bf16[256,2048]{1,0:T(8,128)(2,1)}, u32[]{:S(2)}, u32[]{:S(2)}) collective-permute-start(bf16[256,2048]{1,0:T(8,128)(2,1)} %refs_0_.1), channel_id=1, source_target_pairs={{0,128},{128,256},{256,384},{384,0},{1,129},{129,257},{257,385},{3... | collective-permute-start | bytes 3145736 | tf_op jit(solution)/shard_map/ppermute | solution.py:152
  12.0 53.7 %copy-start.1 = (s32[2048]{0:T(1024)S(1)}, s32[2048]{0:T(1024)}, u32[]{:S(2)}) copy-start(s32[2048]{0:T(1024)} %param.8) | copy-start | bytes 24580
  12.0 53.7 %copy-start.2 = (s32[2048]{0:T(1024)S(1)}, s32[2048]{0:T(1024)}, u32[]{:S(2)}) copy-start(s32[2048]{0:T(1024)} %param.9) | copy-start | bytes 24580
  12.0 53.7 %copy-start.4 = (f32[2000]{0:T(1024)S(1)}, f32[2000]{0:T(1024)}, u32[]{:S(2)}) copy-start(f32[2000]{0:T(1024)} %param.10) | copy-start | bytes 24004
  12.1 43.5 %collective-permute-start = (bf16[1,2048]{1,0:T(2,128)(2,1)S(1)}, bf16[1,2048]{1,0:T(2,128)(2,1)S(1)}, u32[]{:S(2)}, u32[]{:S(2)}) collective-permute-start(bf16[1,2048]{1,0:T(2,128)(2,1)S(1)} %slice.27), channel_id=1, source_target_pairs={{0,64},{64,0},{1,65},{65,1},{2,66},{66,2},{3,67},{67,3},{4,68},{68... | collective-permute-start | bytes 12296 | tf_op jit(solution)/shard_map/ppermute | solution.py:154
  54.9 12.0 %copy-start.3 = (f32[20000]{0:T(1024)S(1)}, f32[20000]{0:T(1024)}, u32[]{:S(2)}) copy-start(f32[20000]{0:T(1024)} %param.11) | copy-start | bytes 240004
  56.2 19.3 %copy-start = (bf16[256,2048]{1,0:T(8,128)(2,1)S(1)}, bf16[256,2048]{1,0:T(8,128)(2,1)}, u32[]{:S(2)}) copy-start(bf16[256,2048]{1,0:T(8,128)(2,1)} %refs_0_.1) | copy-start | bytes 3145732
  57.0 18.5 %all-to-all-start = ((bf16[16,2,2048]{2,1,0:T(2,128)(2,1)}), bf16[16,2,2048]{2,1,0:T(2,128)(2,1)S(1)}, u32[]{:S(2)}, u32[]{:S(2)}) async-start(bf16[16,2,2048]{2,1,0:T(2,128)(2,1)} %broadcast_in_dim.6), calls=%async_computation | async-start | bytes 262144 | tf_op jit(solution)/shard_map/all_to_all | solution.py:160
  63.5 27.2 %collective-permute-start.5 = (bf16[240,2048]{1,0:T(8,128)(2,1)S(1)}, bf16[240,2048]{1,0:T(8,128)(2,1)}, u32[]{:S(2)}, u32[]{:S(2)}) collective-permute-start(bf16[240,2048]{1,0:T(8,128)(2,1)S(1)} %bitcast.42), channel_id=1, source_target_pairs={{0,64},{64,0},{1,65},{65,1},{2,66},{66,2},{3,67},{67,3},{4,68},{68... | collective-permute-start | bytes 2949128 | tf_op jit(solution)/shard_map/ppermute | solution.py:158
  81.7 15.6 %collective-permute-start.4 = (f32[4,128,512]{2,1,0:T(8,128)S(1)}, f32[4,128,512]{2,1,0:T(8,128)S(1)}, u32[]{:S(2)}, u32[]{:S(2)}) collective-permute-start(f32[4,128,512]{2,1,0:T(8,128)S(1)} %get-tuple-element.18), channel_id=1, source_target_pairs={{0,1},{1,0},{2,3},{3,2},{4,5},{5,4},{6,7},{7,6},{8,9},{9,8},{10,11... | collective-permute-start | bytes 3145736 | tf_op jit(solution)/shard_map/ppermute | solution.py:173
  94.9 4.6 %collective-permute-start.6 = (f32[4,128,512]{2,1,0:T(8,128)S(1)}, f32[4,128,512]{2,1,0:T(8,128)S(1)}, u32[]{:S(2)}, u32[]{:S(2)}) collective-permute-start(f32[4,128,512]{2,1,0:T(8,128)S(1)} %get-tuple-element.20), channel_id=1, source_target_pairs={{0,1},{1,0},{2,3},{3,2},{4,5},{5,4},{6,7},{7,6},{8,9},{9,8},{10,11... | collective-permute-start | bytes 3145736 | tf_op jit(solution)/shard_map/ppermute | solution.py:176
  101.3 30.3 %all-to-all-start.1 = ((f32[8,2,64,512]{3,2,1,0:T(8,128)}), f32[8,2,64,512]{3,2,1,0:T(8,128)S(1)}, u32[]{:S(2)}, u32[]{:S(2)}) async-start(f32[8,2,64,512]{3,2,1,0:T(8,128)} %pad_maximum_fusion), calls=%async_computation.1 | async-start | bytes 4194304 | tf_op jit(solution)/shard_map/all_to_all | solution.py:178

commit v4 on v3

v4 whole, which is shorter than its diff:
```python
import functools

import jax
import jax.numpy as jnp
from jax import lax
from jax.experimental import pallas as pl
from jax.experimental.pallas import tpu as pltpu
from jax.sharding import Mesh
from jax.sharding import PartitionSpec as P

ROWS_DEV = 16
LANES = 128
SENT = jnp.bfloat16
VMEM = 24 * 1024 * 1024
SMALL = pl.CostEstimate(flops=1, bytes_accessed=1, transcendentals=0)


def lookup(table, index):
    rows = -(-table.shape[0] // LANES)
    rows += -rows % 8
    grid = jnp.pad(table, (0, rows * LANES - table.shape[0])).reshape(rows, LANES)
    high = (index // LANES)[:, None] == jnp.arange(rows, dtype=jnp.int32)[None, :]
    low = (index % LANES)[:, None] == jnp.arange(LANES, dtype=jnp.int32)[None, :]
    picked = lax.dot_general(
        high.astype(jnp.float32),
        grid,
        (((1,), (0,)), ((), ())),
        precision=lax.Precision.HIGHEST,
        preferred_element_type=jnp.float32,
    )
    return jnp.sum(jnp.where(low, picked, 0.0), axis=1)


def scale_kernel(y_ref, *refs):
    del y_ref
    *coeffs_refs, response_ref, out_ref = refs
    for step, coeffs_ref in enumerate(coeffs_refs):

        @pl.when(pl.program_id(0) == step)
        def _(coeffs_ref=coeffs_ref):
            coeffs = coeffs_ref[...].astype(jnp.float32)
            aux_local = coeffs.shape[0]
            for w in range(2):
                out_ref[0, w * aux_local : (w + 1) * aux_local] = (
                    coeffs * response_ref[w : w + 1, :]
                ).astype(jnp.bfloat16)


def scale(y, coeffs, response):
    n_y = len(coeffs)
    aux_local, depth = coeffs[0].shape
    return pl.pallas_call(
        scale_kernel,
        grid_spec=pltpu.PrefetchScalarGridSpec(
            num_scalar_prefetch=1,
            grid=(n_y,),
            in_specs=[
                *[pl.BlockSpec((aux_local, depth), lambda i, y: (0, 0))] * n_y,
                pl.BlockSpec(response.shape, lambda i, y: (0, 0)),
            ],
            out_specs=pl.BlockSpec(
                (1, 2 * aux_local, depth), lambda i, y: (lax.rem(i + y[0], n_y), 0, 0)
            ),
        ),
        out_shape=jax.ShapeDtypeStruct((n_y, 2 * aux_local, depth), jnp.bfloat16),
        compiler_params=pltpu.CompilerParams(vmem_limit_bytes=VMEM),
        cost_estimate=SMALL,
    )(y, *coeffs, response)


def product_kernel(near_ref, far_ref, scaled_ref, away_ref, kept_ref):
    size = near_ref.shape[0] // 4
    rows = [ref[at * size : (at + 1) * size] for at in range(4) for ref in (near_ref, far_ref)]
    product = lax.dot_general(
        jnp.concatenate(rows, axis=0),
        scaled_ref[0],
        (((1,), (1,)), ((), ())),
        preferred_element_type=jnp.float32,
    )
    half = product.shape[0] // 2
    away_ref[0] = product[:half]
    kept_ref[0] = product[half:]


def products(near, far, scaled):
    n_rows, depth = near.shape
    n_y, columns, _ = scaled.shape
    rows = pl.BlockSpec((n_rows, depth), lambda y: (0, 0))
    return pl.pallas_call(
        product_kernel,
        grid=(n_y,),
        in_specs=[rows, rows, pl.BlockSpec((1, columns, depth), lambda y: (y, 0, 0))],
        out_specs=[pl.BlockSpec((1, n_rows, columns), lambda y: (y, 0, 0))] * 2,
        out_shape=[jax.ShapeDtypeStruct((n_y, n_rows, columns), jnp.float32)] * 2,
        compiler_params=pltpu.CompilerParams(vmem_limit_bytes=VMEM),
        cost_estimate=SMALL,
    )(near, far, scaled)


def add_kernel(*refs):
    *refs, out_ref = refs
    for side in range(2):
        total = refs[2 * side][0] + refs[2 * side + 1][0]
        total = total.reshape((2, -1) + total.shape[1:])
        out_ref[:, side] = total.astype(out_ref.dtype)


def add_cores(own, partner):
    n_y, n_rows, columns = own[0].shape
    return pl.pallas_call(
        add_kernel,
        grid=(n_y,),
        in_specs=[pl.BlockSpec((1, n_rows, columns), lambda y: (y, 0, 0))] * 4,
        out_specs=pl.BlockSpec((2, 2, n_rows // 2, columns), lambda y: (y, 0, 0, 0)),
        out_shape=jax.ShapeDtypeStruct((2 * n_y, 2, n_rows // 2, columns), SENT),
        compiler_params=pltpu.CompilerParams(vmem_limit_bytes=VMEM),
        cost_estimate=SMALL,
    )(*own, *partner)


def total_kernel(place_ref, parts_ref, out_ref):
    n_y, _, _, _, _, n_z, _ = parts_ref.shape
    x_hi, parity = place_ref[0], place_ref[1]
    for y in range(n_y):
        for side in range(2):
            for odd in range(2):
                at = jnp.bitwise_xor(side, x_hi), jnp.bitwise_xor(odd, parity)
                rows = [parts_ref[y, x, at[0], at[1], 0].astype(jnp.float32) for x in range(2)]
                rows = rows[0] + rows[1]
                base = ((2 * y + side) * 2 * n_z + odd) * 4
                for w in range(2):
                    for half in range(2):
                        c = (2 * w + half) * LANES
                        out_ref[pl.ds(base + 2 * half + w, n_z, stride=8), :] = rows[
                            :, c : c + LANES
                        ]


def total_over_x(place, parts):
    n_y, n_x, n_sides, n_parities, n_i, n_z, columns = parts.shape
    n_rows = n_y * n_sides * n_parities * n_z
    out = pl.pallas_call(
        total_kernel,
        grid_spec=pltpu.PrefetchScalarGridSpec(
            num_scalar_prefetch=1,
            grid=(n_i,),
            in_specs=[
                pl.BlockSpec(
                    (n_y, n_x, n_sides, n_parities, 1, n_z, columns),
                    lambda i, place: (0, 0, 0, 0, i, 0, 0),
                )
            ],
            out_specs=pl.BlockSpec((n_rows * 4, LANES), lambda i, place: (i, 0)),
        ),
        out_shape=jax.ShapeDtypeStruct((n_i * n_rows * 4, LANES), jnp.float32),
        compiler_params=pltpu.CompilerParams(vmem_limit_bytes=VMEM),
    )(place, parts)
    out = out.reshape(n_i * n_rows, 2, 2, LANES)
    return jnp.transpose(out, (0, 2, 1, 3)).reshape(-1, 2, 2 * LANES)


def on_device(n_y, n_z, coeffs, occ_index, vir_index, eps_occ, eps_vir, frequencies, offset):
    aux_local, depth = coeffs.shape
    core = lax.axis_index("core")
    place = jnp.stack([lax.axis_index("x_hi"), lax.axis_index("parity")]).astype(jnp.int32)
    y = lax.axis_index("y").reshape(1).astype(jnp.int32)
    swap = [(0, 1), (1, 0)]

    rows = lax.dynamic_slice_in_dim(coeffs, offset[0], ROWS_DEV, 0)
    rows = rows.reshape(2, 2, ROWS_DEV // 4, depth)
    first, second = rows[:, 0], rows[:, 1]
    rows = jnp.where(core == 0, jnp.stack([second, first]), jnp.stack([first, second]))
    rows = rows.reshape(ROWS_DEV, depth)

    shifts = [[(i, (i - shift) % n_y) for i in range(n_y)] for shift in range(n_y)]
    coeffs_y = [coeffs] + [lax.ppermute(coeffs, "y", shifts[shift]) for shift in range(1, n_y)]

    z = ("half_z", "parity")
    gathered = lax.all_gather(rows, "half_z", axis=0)
    near = jnp.transpose(gathered, (1, 0, 2)).reshape(-1, depth)
    middle = near.shape[0] // 2
    near_partner = lax.ppermute(near, "x_hi", swap)
    far = jnp.concatenate(
        [
            lax.ppermute(near[:middle], z, [(i, (i + 1) % n_z) for i in range(n_z)]),
            lax.ppermute(near[middle:], z, [(i, (i - 1) % n_z) for i in range(n_z)]),
        ],
        axis=0,
    )
    far_partner = lax.ppermute(far, "x_hi", swap)

    occ_index, vir_index, _ = lax.optimization_barrier((occ_index, vir_index, gathered))
    energy_gap = lookup(eps_vir, vir_index) - lookup(eps_occ, occ_index)
    squares = frequencies * frequencies
    response = (
        2.0 * energy_gap[None, :] / (energy_gap[None, :] * energy_gap[None, :] + squares[:, None])
    )
    scaled = scale(y, coeffs_y, response)

    sides = []
    for side in ((near, far), (near_partner, far_partner)):
        away, kept = products(*side, scaled)
        sides.append((kept, lax.ppermute(away, "core", swap)))
    parts = lax.all_to_all(add_cores(*sides), ("y", "x_lo"), 0, 0, tiled=True)
    parts = parts.reshape(n_y, 2, 2, 2, ROWS_DEV // 4, n_z // 2, 2 * aux_local)
    return total_over_x(place, parts)


def solution(mesh):
    n_y = 4
    n_z = mesh.shape["aux"] // (2 * n_y)
    split = Mesh(
        mesh.devices.reshape(n_y, 2, n_z // 2, 2, 2, 2),
        ("y", "x_hi", "half_z", "parity", "x_lo", "core"),
    )
    aux, pair = ("y", "x_hi", "half_z", "parity"), ("x_lo", "core")
    return jax.shard_map(
        functools.partial(on_device, n_y, n_z),
        mesh=split,
        in_specs=(P(aux, pair), P(pair), P(pair), P(), P(), P(), P()),
        out_specs=P(pair, None, aux),
        check_vma=False,
    )
```

time: 134 us -> 119 us (0.89)
  waiting for transfers between devices: 35.5 us -> 27.7 us
  blocking collectives: 38.1 us -> 33.9 us
  other arithmetic: 2.9 us -> 0.25 us
  Pallas kernels: 12 us -> 14.1 us
    all_to_all x2 -> x1, waiting for transfers between devices: 33.4 us -> 15.4 us  [on_device(): parts = lax.all_to_all(add_cores(*sides), ('y', 'x_lo'), 0, 0, tiled=True)]
    ppermute x4 -> x6, waiting for transfers between devices: 2.05 us -> 12.3 us  [the longest x1 9.62 us: on_device(): far_partner = lax.ppermute(far, 'x_hi', swap)]
    all_to_all x2 -> x1, starting transfers between devices: 10.1 us -> 3.56 us  [on_device(): parts = lax.all_to_all(add_cores(*sides), ('y', 'x_lo'), 0, 0, tiled=True)]
    ppermute x4 -> x6, starting transfers between devices: 18.1 us -> 23.4 us  [the longest x2 10.1 us: on_device(): sides.append((kept, lax.ppermute(away, 'core', swap)))]
    all_gather x1, blocking collectives: 38.1 us -> 33.9 us  [on_device(): gathered = lax.all_gather(rows, 'half_z', axis=0)]
    pallas_call x2 -> x3, Pallas kernels: 7.23 us -> 8.79 us  [the longest x2 7.21 us: products(): pl.pallas_call(product_kernel, grid=(n_y,), in_specs=[rows, rows, pl.Bloc...]
    another operation x1, other arithmetic: 1.56 us -> 0.08 us  [on_device(): jnp.stack([lax.axis_index('x_hi'), lax.axis_index('parity')])]
  transfers between devices with their start and end apart: 9 -> 10, of which waited for: 3 -> 4; matrix products, arithmetic and copies ran while one was open for 5% -> 4% of each run, Pallas kernels for 8% -> 5%
where the time goes in v4:
time: 119 us
  starting transfers between devices  37.4 us (31%)
  blocking collectives  33.9 us (28%)
  waiting for transfers between devices  27.7 us (23%)
  Pallas kernels  14.1 us (12%)
  matrix products  2.88 us (2%)
  local copies, waits for them, and re-layouts  1.71 us (1%)
    all_gather x1, blocking collectives, on_device(): gathered = lax.all_gather(rows, 'half_z', axis=0)  33.9 us
    all_to_all x1, waiting for transfers between devices, on_device(): parts = lax.all_to_all(add_cores(*sides), ('y', 'x_lo'), 0, 0, tiled=True)  15.4 us
    ppermute x3, starting transfers between devices, on_device(): lax.ppermute(coeffs, 'y', shifts[shift])  10.5 us
    ppermute x2, starting transfers between devices, on_device(): sides.append((kept, lax.ppermute(away, 'core', swap)))  10.1 us
    ppermute x1, waiting for transfers between devices, on_device(): far_partner = lax.ppermute(far, 'x_hi', swap)  9.62 us
    pallas_call x2, Pallas kernels, products(): pl.pallas_call(product_kernel, grid=(n_y,), in_specs=[rows, rows, pl.Bloc...  7.21 us
    ppermute x1, starting transfers between devices, on_device(): near_partner = lax.ppermute(near, 'x_hi', swap)  4.64 us
    ppermute x1, starting transfers between devices, on_device(): lax.ppermute(near[middle:], z, [(i, (i - 1) % n_z) for i in range(n_z)])  3.76 us
  transfers between devices with their start and end apart: 10, of which 4 were waited for; matrix products, arithmetic and copies ran while one was open for 4% of the time, Pallas kernels for 5%

profile of v4, /device:TPU:1, one launch (start us, length us, event | category | flops | bytes accessed | tf_op | source)
XLA Modules:
  0.0 119.0 jit_solution(15125722847589922202)
XLA Ops:
  0.0 5.6 %collective-permute-start.2 = (bf16[256,2048]{1,0:T(8,128)(2,1)}, bf16[256,2048]{1,0:T(8,128)(2,1)S(1)}, u32[]{:S(2)}, u32[]{:S(2)}) collective-permute-start(bf16[256,2048]{1,0:T(8,128)(2,1)} %refs_0_.1), channel_id=1, source_target_pairs={{0,384},{128,0},{256,128},{384,256},{1,385},{129,1},{257,129},{385... | collective-permute-start | bytes 3145736 | tf_op jit(solution)/shard_map/ppermute | solution.py:176
  5.6 2.3 %collective-permute-start.3 = (bf16[256,2048]{1,0:T(8,128)(2,1)}, bf16[256,2048]{1,0:T(8,128)(2,1)}, u32[]{:S(2)}, u32[]{:S(2)}) collective-permute-start(bf16[256,2048]{1,0:T(8,128)(2,1)} %refs_0_.1), channel_id=1, source_target_pairs={{0,256},{128,384},{256,0},{384,128},{1,257},{129,385},{257,1},{385... | collective-permute-start | bytes 3145736 | tf_op jit(solution)/shard_map/ppermute | solution.py:176
  7.9 2.6 %collective-permute-start.4 = (bf16[256,2048]{1,0:T(8,128)(2,1)}, bf16[256,2048]{1,0:T(8,128)(2,1)}, u32[]{:S(2)}, u32[]{:S(2)}) collective-permute-start(bf16[256,2048]{1,0:T(8,128)(2,1)} %refs_0_.1), channel_id=1, source_target_pairs={{0,128},{128,256},{256,384},{384,0},{1,129},{129,257},{257,385},{3... | collective-permute-start | bytes 3145736 | tf_op jit(solution)/shard_map/ppermute | solution.py:176
  11.2 0.9 constant_dynamic-slice_fusion
  12.2 0.1 maximum_select_fusion
  12.2 33.9 %all_gather.3 = bf16[8,16,2048]{2,1,0:T(8,128)(2,1)S(1)} all-gather(bf16[1,16,2048]{2,1,0:T(8,128)(2,1)S(1)} %select_n.50), channel_id=1, replica_groups=mesh['y'=4,'x_hi'=2,'half_z'=8,'parity'=2,'x_lo'=2,'core'=2] {'half_z'}, dimensions={0}, use_global_device_ids=true | all-gather | bytes 589824 | tf_op jit(solution)/shard_map/all_gather | solution.py:179
  46.2 0.2 copy.25
  46.4 2.7 %collective-permute-start = (bf16[64,2048]{1,0:T(8,128)(2,1)S(1)}, bf16[64,2048]{1,0:T(8,128)(2,1)S(1)}, u32[]{:S(2)}, u32[]{:S(2)}) collective-permute-start(bf16[64,2048]{1,0:T(8,128)(2,1)S(1)} %bitcast.41), channel_id=1, source_target_pairs={{0,4},{4,8},{8,12},{12,16},{16,20},{20,24},{24,28},{28,32},{32,36}... | collective-permute-start | bytes 786440 | tf_op jit(solution)/shard_map/ppermute | solution.py:185
  49.1 0.2 copy.24
  49.3 3.8 %collective-permute-start.1 = (bf16[64,2048]{1,0:T(8,128)(2,1)S(1)}, bf16[64,2048]{1,0:T(8,128)(2,1)S(1)}, u32[]{:S(2)}, u32[]{:S(2)}) collective-permute-start(bf16[64,2048]{1,0:T(8,128)(2,1)S(1)} %bitcast.40), channel_id=1, source_target_pairs={{0,60},{4,0},{8,4},{12,8},{16,12},{20,16},{24,20},{28,24},{32,28},... | collective-permute-start | bytes 786440 | tf_op jit(solution)/shard_map/ppermute | solution.py:186
  53.1 1.7 %fusion.1 = f32[2048]{0:T(1024)S(1)} fusion(s32[2048]{0:T(1024)S(1)} %get-tuple-element.27, s32[2048]{0:T(1024)S(1)} %get-tuple-element.28, f32[20000]{0:T(1024)S(1)} %copy-done.3), kind=kOutput, calls=%fused_computation.4 | convolution fusion | flops 504428544 | bytes 104576 | tf_op jit(solution)/shard_map/dot_general | solution.py:24
  54.8 0.0 copy-start.5
  54.8 0.0 copy-start
  54.8 1.2 %fusion = f32[2048]{0:T(1024)S(1)} fusion(s32[2048]{0:T(1024)S(1)} %get-tuple-element.24, s32[2048]{0:T(1024)S(1)} %get-tuple-element.23, f32[2000]{0:T(1024)S(1)} %copy-done.4), kind=kOutput, calls=%fused_computation.3 | convolution fusion | flops 51148800 | bytes 32576 | tf_op jit(solution)/shard_map/dot_general | solution.py:24
  56.0 0.3 copy.23
  56.3 0.0 collective-permute-done
  56.3 4.6 %collective-permute-start.6 = (bf16[128,2048]{1,0:T(8,128)(2,1)S(1)}, bf16[128,2048]{1,0:T(8,128)(2,1)}, u32[]{:S(2)}, u32[]{:S(2)}) collective-permute-start(bf16[128,2048]{1,0:T(8,128)(2,1)S(1)} %bitcast.36), channel_id=1, source_target_pairs={{0,64},{64,0},{1,65},{65,1},{2,66},{66,2},{3,67},{67,3},{4,68},{68... | collective-permute-start | bytes 1572872 | tf_op jit(solution)/shard_map/ppermute | solution.py:182
  61.1 2.1 %collective-permute-start.7 = (bf16[128,2048]{1,0:T(8,128)(2,1)S(1)}, bf16[128,2048]{1,0:T(8,128)(2,1)}, u32[]{:S(2)}, u32[]{:S(2)}) collective-permute-start(bf16[128,2048]{1,0:T(8,128)(2,1)S(1)} %constant_dynamic-update-slice_fusion.far_ref), channel_id=1, source_target_pairs={{0,64},{64,0},{1,65},{65,1},{2,66},{66,2},{3,67},{67,3},{4,68},{68... | collective-permute-start | bytes 1572872 | tf_op jit(solution)/shard_map/ppermute | solution.py:190
  63.2 0.1 add_divide_fusion.refs_4_
  63.4 3.1 %shard_map.73.scaled_ref = bf16[4,512,2048]{2,1,0:T(8,128)(2,1)S(1)} custom-call(s32[1]{0:T(128)} %bitcast.9.y_ref, bf16[256,2048]{1,0:T(8,128)(2,1)S(1)} %copy-done, bf16[256,2048]{1,0:T(8,128)(2,1)S(1)} %collective-permute-done.2.refs_1_, bf16[256,2048]{1,0:T(8,128)(2,1)} %collective-permute-done.3.refs_2_, ...), custom_call_target="tpu_custom_call" | custom-call | flops 1 | bytes 1 | tf_op jit(solution)/shard_map/pallas_call | solution.py:52
  66.5 3.0 %shard_map.74 = (f32[4,128,512]{2,1,0:T(8,128)S(1)}, f32[4,128,512]{2,1,0:T(8,128)S(1)}) custom-call(bf16[128,2048]{1,0:T(8,128)(2,1)S(1)} %bitcast.37, bf16[128,2048]{1,0:T(8,128)(2,1)S(1)} %constant_dynamic-update-slice_fusion.far_ref, bf16[4,512,2048]{2,1,0:T(8,128)(2,1)S(1)} %shard_map.73.scaled_ref), custom_call_target="tpu_custom_call" | custom-call | flops 1 | bytes 1 | tf_op jit(solution)/shard_map/pallas_call | solution.py:89
  69.5 9.6 %collective-permute-done.7.far_ref = bf16[128,2048]{1,0:T(8,128)(2,1)} collective-permute-done((bf16[128,2048]{1,0:T(8,128)(2,1)S(1)}, bf16[128,2048]{1,0:T(8,128)(2,1)}, u32[]{:S(2)}, u32[]{:S(2)}) %collective-permute-start.7) | collective-permute-done | bytes 524320 | tf_op jit(solution)/shard_map/ppermute | solution.py:190
  79.1 4.2 %shard_map.75 = (f32[4,128,512]{2,1,0:T(8,128)S(1)}, f32[4,128,512]{2,1,0:T(8,128)S(1)}) custom-call(bf16[128,2048]{1,0:T(8,128)(2,1)} %collective-permute-done.6.near_ref, bf16[128,2048]{1,0:T(8,128)(2,1)} %collective-permute-done.7.far_ref, bf16[4,512,2048]{2,1,0:T(8,128)(2,1)S(1)} %shard_map.73.scaled_ref), custom_call_target="tpu_custom_call" | custom-call | flops 1 | bytes 1 | tf_op jit(solution)/shard_map/pallas_call | solution.py:89
  83.4 8.2 %collective-permute-start.8 = (f32[4,128,512]{2,1,0:T(8,128)S(1)}, f32[4,128,512]{2,1,0:T(8,128)S(1)}, u32[]{:S(2)}, u32[]{:S(2)}) collective-permute-start(f32[4,128,512]{2,1,0:T(8,128)S(1)} %get-tuple-element.16), channel_id=1, source_target_pairs={{0,1},{1,0},{2,3},{3,2},{4,5},{5,4},{6,7},{7,6},{8,9},{9,8},{10,11... | collective-permute-start | bytes 3145736 | tf_op jit(solution)/shard_map/ppermute | solution.py:203
  91.5 1.9 %collective-permute-start.5 = (f32[4,128,512]{2,1,0:T(8,128)S(1)}, f32[4,128,512]{2,1,0:T(8,128)S(1)}, u32[]{:S(2)}, u32[]{:S(2)}) collective-permute-start(f32[4,128,512]{2,1,0:T(8,128)S(1)} %get-tuple-element.14), channel_id=1, source_target_pairs={{0,1},{1,0},{2,3},{3,2},{4,5},{5,4},{6,7},{7,6},{8,9},{9,8},{10,11... | collective-permute-start | bytes 3145736 | tf_op jit(solution)/shard_map/ppermute | solution.py:203
  93.5 0.3 collective-permute-done.8.refs_3_
  93.8 2.3 %collective-permute-done.5.refs_1_ = f32[4,128,512]{2,1,0:T(8,128)S(1)} collective-permute-done((f32[4,128,512]{2,1,0:T(8,128)S(1)}, f32[4,128,512]{2,1,0:T(8,128)S(1)}, u32[]{:S(2)}, u32[]{:S(2)}) %collective-permute-start.5) | collective-permute-done | bytes 1048608 | tf_op jit(solution)/shard_map/ppermute | solution.py:203
  96.1 1.6 %shard_map.76 = bf16[8,2,64,512]{3,2,1,0:T(8,128)(2,1)} custom-call(f32[4,128,512]{2,1,0:T(8,128)S(1)} %get-tuple-element.13.refs_0_, f32[4,128,512]{2,1,0:T(8,128)S(1)} %collective-permute-done.5.refs_1_, f32[4,128,512]{2,1,0:T(8,128)S(1)} %get-tuple-element.15.refs_2_, f32[4,128,512]{2,1,0:T(8,128)S(1)} %collective-permute-done.8.refs_3_), custom_call_target="tpu_custom_call" | custom-call | flops 1 | bytes 1 | tf_op jit(solution)/shard_map/pallas_call | solution.py:110
  97.7 3.6 %all-to-all-start = ((bf16[8,2,64,512]{3,2,1,0:T(8,128)(2,1)}), bf16[8,2,64,512]{3,2,1,0:T(8,128)(2,1)S(1)}, u32[]{:S(2)}, u32[]{:S(2)}) async-start(bf16[8,2,64,512]{3,2,1,0:T(8,128)(2,1)} %shard_map.76), calls=%async_computation | async-start | bytes 2097152 | tf_op jit(solution)/shard_map/all_to_all | solution.py:204
  101.3 0.1 pad_add_fusion.place_ref
  101.3 15.4 %all-to-all-done = bf16[8,2,64,512]{3,2,1,0:T(8,128)(2,1)S(1)} async-done(((bf16[8,2,64,512]{3,2,1,0:T(8,128)(2,1)}), bf16[8,2,64,512]{3,2,1,0:T(8,128)(2,1)S(1)}, u32[]{:S(2)}, u32[]{:S(2)}) %all-to-all-start) | async-done | bytes 1048608 | tf_op jit(solution)/shard_map/all_to_all | solution.py:204
  116.8 2.2 %shard_map.77 = f32[2048,128]{1,0:T(8,128)} custom-call(s32[2]{0:T(128)S(1)} %pad_add_fusion.place_ref, bf16[4,2,2,2,4,8,512]{6,5,4,3,2,1,0:T(8,128)(2,1)S(1)} %bitcast.35), custom_call_target="tpu_custom_call" | custom-call | tf_op jit(solution)/shard_map/pallas_call | solution.py:142
  (24 shorter events, 0.2 us)
Async XLA Ops:
  0.0 53.0 %copy-start.1 = (s32[2048]{0:T(1024)S(1)}, s32[2048]{0:T(1024)}, u32[]{:S(2)}) copy-start(s32[2048]{0:T(1024)} %param.8) | copy-start | bytes 24580
  0.0 53.1 %copy-start.2 = (s32[2048]{0:T(1024)S(1)}, s32[2048]{0:T(1024)}, u32[]{:S(2)}) copy-start(s32[2048]{0:T(1024)} %param.9) | copy-start | bytes 24580
  0.0 53.1 %copy-start.3 = (f32[20000]{0:T(1024)S(1)}, f32[20000]{0:T(1024)}, u32[]{:S(2)}) copy-start(f32[20000]{0:T(1024)} %param.11) | copy-start | bytes 240004
  0.0 63.3 %collective-permute-start.2 = (bf16[256,2048]{1,0:T(8,128)(2,1)}, bf16[256,2048]{1,0:T(8,128)(2,1)S(1)}, u32[]{:S(2)}, u32[]{:S(2)}) collective-permute-start(bf16[256,2048]{1,0:T(8,128)(2,1)} %refs_0_.1), channel_id=1, source_target_pairs={{0,384},{128,0},{256,128},{384,256},{1,385},{129,1},{257,129},{385... | collective-permute-start | bytes 3145736 | tf_op jit(solution)/shard_map/ppermute | solution.py:176
  5.6 57.7 %collective-permute-start.3 = (bf16[256,2048]{1,0:T(8,128)(2,1)}, bf16[256,2048]{1,0:T(8,128)(2,1)}, u32[]{:S(2)}, u32[]{:S(2)}) collective-permute-start(bf16[256,2048]{1,0:T(8,128)(2,1)} %refs_0_.1), channel_id=1, source_target_pairs={{0,256},{128,384},{256,0},{384,128},{1,257},{129,385},{257,1},{385... | collective-permute-start | bytes 3145736 | tf_op jit(solution)/shard_map/ppermute | solution.py:176
  7.9 55.5 %collective-permute-start.4 = (bf16[256,2048]{1,0:T(8,128)(2,1)}, bf16[256,2048]{1,0:T(8,128)(2,1)}, u32[]{:S(2)}, u32[]{:S(2)}) collective-permute-start(bf16[256,2048]{1,0:T(8,128)(2,1)} %refs_0_.1), channel_id=1, source_target_pairs={{0,128},{128,256},{256,384},{384,0},{1,129},{129,257},{257,385},{3... | collective-permute-start | bytes 3145736 | tf_op jit(solution)/shard_map/ppermute | solution.py:176
  46.2 8.7 %copy-start.4 = (f32[2000]{0:T(1024)S(1)}, f32[2000]{0:T(1024)}, u32[]{:S(2)}) copy-start(f32[2000]{0:T(1024)} %param.10) | copy-start | bytes 24004
  46.4 10.0 %collective-permute-start = (bf16[64,2048]{1,0:T(8,128)(2,1)S(1)}, bf16[64,2048]{1,0:T(8,128)(2,1)S(1)}, u32[]{:S(2)}, u32[]{:S(2)}) collective-permute-start(bf16[64,2048]{1,0:T(8,128)(2,1)S(1)} %bitcast.41), channel_id=1, source_target_pairs={{0,4},{4,8},{8,12},{12,16},{16,20},{20,24},{24,28},{28,32},{32,36}... | collective-permute-start | bytes 786440 | tf_op jit(solution)/shard_map/ppermute | solution.py:185
  49.3 11.7 %collective-permute-start.1 = (bf16[64,2048]{1,0:T(8,128)(2,1)S(1)}, bf16[64,2048]{1,0:T(8,128)(2,1)S(1)}, u32[]{:S(2)}, u32[]{:S(2)}) collective-permute-start(bf16[64,2048]{1,0:T(8,128)(2,1)S(1)} %bitcast.40), channel_id=1, source_target_pairs={{0,60},{4,0},{8,4},{12,8},{16,12},{20,16},{24,20},{28,24},{32,28},... | collective-permute-start | bytes 786440 | tf_op jit(solution)/shard_map/ppermute | solution.py:186
  54.8 8.4 %copy-start.5 = (f32[2]{0:T(128)S(1)}, f32[2]{0:T(128)}, u32[]{:S(2)}) copy-start(f32[2]{0:T(128)} %param.12) | copy-start | bytes 28
  54.8 8.6 %copy-start = (bf16[256,2048]{1,0:T(8,128)(2,1)S(1)}, bf16[256,2048]{1,0:T(8,128)(2,1)}, u32[]{:S(2)}) copy-start(bf16[256,2048]{1,0:T(8,128)(2,1)} %refs_0_.1) | copy-start | bytes 3145732
  56.3 13.2 %collective-permute-start.6 = (bf16[128,2048]{1,0:T(8,128)(2,1)S(1)}, bf16[128,2048]{1,0:T(8,128)(2,1)}, u32[]{:S(2)}, u32[]{:S(2)}) collective-permute-start(bf16[128,2048]{1,0:T(8,128)(2,1)S(1)} %bitcast.36), channel_id=1, source_target_pairs={{0,64},{64,0},{1,65},{65,1},{2,66},{66,2},{3,67},{67,3},{4,68},{68... | collective-permute-start | bytes 1572872 | tf_op jit(solution)/shard_map/ppermute | solution.py:182
  61.1 18.1 %collective-permute-start.7 = (bf16[128,2048]{1,0:T(8,128)(2,1)S(1)}, bf16[128,2048]{1,0:T(8,128)(2,1)}, u32[]{:S(2)}, u32[]{:S(2)}) collective-permute-start(bf16[128,2048]{1,0:T(8,128)(2,1)S(1)} %constant_dynamic-update-slice_fusion.far_ref), channel_id=1, source_target_pairs={{0,64},{64,0},{1,65},{65,1},{2,66},{66,2},{3,67},{67,3},{4,68},{68... | collective-permute-start | bytes 1572872 | tf_op jit(solution)/shard_map/ppermute | solution.py:190
  83.4 10.5 %collective-permute-start.8 = (f32[4,128,512]{2,1,0:T(8,128)S(1)}, f32[4,128,512]{2,1,0:T(8,128)S(1)}, u32[]{:S(2)}, u32[]{:S(2)}) collective-permute-start(f32[4,128,512]{2,1,0:T(8,128)S(1)} %get-tuple-element.16), channel_id=1, source_target_pairs={{0,1},{1,0},{2,3},{3,2},{4,5},{5,4},{6,7},{7,6},{8,9},{9,8},{10,11... | collective-permute-start | bytes 3145736 | tf_op jit(solution)/shard_map/ppermute | solution.py:203
  91.5 4.6 %collective-permute-start.5 = (f32[4,128,512]{2,1,0:T(8,128)S(1)}, f32[4,128,512]{2,1,0:T(8,128)S(1)}, u32[]{:S(2)}, u32[]{:S(2)}) collective-permute-start(f32[4,128,512]{2,1,0:T(8,128)S(1)} %get-tuple-element.14), channel_id=1, source_target_pairs={{0,1},{1,0},{2,3},{3,2},{4,5},{5,4},{6,7},{7,6},{8,9},{9,8},{10,11... | collective-permute-start | bytes 3145736 | tf_op jit(solution)/shard_map/ppermute | solution.py:203
  97.7 19.1 %all-to-all-start = ((bf16[8,2,64,512]{3,2,1,0:T(8,128)(2,1)}), bf16[8,2,64,512]{3,2,1,0:T(8,128)(2,1)S(1)}, u32[]{:S(2)}, u32[]{:S(2)}) async-start(bf16[8,2,64,512]{3,2,1,0:T(8,128)(2,1)} %shard_map.76), calls=%async_computation | async-start | bytes 2097152 | tf_op jit(solution)/shard_map/all_to_all | solution.py:204

commit v5 on v4

--- a/solution.py
+++ b/solution.py
@@ -11,7 +11,7 @@
 ROWS_DEV = 16
 LANES = 128
 SENT = jnp.bfloat16
-VMEM = 24 * 1024 * 1024
+VMEM = 16 * 1024 * 1024
 SMALL = pl.CostEstimate(flops=1, bytes_accessed=1, transcendentals=0)
 
 
@@ -31,41 +31,29 @@
     return jnp.sum(jnp.where(low, picked, 0.0), axis=1)
 
 
-def scale_kernel(y_ref, *refs):
-    del y_ref
-    *coeffs_refs, response_ref, out_ref = refs
-    for step, coeffs_ref in enumerate(coeffs_refs):
-
-        @pl.when(pl.program_id(0) == step)
-        def _(coeffs_ref=coeffs_ref):
-            coeffs = coeffs_ref[...].astype(jnp.float32)
-            aux_local = coeffs.shape[0]
-            for w in range(2):
-                out_ref[0, w * aux_local : (w + 1) * aux_local] = (
-                    coeffs * response_ref[w : w + 1, :]
-                ).astype(jnp.bfloat16)
-
-
-def scale(y, coeffs, response):
-    n_y = len(coeffs)
-    aux_local, depth = coeffs[0].shape
+def scale_kernel(coeffs_ref, response_ref, out_ref):
+    coeffs = coeffs_ref[0].astype(jnp.float32)
+    aux_local = coeffs.shape[0]
+    for w in range(2):
+        out_ref[0, w * aux_local : (w + 1) * aux_local] = (
+            coeffs * response_ref[w : w + 1, :]
+        ).astype(jnp.bfloat16)
+
+
+def scale(coeffs, response):
+    n_y, aux_local, depth = coeffs.shape
     return pl.pallas_call(
         scale_kernel,
-        grid_spec=pltpu.PrefetchScalarGridSpec(
-            num_scalar_prefetch=1,
-            grid=(n_y,),
-            in_specs=[
-                *[pl.BlockSpec((aux_local, depth), lambda i, y: (0, 0))] * n_y,
-                pl.BlockSpec(response.shape, lambda i, y: (0, 0)),
-            ],
-            out_specs=pl.BlockSpec(
-                (1, 2 * aux_local, depth), lambda i, y: (lax.rem(i + y[0], n_y), 0, 0)
-            ),
-        ),
+        grid=(n_y,),
+        in_specs=[
+            pl.BlockSpec((1, aux_local, depth), lambda y: (y, 0, 0)),
+            pl.BlockSpec(response.shape, lambda y: (0, 0)),
+        ],
+        out_specs=pl.BlockSpec((1, 2 * aux_local, depth), lambda y: (y, 0, 0)),
         out_shape=jax.ShapeDtypeStruct((n_y, 2 * aux_local, depth), jnp.bfloat16),
         compiler_params=pltpu.CompilerParams(vmem_limit_bytes=VMEM),
         cost_estimate=SMALL,
-    )(y, *coeffs, response)
+    )(coeffs, response)
 
 
 def product_kernel(near_ref, far_ref, scaled_ref, away_ref, kept_ref):
@@ -163,7 +151,6 @@
     aux_local, depth = coeffs.shape
     core = lax.axis_index("core")
     place = jnp.stack([lax.axis_index("x_hi"), lax.axis_index("parity")]).astype(jnp.int32)
-    y = lax.axis_index("y").reshape(1).astype(jnp.int32)
     swap = [(0, 1), (1, 0)]
 
     rows = lax.dynamic_slice_in_dim(coeffs, offset[0], ROWS_DEV, 0)
@@ -172,30 +159,21 @@
     rows = jnp.where(core == 0, jnp.stack([second, first]), jnp.stack([first, second]))
     rows = rows.reshape(ROWS_DEV, depth)
 
-    shifts = [[(i, (i - shift) % n_y) for i in range(n_y)] for shift in range(n_y)]
-    coeffs_y = [coeffs] + [lax.ppermute(coeffs, "y", shifts[shift]) for shift in range(1, n_y)]
-
-    z = ("half_z", "parity")
+    coeffs_y = jnp.broadcast_to(coeffs[None], (n_y, aux_local, depth))
+    coeffs_y = lax.all_to_all(coeffs_y, "y", 0, 0, tiled=True)
+
     gathered = lax.all_gather(rows, "half_z", axis=0)
     near = jnp.transpose(gathered, (1, 0, 2)).reshape(-1, depth)
-    middle = near.shape[0] // 2
     near_partner = lax.ppermute(near, "x_hi", swap)
-    far = jnp.concatenate(
-        [
-            lax.ppermute(near[:middle], z, [(i, (i + 1) % n_z) for i in range(n_z)]),
-            lax.ppermute(near[middle:], z, [(i, (i - 1) % n_z) for i in range(n_z)]),
-        ],
-        axis=0,
-    )
+    far = lax.ppermute(near, "parity", swap)
     far_partner = lax.ppermute(far, "x_hi", swap)
 
-    occ_index, vir_index, _ = lax.optimization_barrier((occ_index, vir_index, gathered))
     energy_gap = lookup(eps_vir, vir_index) - lookup(eps_occ, occ_index)
     squares = frequencies * frequencies
     response = (
         2.0 * energy_gap[None, :] / (energy_gap[None, :] * energy_gap[None, :] + squares[:, None])
     )
-    scaled = scale(y, coeffs_y, response)
+    scaled = scale(coeffs_y, response)
 
     sides = []
     for side in ((near, far), (near_partner, far_partner)):

time: 119 us -> 109 us (0.916)
  waiting for transfers between devices: 27.7 us -> 17.4 us
  local copies, waits for them, and re-layouts: 1.71 us -> 5.04 us
  starting transfers between devices: 37.4 us -> 35.2 us
    ppermute x5 -> x1, starting transfers between devices: 17 us -> 2.81 us  [on_device(): far = lax.ppermute(near, 'parity', swap)]
    ppermute x1, waiting for transfers between devices: 9.62 us -> 0.01 us  [on_device(): far_partner = lax.ppermute(far, 'x_hi', swap)]
    all_to_all x0 -> x1, starting transfers between devices: none -> 5.16 us  [on_device(): coeffs_y = lax.all_to_all(coeffs_y, 'y', 0, 0, tiled=True)]
    broadcast_in_dim x0 -> x1, local copies, waits for them, and re-layouts: none -> 3.73 us  [on_device(): coeffs_y = jnp.broadcast_to(coeffs[None], (n_y, aux_local, depth))]
    ppermute x1, starting transfers between devices: 2.14 us -> 4.52 us  [on_device(): far_partner = lax.ppermute(far, 'x_hi', swap)]
    ppermute x2, starting transfers between devices: 10.1 us -> 12.4 us  [on_device(): sides.append((kept, lax.ppermute(away, 'core', swap)))]
    all_to_all x1, starting transfers between devices: 3.56 us -> 5.72 us  [on_device(): parts = lax.all_to_all(add_cores(*sides), ('y', 'x_lo'), 0, 0, tiled=True)]
  transfers between devices with their start and end apart: 10 -> 7, of which waited for: 4 -> 2; matrix products, arithmetic and copies ran while one was open for 4% -> 4% of each run, Pallas kernels for 5% -> 9%
where the time goes in v5:
time: 109 us; the launch traced here: 108 us
  starting transfers between devices  35.2 us (32%)
  blocking collectives  33.1 us (30%)
  waiting for transfers between devices  17.4 us (16%)
  Pallas kernels  13.4 us (12%)
  local copies, waits for them, and re-layouts  5.04 us (5%)
  matrix products  2.87 us (3%)
    all_gather x1, blocking collectives, on_device(): gathered = lax.all_gather(rows, 'half_z', axis=0)  33.1 us
    all_to_all x1, waiting for transfers between devices, on_device(): parts = lax.all_to_all(add_cores(*sides), ('y', 'x_lo'), 0, 0, tiled=True)  15.1 us
    ppermute x2, starting transfers between devices, on_device(): sides.append((kept, lax.ppermute(away, 'core', swap)))  12.4 us
    pallas_call x2, Pallas kernels, products(): pl.pallas_call(product_kernel, grid=(n_y,), in_specs=[rows, rows, pl.Bloc...  6.02 us
    all_to_all x1, starting transfers between devices, on_device(): parts = lax.all_to_all(add_cores(*sides), ('y', 'x_lo'), 0, 0, tiled=True)  5.72 us
    all_to_all x1, starting transfers between devices, on_device(): coeffs_y = lax.all_to_all(coeffs_y, 'y', 0, 0, tiled=True)  5.16 us
    ppermute x1, starting transfers between devices, on_device(): near_partner = lax.ppermute(near, 'x_hi', swap)  4.65 us
    ppermute x1, starting transfers between devices, on_device(): far_partner = lax.ppermute(far, 'x_hi', swap)  4.52 us
  transfers between devices with their start and end apart: 7, of which 2 were waited for; matrix products, arithmetic and copies ran while one was open for 4% of the time, Pallas kernels for 9%

profile of v5, /device:TPU:1, one launch (start us, length us, event | category | flops | bytes accessed | tf_op | source)
XLA Modules:
  0.0 108.1 jit_solution(2908100460019122108)
XLA Ops:
  0.0 3.7 %broadcast_in_dim.6 = bf16[4,256,2048]{2,1,0:T(8,128)(2,1)} broadcast(bf16[256,2048]{1,0:T(8,128)(2,1)} %param.7), dimensions={1,2} | broadcast | bytes 5242880 | tf_op jit(solution)/shard_map/broadcast_in_dim | solution.py:162
  3.7 5.2 %all-to-all-start = ((bf16[4,256,2048]{2,1,0:T(8,128)(2,1)}), bf16[4,256,2048]{2,1,0:T(8,128)(2,1)}, u32[]{:S(2)}, u32[]{:S(2)}) async-start(bf16[4,256,2048]{2,1,0:T(8,128)(2,1)} %broadcast_in_dim.6), calls=%async_computation | async-start | bytes 8388608 | tf_op jit(solution)/shard_map/all_to_all | solution.py:163
  9.6 0.9 constant_dynamic-slice_fusion
  10.6 0.1 maximum_select_fusion
  10.7 33.1 %all_gather.3 = bf16[8,16,2048]{2,1,0:T(8,128)(2,1)S(1)} all-gather(bf16[1,16,2048]{2,1,0:T(8,128)(2,1)S(1)} %select_n.50), channel_id=1, replica_groups=mesh['y'=4,'x_hi'=2,'half_z'=8,'parity'=2,'x_lo'=2,'core'=2] {'half_z'}, dimensions={0}, use_global_device_ids=true | all-gather | bytes 589824 | tf_op jit(solution)/shard_map/all_gather | solution.py:165
  43.7 0.3 copy.17
  44.0 2.8 %collective-permute-start = (bf16[128,2048]{1,0:T(8,128)(2,1)S(1)}, bf16[128,2048]{1,0:T(8,128)(2,1)S(1)}, u32[]{:S(2)}, u32[]{:S(2)}) collective-permute-start(bf16[128,2048]{1,0:T(8,128)(2,1)S(1)} %bitcast.29), channel_id=1, source_target_pairs={{0,4},{4,0},{1,5},{5,1},{2,6},{6,2},{3,7},{7,3},{8,12},{12,8},{9,1... | collective-permute-start | bytes 1572872 | tf_op jit(solution)/shard_map/ppermute | solution.py:168
  46.8 4.7 %collective-permute-start.2 = (bf16[128,2048]{1,0:T(8,128)(2,1)S(1)}, bf16[128,2048]{1,0:T(8,128)(2,1)S(1)}, u32[]{:S(2)}, u32[]{:S(2)}) collective-permute-start(bf16[128,2048]{1,0:T(8,128)(2,1)S(1)} %bitcast.30), channel_id=1, source_target_pairs={{0,64},{64,0},{1,65},{65,1},{2,66},{66,2},{3,67},{67,3},{4,68},{68... | collective-permute-start | bytes 1572872 | tf_op jit(solution)/shard_map/ppermute | solution.py:167
  51.5 0.0 copy-done
  51.5 0.0 copy-done.3
  51.5 1.2 %fusion = f32[2048]{0:T(1024)S(1)} fusion(s32[2048]{0:T(1024)S(1)} %get-tuple-element.18, s32[2048]{0:T(1024)S(1)} %get-tuple-element.17, f32[2000]{0:T(1024)S(1)} %copy-done.3), kind=kOutput, calls=%fused_computation.3 | convolution fusion | flops 51148800 | bytes 32576 | tf_op jit(solution)/shard_map/dot_general | solution.py:24
  52.7 0.0 copy-done.1
  52.8 0.0 copy-done.2
  52.8 1.7 %fusion.1 = f32[2048]{0:T(1024)S(1)} fusion(s32[2048]{0:T(1024)S(1)} %get-tuple-element.20, s32[2048]{0:T(1024)S(1)} %get-tuple-element.19, f32[20000]{0:T(1024)S(1)} %copy-done.2), kind=kOutput, calls=%fused_computation.4 | convolution fusion | flops 504428544 | bytes 104576 | tf_op jit(solution)/shard_map/dot_general | solution.py:24
  54.5 0.0 collective-permute-done.far_ref
  54.5 4.5 %collective-permute-start.3 = (bf16[128,2048]{1,0:T(8,128)(2,1)S(1)}, bf16[128,2048]{1,0:T(8,128)(2,1)S(1)}, u32[]{:S(2)}, u32[]{:S(2)}) collective-permute-start(bf16[128,2048]{1,0:T(8,128)(2,1)S(1)} %collective-permute-done.far_ref), channel_id=1, source_target_pairs={{0,64},{64,0},{1,65},{65,1},{2,66},{66,2},{3,67},{67,3},{4,68},{68... | collective-permute-start | bytes 1572872 | tf_op jit(solution)/shard_map/ppermute | solution.py:169
  59.0 0.1 add_divide_fusion.response_ref
  59.1 0.0 all-to-all-done.coeffs_ref
  59.1 3.6 %shard_map.73.scaled_ref = bf16[4,512,2048]{2,1,0:T(8,128)(2,1)S(1)} custom-call(bf16[4,256,2048]{2,1,0:T(8,128)(2,1)} %all-to-all-done.coeffs_ref, f32[2,2048]{1,0:T(2,128)S(1)} %add_divide_fusion.response_ref), custom_call_target="tpu_custom_call" | custom-call | flops 1 | bytes 1 | tf_op jit(solution)/shard_map/pallas_call | solution.py:45
  62.8 3.0 %shard_map.74 = (f32[4,128,512]{2,1,0:T(8,128)S(1)}, f32[4,128,512]{2,1,0:T(8,128)S(1)}) custom-call(bf16[128,2048]{1,0:T(8,128)(2,1)S(1)} %bitcast.31, bf16[128,2048]{1,0:T(8,128)(2,1)S(1)} %collective-permute-done.far_ref, bf16[4,512,2048]{2,1,0:T(8,128)(2,1)S(1)} %shard_map.73.scaled_ref), custom_call_target="tpu_custom_call" | custom-call | flops 1 | bytes 1 | tf_op jit(solution)/shard_map/pallas_call | solution.py:77
  65.8 8.3 %collective-permute-start.1 = (f32[4,128,512]{2,1,0:T(8,128)S(1)}, f32[4,128,512]{2,1,0:T(8,128)S(1)}, u32[]{:S(2)}, u32[]{:S(2)}) collective-permute-start(f32[4,128,512]{2,1,0:T(8,128)S(1)} %get-tuple-element.10), channel_id=1, source_target_pairs={{0,1},{1,0},{2,3},{3,2},{4,5},{5,4},{6,7},{7,6},{8,9},{9,8},{10,11... | collective-permute-start | bytes 3145736 | tf_op jit(solution)/shard_map/ppermute | solution.py:181
  74.1 0.0 collective-permute-done.2.near_ref
  74.1 0.0 collective-permute-done.3.far_ref
  74.1 3.0 %shard_map.75 = (f32[4,128,512]{2,1,0:T(8,128)S(1)}, f32[4,128,512]{2,1,0:T(8,128)S(1)}) custom-call(bf16[128,2048]{1,0:T(8,128)(2,1)S(1)} %collective-permute-done.2.near_ref, bf16[128,2048]{1,0:T(8,128)(2,1)S(1)} %collective-permute-done.3.far_ref, bf16[4,512,2048]{2,1,0:T(8,128)(2,1)S(1)} %shard_map.73.scaled_ref), custom_call_target="tpu_custom_call" | custom-call | flops 1 | bytes 1 | tf_op jit(solution)/shard_map/pallas_call | solution.py:77
  77.1 4.0 %collective-permute-start.4 = (f32[4,128,512]{2,1,0:T(8,128)S(1)}, f32[4,128,512]{2,1,0:T(8,128)S(1)}, u32[]{:S(2)}, u32[]{:S(2)}) collective-permute-start(f32[4,128,512]{2,1,0:T(8,128)S(1)} %get-tuple-element.12), channel_id=1, source_target_pairs={{0,1},{1,0},{2,3},{3,2},{4,5},{5,4},{6,7},{7,6},{8,9},{9,8},{10,11... | collective-permute-start | bytes 3145736 | tf_op jit(solution)/shard_map/ppermute | solution.py:181
  81.2 0.0 collective-permute-done.1.refs_1_
  81.2 2.3 %collective-permute-done.4.refs_3_ = f32[4,128,512]{2,1,0:T(8,128)S(1)} collective-permute-done((f32[4,128,512]{2,1,0:T(8,128)S(1)}, f32[4,128,512]{2,1,0:T(8,128)S(1)}, u32[]{:S(2)}, u32[]{:S(2)}) %collective-permute-start.4) | collective-permute-done | bytes 1048608 | tf_op jit(solution)/shard_map/ppermute | solution.py:181
  83.5 1.6 %shard_map.76 = bf16[8,2,64,512]{3,2,1,0:T(8,128)(2,1)} custom-call(f32[4,128,512]{2,1,0:T(8,128)S(1)} %get-tuple-element.9.refs_0_, f32[4,128,512]{2,1,0:T(8,128)S(1)} %collective-permute-done.1.refs_1_, f32[4,128,512]{2,1,0:T(8,128)S(1)} %get-tuple-element.11.refs_2_, f32[4,128,512]{2,1,0:T(8,128)S(1)} %collective-permute-done.4.refs_3_), custom_call_target="tpu_custom_call" | custom-call | flops 1 | bytes 1 | tf_op jit(solution)/shard_map/pallas_call | solution.py:98
  85.0 5.7 %all-to-all-start.1 = ((bf16[8,2,64,512]{3,2,1,0:T(8,128)(2,1)}), bf16[8,2,64,512]{3,2,1,0:T(8,128)(2,1)S(1)}, u32[]{:S(2)}, u32[]{:S(2)}) async-start(bf16[8,2,64,512]{3,2,1,0:T(8,128)(2,1)} %shard_map.76), calls=%async_computation.1 | async-start | bytes 2097152 | tf_op jit(solution)/shard_map/all_to_all | solution.py:182
  90.8 0.1 pad_add_fusion.place_ref
  90.8 15.1 %all-to-all-done.1 = bf16[8,2,64,512]{3,2,1,0:T(8,128)(2,1)S(1)} async-done(((bf16[8,2,64,512]{3,2,1,0:T(8,128)(2,1)}), bf16[8,2,64,512]{3,2,1,0:T(8,128)(2,1)S(1)}, u32[]{:S(2)}, u32[]{:S(2)}) %all-to-all-start.1) | async-done | bytes 1048608 | tf_op jit(solution)/shard_map/all_to_all | solution.py:182
  105.9 2.2 %shard_map.77 = f32[2048,128]{1,0:T(8,128)} custom-call(s32[2]{0:T(128)S(1)} %pad_add_fusion.place_ref, bf16[4,2,2,2,4,8,512]{6,5,4,3,2,1,0:T(8,128)(2,1)S(1)} %bitcast.28), custom_call_target="tpu_custom_call" | custom-call | tf_op jit(solution)/shard_map/pallas_call | solution.py:130
  (13 shorter events, 0.1 us)
Async XLA Ops:
  3.7 47.8 %copy-start = (s32[2048]{0:T(1024)S(1)}, s32[2048]{0:T(1024)}, u32[]{:S(2)}) copy-start(s32[2048]{0:T(1024)} %param.8) | copy-start | bytes 24580
  3.7 47.8 %copy-start.3 = (f32[2000]{0:T(1024)S(1)}, f32[2000]{0:T(1024)}, u32[]{:S(2)}) copy-start(f32[2000]{0:T(1024)} %param.10) | copy-start | bytes 24004
  3.7 49.0 %copy-start.1 = (s32[2048]{0:T(1024)S(1)}, s32[2048]{0:T(1024)}, u32[]{:S(2)}) copy-start(s32[2048]{0:T(1024)} %param.9) | copy-start | bytes 24580
  3.7 49.0 %copy-start.2 = (f32[20000]{0:T(1024)S(1)}, f32[20000]{0:T(1024)}, u32[]{:S(2)}) copy-start(f32[20000]{0:T(1024)} %param.11) | copy-start | bytes 240004
  3.7 55.4 %all-to-all-start = ((bf16[4,256,2048]{2,1,0:T(8,128)(2,1)}), bf16[4,256,2048]{2,1,0:T(8,128)(2,1)}, u32[]{:S(2)}, u32[]{:S(2)}) async-start(bf16[4,256,2048]{2,1,0:T(8,128)(2,1)} %broadcast_in_dim.6), calls=%async_computation | async-start | bytes 8388608 | tf_op jit(solution)/shard_map/all_to_all | solution.py:163
  8.9 50.1 %copy-start.4 = (f32[2]{0:T(128)S(1)}, f32[2]{0:T(128)}, u32[]{:S(2)}) copy-start(f32[2]{0:T(128)} %param.12) | copy-start | bytes 28
  44.0 10.4 %collective-permute-start = (bf16[128,2048]{1,0:T(8,128)(2,1)S(1)}, bf16[128,2048]{1,0:T(8,128)(2,1)S(1)}, u32[]{:S(2)}, u32[]{:S(2)}) collective-permute-start(bf16[128,2048]{1,0:T(8,128)(2,1)S(1)} %bitcast.29), channel_id=1, source_target_pairs={{0,4},{4,0},{1,5},{5,1},{2,6},{6,2},{3,7},{7,3},{8,12},{12,8},{9,1... | collective-permute-start | bytes 1572872 | tf_op jit(solution)/shard_map/ppermute | solution.py:168
  46.8 27.3 %collective-permute-start.2 = (bf16[128,2048]{1,0:T(8,128)(2,1)S(1)}, bf16[128,2048]{1,0:T(8,128)(2,1)S(1)}, u32[]{:S(2)}, u32[]{:S(2)}) collective-permute-start(bf16[128,2048]{1,0:T(8,128)(2,1)S(1)} %bitcast.30), channel_id=1, source_target_pairs={{0,64},{64,0},{1,65},{65,1},{2,66},{66,2},{3,67},{67,3},{4,68},{68... | collective-permute-start | bytes 1572872 | tf_op jit(solution)/shard_map/ppermute | solution.py:167
  54.5 19.6 %collective-permute-start.3 = (bf16[128,2048]{1,0:T(8,128)(2,1)S(1)}, bf16[128,2048]{1,0:T(8,128)(2,1)S(1)}, u32[]{:S(2)}, u32[]{:S(2)}) collective-permute-start(bf16[128,2048]{1,0:T(8,128)(2,1)S(1)} %collective-permute-done.far_ref), channel_id=1, source_target_pairs={{0,64},{64,0},{1,65},{65,1},{2,66},{66,2},{3,67},{67,3},{4,68},{68... | collective-permute-start | bytes 1572872 | tf_op jit(solution)/shard_map/ppermute | solution.py:169
  65.8 15.4 %collective-permute-start.1 = (f32[4,128,512]{2,1,0:T(8,128)S(1)}, f32[4,128,512]{2,1,0:T(8,128)S(1)}, u32[]{:S(2)}, u32[]{:S(2)}) collective-permute-start(f32[4,128,512]{2,1,0:T(8,128)S(1)} %get-tuple-element.10), channel_id=1, source_target_pairs={{0,1},{1,0},{2,3},{3,2},{4,5},{5,4},{6,7},{7,6},{8,9},{9,8},{10,11... | collective-permute-start | bytes 3145736 | tf_op jit(solution)/shard_map/ppermute | solution.py:181
  77.1 6.3 %collective-permute-start.4 = (f32[4,128,512]{2,1,0:T(8,128)S(1)}, f32[4,128,512]{2,1,0:T(8,128)S(1)}, u32[]{:S(2)}, u32[]{:S(2)}) collective-permute-start(f32[4,128,512]{2,1,0:T(8,128)S(1)} %get-tuple-element.12), channel_id=1, source_target_pairs={{0,1},{1,0},{2,3},{3,2},{4,5},{5,4},{6,7},{7,6},{8,9},{9,8},{10,11... | collective-permute-start | bytes 3145736 | tf_op jit(solution)/shard_map/ppermute | solution.py:181
  85.0 20.9 %all-to-all-start.1 = ((bf16[8,2,64,512]{3,2,1,0:T(8,128)(2,1)}), bf16[8,2,64,512]{3,2,1,0:T(8,128)(2,1)S(1)}, u32[]{:S(2)}, u32[]{:S(2)}) async-start(bf16[8,2,64,512]{3,2,1,0:T(8,128)(2,1)} %shard_map.76), calls=%async_computation.1 | async-start | bytes 2097152 | tf_op jit(solution)/shard_map/all_to_all | solution.py:182

commit v6 on v5

--- a/solution.py
+++ b/solution.py
@@ -1,4 +1,5 @@
 import functools
+import itertools
 
 import jax
 import jax.numpy as jnp
@@ -59,15 +60,14 @@
 def product_kernel(near_ref, far_ref, scaled_ref, away_ref, kept_ref):
     size = near_ref.shape[0] // 4
     rows = [ref[at * size : (at + 1) * size] for at in range(4) for ref in (near_ref, far_ref)]
-    product = lax.dot_general(
-        jnp.concatenate(rows, axis=0),
-        scaled_ref[0],
-        (((1,), (1,)), ((), ())),
-        preferred_element_type=jnp.float32,
-    )
-    half = product.shape[0] // 2
-    away_ref[0] = product[:half]
-    kept_ref[0] = product[half:]
+    rows = jnp.concatenate(rows, axis=0)
+    half = rows.shape[0] // 2
+    for y in range(scaled_ref.shape[0]):
+        product = lax.dot_general(
+            rows, scaled_ref[y], (((1,), (1,)), ((), ())), preferred_element_type=jnp.float32
+        )
+        away_ref[y] = product[:half]
+        kept_ref[y] = product[half:]
 
 
 def products(near, far, scaled):
@@ -76,9 +76,9 @@
     rows = pl.BlockSpec((n_rows, depth), lambda y: (0, 0))
     return pl.pallas_call(
         product_kernel,
-        grid=(n_y,),
-        in_specs=[rows, rows, pl.BlockSpec((1, columns, depth), lambda y: (y, 0, 0))],
-        out_specs=[pl.BlockSpec((1, n_rows, columns), lambda y: (y, 0, 0))] * 2,
+        grid=(n_y // 2,),
+        in_specs=[rows, rows, pl.BlockSpec((2, columns, depth), lambda y: (y, 0, 0))],
+        out_specs=[pl.BlockSpec((2, n_rows, columns), lambda y: (y, 0, 0))] * 2,
         out_shape=[jax.ShapeDtypeStruct((n_y, n_rows, columns), jnp.float32)] * 2,
         compiler_params=pltpu.CompilerParams(vmem_limit_bytes=VMEM),
         cost_estimate=SMALL,
@@ -88,8 +88,8 @@
 def add_kernel(*refs):
     *refs, out_ref = refs
     for side in range(2):
-        total = refs[2 * side][0] + refs[2 * side + 1][0]
-        total = total.reshape((2, -1) + total.shape[1:])
+        total = refs[2 * side][...] + refs[2 * side + 1][...]
+        total = total.reshape((out_ref.shape[0], -1, total.shape[-1]))
         out_ref[:, side] = total.astype(out_ref.dtype)
 
 
@@ -97,9 +97,9 @@
     n_y, n_rows, columns = own[0].shape
     return pl.pallas_call(
         add_kernel,
-        grid=(n_y,),
-        in_specs=[pl.BlockSpec((1, n_rows, columns), lambda y: (y, 0, 0))] * 4,
-        out_specs=pl.BlockSpec((2, 2, n_rows // 2, columns), lambda y: (y, 0, 0, 0)),
+        grid=(n_y // 2,),
+        in_specs=[pl.BlockSpec((2, n_rows, columns), lambda y: (y, 0, 0))] * 4,
+        out_specs=pl.BlockSpec((4, 2, n_rows // 2, columns), lambda y: (y, 0, 0, 0)),
         out_shape=jax.ShapeDtypeStruct((2 * n_y, 2, n_rows // 2, columns), SENT),
         compiler_params=pltpu.CompilerParams(vmem_limit_bytes=VMEM),
         cost_estimate=SMALL,
@@ -107,21 +107,17 @@
 
 
 def total_kernel(place_ref, parts_ref, out_ref):
-    n_y, _, _, _, _, n_z, _ = parts_ref.shape
+    n_y, _, _, _, n_i, n_z, _ = parts_ref.shape
     x_hi, parity = place_ref[0], place_ref[1]
-    for y in range(n_y):
-        for side in range(2):
-            for odd in range(2):
-                at = jnp.bitwise_xor(side, x_hi), jnp.bitwise_xor(odd, parity)
-                rows = [parts_ref[y, x, at[0], at[1], 0].astype(jnp.float32) for x in range(2)]
-                rows = rows[0] + rows[1]
-                base = ((2 * y + side) * 2 * n_z + odd) * 4
-                for w in range(2):
-                    for half in range(2):
-                        c = (2 * w + half) * LANES
-                        out_ref[pl.ds(base + 2 * half + w, n_z, stride=8), :] = rows[
-                            :, c : c + LANES
-                        ]
+    for i, y, side, odd in itertools.product(range(n_i), range(n_y), range(2), range(2)):
+        at = jnp.bitwise_xor(side, x_hi), jnp.bitwise_xor(odd, parity)
+        rows = [parts_ref[y, x, at[0], at[1], i].astype(jnp.float32) for x in range(2)]
+        rows = rows[0] + rows[1]
+        base = (((n_y * i + y) * 2 + side) * 2 * n_z + odd) * 4
+        for w in range(2):
+            for half in range(2):
+                c = (2 * w + half) * LANES
+                out_ref[pl.ds(base + 2 * half + w, n_z, stride=8), :] = rows[:, c : c + LANES]
 
 
 def total_over_x(place, parts):
@@ -131,14 +127,14 @@
         total_kernel,
         grid_spec=pltpu.PrefetchScalarGridSpec(
             num_scalar_prefetch=1,
-            grid=(n_i,),
+            grid=(n_i // 2,),
             in_specs=[
                 pl.BlockSpec(
-                    (n_y, n_x, n_sides, n_parities, 1, n_z, columns),
+                    (n_y, n_x, n_sides, n_parities, 2, n_z, columns),
                     lambda i, place: (0, 0, 0, 0, i, 0, 0),
                 )
             ],
-            out_specs=pl.BlockSpec((n_rows * 4, LANES), lambda i, place: (i, 0)),
+            out_specs=pl.BlockSpec((2 * n_rows * 4, LANES), lambda i, place: (i, 0)),
         ),
         out_shape=jax.ShapeDtypeStruct((n_i * n_rows * 4, LANES), jnp.float32),
         compiler_params=pltpu.CompilerParams(vmem_limit_bytes=VMEM),

time: 109 us -> 107 us (0.982)
  Pallas kernels: 13.4 us -> 11.6 us
    pallas_call x3, Pallas kernels: 7.61 us -> 6.26 us  [the longest x2 5.2 us: products(): pl.pallas_call(product_kernel, grid=(n_y // 2,), in_specs=[rows, rows, pl...]
  transfers between devices with their start and end apart: 7 -> 7, of which waited for: 2 -> 2; matrix products, arithmetic and copies ran while one was open for 4% -> 4% of each run, Pallas kernels for 9% -> 8%
where the time goes in v6:
time: 107 us
  starting transfers between devices  35.6 us (33%)
  blocking collectives  33.1 us (31%)
  waiting for transfers between devices  17.4 us (16%)
  Pallas kernels  11.6 us (11%)
  local copies, waits for them, and re-layouts  5.04 us (5%)
  matrix products  2.87 us (3%)
    all_gather x1, blocking collectives, on_device(): gathered = lax.all_gather(rows, 'half_z', axis=0)  33.1 us
    all_to_all x1, waiting for transfers between devices, on_device(): parts = lax.all_to_all(add_cores(*sides), ('y', 'x_lo'), 0, 0, tiled=True)  15.1 us
    ppermute x2, starting transfers between devices, on_device(): sides.append((kept, lax.ppermute(away, 'core', swap)))  12.8 us
    all_to_all x1, starting transfers between devices, on_device(): parts = lax.all_to_all(add_cores(*sides), ('y', 'x_lo'), 0, 0, tiled=True)  5.72 us
    pallas_call x2, Pallas kernels, products(): pl.pallas_call(product_kernel, grid=(n_y // 2,), in_specs=[rows, rows, pl...  5.2 us
    all_to_all x1, starting transfers between devices, on_device(): coeffs_y = lax.all_to_all(coeffs_y, 'y', 0, 0, tiled=True)  5.16 us
    ppermute x1, starting transfers between devices, on_device(): near_partner = lax.ppermute(near, 'x_hi', swap)  4.65 us
    ppermute x1, starting transfers between devices, on_device(): far_partner = lax.ppermute(far, 'x_hi', swap)  4.52 us
  transfers between devices with their start and end apart: 7, of which 2 were waited for; matrix products, arithmetic and copies ran while one was open for 4% of the time, Pallas kernels for 8%

profile of v6, /device:TPU:1, one launch (start us, length us, event | category | flops | bytes accessed | tf_op | source)
XLA Modules:
  0.0 106.7 jit_solution(756337247239386678)
XLA Ops:
  0.0 3.7 %broadcast_in_dim.6 = bf16[4,256,2048]{2,1,0:T(8,128)(2,1)} broadcast(bf16[256,2048]{1,0:T(8,128)(2,1)} %param.7), dimensions={1,2} | broadcast | bytes 5242880 | tf_op jit(solution)/shard_map/broadcast_in_dim | solution.py:158
  3.7 5.2 %all-to-all-start = ((bf16[4,256,2048]{2,1,0:T(8,128)(2,1)}), bf16[4,256,2048]{2,1,0:T(8,128)(2,1)}, u32[]{:S(2)}, u32[]{:S(2)}) async-start(bf16[4,256,2048]{2,1,0:T(8,128)(2,1)} %broadcast_in_dim.6), calls=%async_computation | async-start | bytes 8388608 | tf_op jit(solution)/shard_map/all_to_all | solution.py:159
  9.6 0.9 constant_dynamic-slice_fusion
  10.6 0.1 maximum_select_fusion
  10.7 33.1 %all_gather.3 = bf16[8,16,2048]{2,1,0:T(8,128)(2,1)S(1)} all-gather(bf16[1,16,2048]{2,1,0:T(8,128)(2,1)S(1)} %select_n.50), channel_id=1, replica_groups=mesh['y'=4,'x_hi'=2,'half_z'=8,'parity'=2,'x_lo'=2,'core'=2] {'half_z'}, dimensions={0}, use_global_device_ids=true | all-gather | bytes 589824 | tf_op jit(solution)/shard_map/all_gather | solution.py:161
  43.7 0.3 copy.17
  44.0 2.8 %collective-permute-start = (bf16[128,2048]{1,0:T(8,128)(2,1)S(1)}, bf16[128,2048]{1,0:T(8,128)(2,1)S(1)}, u32[]{:S(2)}, u32[]{:S(2)}) collective-permute-start(bf16[128,2048]{1,0:T(8,128)(2,1)S(1)} %bitcast.29), channel_id=1, source_target_pairs={{0,4},{4,0},{1,5},{5,1},{2,6},{6,2},{3,7},{7,3},{8,12},{12,8},{9,1... | collective-permute-start | bytes 1572872 | tf_op jit(solution)/shard_map/ppermute | solution.py:164
  46.8 4.7 %collective-permute-start.2 = (bf16[128,2048]{1,0:T(8,128)(2,1)S(1)}, bf16[128,2048]{1,0:T(8,128)(2,1)S(1)}, u32[]{:S(2)}, u32[]{:S(2)}) collective-permute-start(bf16[128,2048]{1,0:T(8,128)(2,1)S(1)} %bitcast.30), channel_id=1, source_target_pairs={{0,64},{64,0},{1,65},{65,1},{2,66},{66,2},{3,67},{67,3},{4,68},{68... | collective-permute-start | bytes 1572872 | tf_op jit(solution)/shard_map/ppermute | solution.py:163
  51.5 0.0 copy-done
  51.5 0.0 copy-done.3
  51.5 1.2 %fusion = f32[2048]{0:T(1024)S(1)} fusion(s32[2048]{0:T(1024)S(1)} %get-tuple-element.18, s32[2048]{0:T(1024)S(1)} %get-tuple-element.17, f32[2000]{0:T(1024)S(1)} %copy-done.3), kind=kOutput, calls=%fused_computation.3 | convolution fusion | flops 51148800 | bytes 32576 | tf_op jit(solution)/shard_map/dot_general | solution.py:25
  52.7 0.0 copy-done.1
  52.8 0.0 copy-done.2
  52.8 1.7 %fusion.1 = f32[2048]{0:T(1024)S(1)} fusion(s32[2048]{0:T(1024)S(1)} %get-tuple-element.20, s32[2048]{0:T(1024)S(1)} %get-tuple-element.19, f32[20000]{0:T(1024)S(1)} %copy-done.2), kind=kOutput, calls=%fused_computation.4 | convolution fusion | flops 504428544 | bytes 104576 | tf_op jit(solution)/shard_map/dot_general | solution.py:25
  54.5 0.0 collective-permute-done.far_ref
  54.5 4.5 %collective-permute-start.3 = (bf16[128,2048]{1,0:T(8,128)(2,1)S(1)}, bf16[128,2048]{1,0:T(8,128)(2,1)S(1)}, u32[]{:S(2)}, u32[]{:S(2)}) collective-permute-start(bf16[128,2048]{1,0:T(8,128)(2,1)S(1)} %collective-permute-done.far_ref), channel_id=1, source_target_pairs={{0,64},{64,0},{1,65},{65,1},{2,66},{66,2},{3,67},{67,3},{4,68},{68... | collective-permute-start | bytes 1572872 | tf_op jit(solution)/shard_map/ppermute | solution.py:165
  59.0 0.1 add_divide_fusion.response_ref
  59.1 0.0 all-to-all-done.coeffs_ref
  59.1 3.6 %shard_map.73.scaled_ref = bf16[4,512,2048]{2,1,0:T(8,128)(2,1)S(1)} custom-call(bf16[4,256,2048]{2,1,0:T(8,128)(2,1)} %all-to-all-done.coeffs_ref, f32[2,2048]{1,0:T(2,128)S(1)} %add_divide_fusion.response_ref), custom_call_target="tpu_custom_call" | custom-call | flops 1 | bytes 1 | tf_op jit(solution)/shard_map/pallas_call | solution.py:46
  62.8 2.6 %shard_map.74 = (f32[4,128,512]{2,1,0:T(8,128)S(1)}, f32[4,128,512]{2,1,0:T(8,128)S(1)}) custom-call(bf16[128,2048]{1,0:T(8,128)(2,1)S(1)} %bitcast.31, bf16[128,2048]{1,0:T(8,128)(2,1)S(1)} %collective-permute-done.far_ref, bf16[4,512,2048]{2,1,0:T(8,128)(2,1)S(1)} %shard_map.73.scaled_ref), custom_call_target="tpu_custom_call" | custom-call | flops 1 | bytes 1 | tf_op jit(solution)/shard_map/pallas_call | solution.py:77
  65.4 8.3 %collective-permute-start.1 = (f32[4,128,512]{2,1,0:T(8,128)S(1)}, f32[4,128,512]{2,1,0:T(8,128)S(1)}, u32[]{:S(2)}, u32[]{:S(2)}) collective-permute-start(f32[4,128,512]{2,1,0:T(8,128)S(1)} %get-tuple-element.10), channel_id=1, source_target_pairs={{0,1},{1,0},{2,3},{3,2},{4,5},{5,4},{6,7},{7,6},{8,9},{9,8},{10,11... | collective-permute-start | bytes 3145736 | tf_op jit(solution)/shard_map/ppermute | solution.py:177
  73.7 0.0 collective-permute-done.2.near_ref
  73.7 0.0 collective-permute-done.3.far_ref
  73.7 2.6 %shard_map.75 = (f32[4,128,512]{2,1,0:T(8,128)S(1)}, f32[4,128,512]{2,1,0:T(8,128)S(1)}) custom-call(bf16[128,2048]{1,0:T(8,128)(2,1)S(1)} %collective-permute-done.2.near_ref, bf16[128,2048]{1,0:T(8,128)(2,1)S(1)} %collective-permute-done.3.far_ref, bf16[4,512,2048]{2,1,0:T(8,128)(2,1)S(1)} %shard_map.73.scaled_ref), custom_call_target="tpu_custom_call" | custom-call | flops 1 | bytes 1 | tf_op jit(solution)/shard_map/pallas_call | solution.py:77
  76.3 4.5 %collective-permute-start.4 = (f32[4,128,512]{2,1,0:T(8,128)S(1)}, f32[4,128,512]{2,1,0:T(8,128)S(1)}, u32[]{:S(2)}, u32[]{:S(2)}) collective-permute-start(f32[4,128,512]{2,1,0:T(8,128)S(1)} %get-tuple-element.12), channel_id=1, source_target_pairs={{0,1},{1,0},{2,3},{3,2},{4,5},{5,4},{6,7},{7,6},{8,9},{9,8},{10,11... | collective-permute-start | bytes 3145736 | tf_op jit(solution)/shard_map/ppermute | solution.py:177
  80.8 0.0 collective-permute-done.1.refs_1_
  80.8 2.3 %collective-permute-done.4.refs_3_ = f32[4,128,512]{2,1,0:T(8,128)S(1)} collective-permute-done((f32[4,128,512]{2,1,0:T(8,128)S(1)}, f32[4,128,512]{2,1,0:T(8,128)S(1)}, u32[]{:S(2)}, u32[]{:S(2)}) %collective-permute-start.4) | collective-permute-done | bytes 1048608 | tf_op jit(solution)/shard_map/ppermute | solution.py:177
  83.0 1.1 shard_map.76
  84.1 5.7 %all-to-all-start.1 = ((bf16[8,2,64,512]{3,2,1,0:T(8,128)(2,1)}), bf16[8,2,64,512]{3,2,1,0:T(8,128)(2,1)S(1)}, u32[]{:S(2)}, u32[]{:S(2)}) async-start(bf16[8,2,64,512]{3,2,1,0:T(8,128)(2,1)} %shard_map.76), calls=%async_computation.1 | async-start | bytes 2097152 | tf_op jit(solution)/shard_map/all_to_all | solution.py:178
  89.8 0.1 pad_add_fusion.place_ref
  89.9 15.1 %all-to-all-done.1 = bf16[8,2,64,512]{3,2,1,0:T(8,128)(2,1)S(1)} async-done(((bf16[8,2,64,512]{3,2,1,0:T(8,128)(2,1)}), bf16[8,2,64,512]{3,2,1,0:T(8,128)(2,1)S(1)}, u32[]{:S(2)}, u32[]{:S(2)}) %all-to-all-start.1) | async-done | bytes 1048608 | tf_op jit(solution)/shard_map/all_to_all | solution.py:178
  105.0 1.7 %shard_map.77 = f32[2048,128]{1,0:T(8,128)} custom-call(s32[2]{0:T(128)S(1)} %pad_add_fusion.place_ref, bf16[4,2,2,2,4,8,512]{6,5,4,3,2,1,0:T(8,128)(2,1)S(1)} %bitcast.28), custom_call_target="tpu_custom_call" | custom-call | tf_op jit(solution)/shard_map/pallas_call | solution.py:126
  (13 shorter events, 0.1 us)
Async XLA Ops:
  3.7 47.8 %copy-start = (s32[2048]{0:T(1024)S(1)}, s32[2048]{0:T(1024)}, u32[]{:S(2)}) copy-start(s32[2048]{0:T(1024)} %param.8) | copy-start | bytes 24580
  3.7 47.8 %copy-start.3 = (f32[2000]{0:T(1024)S(1)}, f32[2000]{0:T(1024)}, u32[]{:S(2)}) copy-start(f32[2000]{0:T(1024)} %param.10) | copy-start | bytes 24004
  3.7 49.0 %copy-start.1 = (s32[2048]{0:T(1024)S(1)}, s32[2048]{0:T(1024)}, u32[]{:S(2)}) copy-start(s32[2048]{0:T(1024)} %param.9) | copy-start | bytes 24580
  3.7 49.0 %copy-start.2 = (f32[20000]{0:T(1024)S(1)}, f32[20000]{0:T(1024)}, u32[]{:S(2)}) copy-start(f32[20000]{0:T(1024)} %param.11) | copy-start | bytes 240004
  3.7 55.4 %all-to-all-start = ((bf16[4,256,2048]{2,1,0:T(8,128)(2,1)}), bf16[4,256,2048]{2,1,0:T(8,128)(2,1)}, u32[]{:S(2)}, u32[]{:S(2)}) async-start(bf16[4,256,2048]{2,1,0:T(8,128)(2,1)} %broadcast_in_dim.6), calls=%async_computation | async-start | bytes 8388608 | tf_op jit(solution)/shard_map/all_to_all | solution.py:159
  8.9 50.1 %copy-start.4 = (f32[2]{0:T(128)S(1)}, f32[2]{0:T(128)}, u32[]{:S(2)}) copy-start(f32[2]{0:T(128)} %param.12) | copy-start | bytes 28
  44.0 10.4 %collective-permute-start = (bf16[128,2048]{1,0:T(8,128)(2,1)S(1)}, bf16[128,2048]{1,0:T(8,128)(2,1)S(1)}, u32[]{:S(2)}, u32[]{:S(2)}) collective-permute-start(bf16[128,2048]{1,0:T(8,128)(2,1)S(1)} %bitcast.29), channel_id=1, source_target_pairs={{0,4},{4,0},{1,5},{5,1},{2,6},{6,2},{3,7},{7,3},{8,12},{12,8},{9,1... | collective-permute-start | bytes 1572872 | tf_op jit(solution)/shard_map/ppermute | solution.py:164
  46.8 26.8 %collective-permute-start.2 = (bf16[128,2048]{1,0:T(8,128)(2,1)S(1)}, bf16[128,2048]{1,0:T(8,128)(2,1)S(1)}, u32[]{:S(2)}, u32[]{:S(2)}) collective-permute-start(bf16[128,2048]{1,0:T(8,128)(2,1)S(1)} %bitcast.30), channel_id=1, source_target_pairs={{0,64},{64,0},{1,65},{65,1},{2,66},{66,2},{3,67},{67,3},{4,68},{68... | collective-permute-start | bytes 1572872 | tf_op jit(solution)/shard_map/ppermute | solution.py:163
  54.5 19.2 %collective-permute-start.3 = (bf16[128,2048]{1,0:T(8,128)(2,1)S(1)}, bf16[128,2048]{1,0:T(8,128)(2,1)S(1)}, u32[]{:S(2)}, u32[]{:S(2)}) collective-permute-start(bf16[128,2048]{1,0:T(8,128)(2,1)S(1)} %collective-permute-done.far_ref), channel_id=1, source_target_pairs={{0,64},{64,0},{1,65},{65,1},{2,66},{66,2},{3,67},{67,3},{4,68},{68... | collective-permute-start | bytes 1572872 | tf_op jit(solution)/shard_map/ppermute | solution.py:165
  65.4 15.4 %collective-permute-start.1 = (f32[4,128,512]{2,1,0:T(8,128)S(1)}, f32[4,128,512]{2,1,0:T(8,128)S(1)}, u32[]{:S(2)}, u32[]{:S(2)}) collective-permute-start(f32[4,128,512]{2,1,0:T(8,128)S(1)} %get-tuple-element.10), channel_id=1, source_target_pairs={{0,1},{1,0},{2,3},{3,2},{4,5},{5,4},{6,7},{7,6},{8,9},{9,8},{10,11... | collective-permute-start | bytes 3145736 | tf_op jit(solution)/shard_map/ppermute | solution.py:177
  76.3 6.7 %collective-permute-start.4 = (f32[4,128,512]{2,1,0:T(8,128)S(1)}, f32[4,128,512]{2,1,0:T(8,128)S(1)}, u32[]{:S(2)}, u32[]{:S(2)}) collective-permute-start(f32[4,128,512]{2,1,0:T(8,128)S(1)} %get-tuple-element.12), channel_id=1, source_target_pairs={{0,1},{1,0},{2,3},{3,2},{4,5},{5,4},{6,7},{7,6},{8,9},{9,8},{10,11... | collective-permute-start | bytes 3145736 | tf_op jit(solution)/shard_map/ppermute | solution.py:177
  84.1 20.9 %all-to-all-start.1 = ((bf16[8,2,64,512]{3,2,1,0:T(8,128)(2,1)}), bf16[8,2,64,512]{3,2,1,0:T(8,128)(2,1)S(1)}, u32[]{:S(2)}, u32[]{:S(2)}) async-start(bf16[8,2,64,512]{3,2,1,0:T(8,128)(2,1)} %shard_map.76), calls=%async_computation.1 | async-start | bytes 2097152 | tf_op jit(solution)/shard_map/all_to_all | solution.py:178

commit v7 on v6

--- a/solution.py
+++ b/solution.py
@@ -32,6 +32,35 @@
     return jnp.sum(jnp.where(low, picked, 0.0), axis=1)
 
 
+def repeat_kernel(source_ref, out_ref, block_ref, sems):
+    fetch = pltpu.make_async_copy(source_ref, block_ref, sems.at[0])
+    fetch.start()
+    fetch.wait()
+    copies = [
+        pltpu.make_async_copy(block_ref, out_ref.at[at], sems.at[at])
+        for at in range(out_ref.shape[0])
+    ]
+    for copy in copies:
+        copy.start()
+    for copy in copies:
+        copy.wait()
+
+
+def repeat(block, times):
+    return pl.pallas_call(
+        repeat_kernel,
+        in_specs=[pl.BlockSpec(memory_space=pltpu.HBM)],
+        out_specs=pl.BlockSpec(memory_space=pltpu.HBM),
+        out_shape=jax.ShapeDtypeStruct((times,) + block.shape, block.dtype),
+        scratch_shapes=[
+            pltpu.VMEM(block.shape, block.dtype),
+            pltpu.SemaphoreType.DMA((times,)),
+        ],
+        compiler_params=pltpu.CompilerParams(vmem_limit_bytes=60 * 1024 * 1024),
+        cost_estimate=SMALL,
+    )(block)
+
+
 def scale_kernel(coeffs_ref, response_ref, out_ref):
     coeffs = coeffs_ref[0].astype(jnp.float32)
     aux_local = coeffs.shape[0]
@@ -57,9 +86,13 @@
     )(coeffs, response)
 
 
-def product_kernel(near_ref, far_ref, scaled_ref, away_ref, kept_ref):
+def product_kernel(core_ref, near_ref, far_ref, scaled_ref, away_ref, kept_ref):
     size = near_ref.shape[0] // 4
-    rows = [ref[at * size : (at + 1) * size] for at in range(4) for ref in (near_ref, far_ref)]
+    rows = []
+    for core in (1 - core_ref[0], core_ref[0]):
+        for x in range(2):
+            at = pl.multiple_of((2 * x + core) * size, size)
+            rows += [ref[pl.ds(at, size)] for ref in (near_ref, far_ref)]
     rows = jnp.concatenate(rows, axis=0)
     half = rows.shape[0] // 2
     for y in range(scaled_ref.shape[0]):
@@ -70,19 +103,26 @@
         kept_ref[y] = product[half:]
 
 
-def products(near, far, scaled):
+def products(core, near, far, scaled):
     n_rows, depth = near.shape
     n_y, columns, _ = scaled.shape
-    rows = pl.BlockSpec((n_rows, depth), lambda y: (0, 0))
+    rows = pl.BlockSpec((n_rows, depth), lambda y, core: (0, 0))
     return pl.pallas_call(
         product_kernel,
-        grid=(n_y // 2,),
-        in_specs=[rows, rows, pl.BlockSpec((2, columns, depth), lambda y: (y, 0, 0))],
-        out_specs=[pl.BlockSpec((2, n_rows, columns), lambda y: (y, 0, 0))] * 2,
+        grid_spec=pltpu.PrefetchScalarGridSpec(
+            num_scalar_prefetch=1,
+            grid=(n_y // 2,),
+            in_specs=[
+                rows,
+                rows,
+                pl.BlockSpec((2, columns, depth), lambda y, core: (y, 0, 0)),
+            ],
+            out_specs=[pl.BlockSpec((2, n_rows, columns), lambda y, core: (y, 0, 0))] * 2,
+        ),
         out_shape=[jax.ShapeDtypeStruct((n_y, n_rows, columns), jnp.float32)] * 2,
         compiler_params=pltpu.CompilerParams(vmem_limit_bytes=VMEM),
         cost_estimate=SMALL,
-    )(near, far, scaled)
+    )(core, near, far, scaled)
 
 
 def add_kernel(*refs):
@@ -145,17 +185,13 @@
 
 def on_device(n_y, n_z, coeffs, occ_index, vir_index, eps_occ, eps_vir, frequencies, offset):
     aux_local, depth = coeffs.shape
-    core = lax.axis_index("core")
+    core = lax.axis_index("core").reshape(1).astype(jnp.int32)
     place = jnp.stack([lax.axis_index("x_hi"), lax.axis_index("parity")]).astype(jnp.int32)
     swap = [(0, 1), (1, 0)]
 
     rows = lax.dynamic_slice_in_dim(coeffs, offset[0], ROWS_DEV, 0)
-    rows = rows.reshape(2, 2, ROWS_DEV // 4, depth)
-    first, second = rows[:, 0], rows[:, 1]
-    rows = jnp.where(core == 0, jnp.stack([second, first]), jnp.stack([first, second]))
-    rows = rows.reshape(ROWS_DEV, depth)
-
-    coeffs_y = jnp.broadcast_to(coeffs[None], (n_y, aux_local, depth))
+
+    coeffs_y = repeat(coeffs, n_y)
     coeffs_y = lax.all_to_all(coeffs_y, "y", 0, 0, tiled=True)
 
     gathered = lax.all_gather(rows, "half_z", axis=0)
@@ -173,7 +209,7 @@
 
     sides = []
     for side in ((near, far), (near_partner, far_partner)):
-        away, kept = products(*side, scaled)
+        away, kept = products(core, *side, scaled)
         sides.append((kept, lax.ppermute(away, "core", swap)))
     parts = lax.all_to_all(add_cores(*sides), ("y", "x_lo"), 0, 0, tiled=True)
     parts = parts.reshape(n_y, 2, 2, 2, ROWS_DEV // 4, n_z // 2, 2 * aux_local)

time: 107 us -> 112 us (1.047)
  waiting for transfers between devices: 17.4 us -> 27.1 us
  starting transfers between devices: 35.6 us -> 31 us
  local copies, waits for them, and re-layouts: 5.04 us -> 1.24 us
  Pallas kernels: 11.6 us -> 14.8 us
    ppermute x1, waiting for transfers between devices: 0.01 us -> 9.12 us  [on_device(): far_partner = lax.ppermute(far, 'x_hi', swap)]
    ppermute x2, starting transfers between devices: 12.8 us -> 8.22 us  [on_device(): sides.append((kept, lax.ppermute(away, 'core', swap)))]
    broadcast_in_dim x1 -> x0, local copies, waits for them, and re-layouts: 3.73 us -> none  [on_device(): coeffs_y = jnp.broadcast_to(coeffs[None], (n_y, aux_local, depth))]
    pallas_call x2 -> x3, Pallas kernels: 5.2 us -> 8.42 us  [the longest x2 5.18 us: products(): pl.pallas_call(product_kernel, grid_spec=pltpu.PrefetchScalarGridSpec(num...]
  transfers between devices with their start and end apart: 7 -> 7, of which waited for: 2 -> 3; matrix products, arithmetic and copies ran while one was open for 4% -> 4% of each run, Pallas kernels for 8% -> 6%
where the time goes in v7:
time: 112 us; the launch traced here: 111 us
  blocking collectives  33.1 us (30%)
  starting transfers between devices  31 us (28%)
  waiting for transfers between devices  27.1 us (24%)
  Pallas kernels  14.8 us (13%)
  matrix products  2.87 us (3%)
  local copies, waits for them, and re-layouts  1.24 us (1%)
    all_gather x1, blocking collectives, on_device(): gathered = lax.all_gather(rows, 'half_z', axis=0)  33.1 us
    all_to_all x1, waiting for transfers between devices, on_device(): parts = lax.all_to_all(add_cores(*sides), ('y', 'x_lo'), 0, 0, tiled=True)  15.3 us
    ppermute x1, waiting for transfers between devices, on_device(): far_partner = lax.ppermute(far, 'x_hi', swap)  9.12 us
    ppermute x2, starting transfers between devices, on_device(): sides.append((kept, lax.ppermute(away, 'core', swap)))  8.22 us
    all_to_all x1, starting transfers between devices, on_device(): parts = lax.all_to_all(add_cores(*sides), ('y', 'x_lo'), 0, 0, tiled=True)  5.63 us
    pallas_call x2, Pallas kernels, products(): pl.pallas_call(product_kernel, grid_spec=pltpu.PrefetchScalarGridSpec(num...  5.18 us
    all_to_all x1, starting transfers between devices, on_device(): coeffs_y = lax.all_to_all(coeffs_y, 'y', 0, 0, tiled=True)  5.16 us
    ppermute x1, starting transfers between devices, on_device(): near_partner = lax.ppermute(near, 'x_hi', swap)  4.65 us
  transfers between devices with their start and end apart: 7, of which 3 were waited for; matrix products, arithmetic and copies ran while one was open for 4% of the time, Pallas kernels for 6%

profile of v7, /device:TPU:1, one launch (start us, length us, event | category | flops | bytes accessed | tf_op | source)
XLA Modules:
  0.0 111.1 jit_solution(7234958338573270440)
XLA Ops:
  0.0 3.2 %shard_map.73 = bf16[4,256,2048]{2,1,0:T(8,128)(2,1)} custom-call(bf16[256,2048]{1,0:T(8,128)(2,1)} %source_ref.1), custom_call_target="tpu_custom_call" | custom-call | flops 1 | bytes 1 | tf_op jit(solution)/shard_map/pallas_call | solution.py:50
  3.2 0.0 copy-start
  3.3 0.0 copy-start.3
  3.3 0.0 copy-start.1
  3.3 0.0 copy-start.2
  3.3 5.2 %all-to-all-start = ((bf16[4,256,2048]{2,1,0:T(8,128)(2,1)}), bf16[4,256,2048]{2,1,0:T(8,128)(2,1)}, u32[]{:S(2)}, u32[]{:S(2)}) async-start(bf16[4,256,2048]{2,1,0:T(8,128)(2,1)} %shard_map.73), calls=%async_computation | async-start | bytes 8388608 | tf_op jit(solution)/shard_map/all_to_all | solution.py:195
  9.1 0.9 constant_dynamic-slice_fusion
  10.0 33.1 %all-gather = bf16[128,2048]{1,0:T(8,128)(2,1)S(1)} all-gather(bf16[16,2048]{1,0:T(8,128)(2,1)S(1)} %constant_dynamic-slice_fusion), channel_id=2, replica_groups=mesh['y'=4,'x_hi'=2,'half_z'=8,'parity'=2,'x_lo'=2,'core'=2] {'half_z'}, dimensions={0}, use_global_device_ids=true | all-gather | bytes 589824 | tf_op jit(solution)/shard_map/all_gather | solution.py:197
  43.1 0.3 copy.11
  43.4 2.8 %collective-permute-start = (bf16[128,2048]{1,0:T(8,128)(2,1)S(1)}, bf16[128,2048]{1,0:T(8,128)(2,1)S(1)}, u32[]{:S(2)}, u32[]{:S(2)}) collective-permute-start(bf16[128,2048]{1,0:T(8,128)(2,1)S(1)} %bitcast.26), channel_id=1, source_target_pairs={{0,4},{4,0},{1,5},{5,1},{2,6},{6,2},{3,7},{7,3},{8,12},{12,8},{9,1... | collective-permute-start | bytes 1572872 | tf_op jit(solution)/shard_map/ppermute | solution.py:200
  46.2 4.7 %collective-permute-start.2 = (bf16[128,2048]{1,0:T(8,128)(2,1)S(1)}, bf16[128,2048]{1,0:T(8,128)(2,1)S(1)}, u32[]{:S(2)}, u32[]{:S(2)}) collective-permute-start(bf16[128,2048]{1,0:T(8,128)(2,1)S(1)} %bitcast.27), channel_id=1, source_target_pairs={{0,64},{64,0},{1,65},{65,1},{2,66},{66,2},{3,67},{67,3},{4,68},{68... | collective-permute-start | bytes 1572872 | tf_op jit(solution)/shard_map/ppermute | solution.py:199
  50.9 1.2 %fusion = f32[2048]{0:T(1024)S(1)} fusion(s32[2048]{0:T(1024)S(1)} %get-tuple-element.16, s32[2048]{0:T(1024)S(1)} %get-tuple-element.15, f32[2000]{0:T(1024)S(1)} %copy-done.3), kind=kOutput, calls=%fused_computation.3 | convolution fusion | flops 51148800 | bytes 32576 | tf_op jit(solution)/shard_map/dot_general | solution.py:25
  52.2 1.7 %fusion.1 = f32[2048]{0:T(1024)S(1)} fusion(s32[2048]{0:T(1024)S(1)} %get-tuple-element.18, s32[2048]{0:T(1024)S(1)} %get-tuple-element.17, f32[20000]{0:T(1024)S(1)} %copy-done.2), kind=kOutput, calls=%fused_computation.4 | convolution fusion | flops 504428544 | bytes 104576 | tf_op jit(solution)/shard_map/dot_general | solution.py:25
  53.8 0.0 collective-permute-done.far_ref
  53.9 4.5 %collective-permute-start.3 = (bf16[128,2048]{1,0:T(8,128)(2,1)S(1)}, bf16[128,2048]{1,0:T(8,128)(2,1)S(1)}, u32[]{:S(2)}, u32[]{:S(2)}) collective-permute-start(bf16[128,2048]{1,0:T(8,128)(2,1)S(1)} %collective-permute-done.far_ref), channel_id=1, source_target_pairs={{0,64},{64,0},{1,65},{65,1},{2,66},{66,2},{3,67},{67,3},{4,68},{68... | collective-permute-start | bytes 1572872 | tf_op jit(solution)/shard_map/ppermute | solution.py:201
  58.4 0.0 copy-done.4
  58.4 0.1 add_divide_fusion.response_ref
  58.5 0.0 all-to-all-done.coeffs_ref
  58.5 3.6 %shard_map.74.scaled_ref = bf16[4,512,2048]{2,1,0:T(8,128)(2,1)S(1)} custom-call(bf16[4,256,2048]{2,1,0:T(8,128)(2,1)} %all-to-all-done.coeffs_ref, f32[2,2048]{1,0:T(2,128)S(1)} %add_divide_fusion.response_ref), custom_call_target="tpu_custom_call" | custom-call | flops 1 | bytes 1 | tf_op jit(solution)/shard_map/pallas_call | solution.py:75
  62.1 0.0 collective-permute-done.2.near_ref
  62.1 9.1 %collective-permute-done.3.far_ref = bf16[128,2048]{1,0:T(8,128)(2,1)S(1)} collective-permute-done((bf16[128,2048]{1,0:T(8,128)(2,1)S(1)}, bf16[128,2048]{1,0:T(8,128)(2,1)S(1)}, u32[]{:S(2)}, u32[]{:S(2)}) %collective-permute-start.3) | collective-permute-done | bytes 524320 | tf_op jit(solution)/shard_map/ppermute | solution.py:201
  71.3 2.6 %shard_map.76 = (f32[4,128,512]{2,1,0:T(8,128)S(1)}, f32[4,128,512]{2,1,0:T(8,128)S(1)}) custom-call(s32[1]{0:T(128)} %bitcast.2.core_ref, bf16[128,2048]{1,0:T(8,128)(2,1)S(1)} %collective-permute-done.2.near_ref, bf16[128,2048]{1,0:T(8,128)(2,1)S(1)} %collective-permute-done.3.far_ref, bf16[4,512,2048]{2,1,0:T(8,128)(2,1)S(1)} %shard_map.74.scaled_ref), custom_call_target="tpu_custom_call" | custom-call | flops 1 | bytes 1 | tf_op jit(solution)/shard_map/pallas_call | solution.py:110
  73.8 6.3 %collective-permute-start.4 = (f32[4,128,512]{2,1,0:T(8,128)S(1)}, f32[4,128,512]{2,1,0:T(8,128)S(1)}, u32[]{:S(2)}, u32[]{:S(2)}) collective-permute-start(f32[4,128,512]{2,1,0:T(8,128)S(1)} %get-tuple-element.12), channel_id=1, source_target_pairs={{0,1},{1,0},{2,3},{3,2},{4,5},{5,4},{6,7},{7,6},{8,9},{9,8},{10,11... | collective-permute-start | bytes 3145736 | tf_op jit(solution)/shard_map/ppermute | solution.py:213
  80.1 2.6 %shard_map.75 = (f32[4,128,512]{2,1,0:T(8,128)S(1)}, f32[4,128,512]{2,1,0:T(8,128)S(1)}) custom-call(s32[1]{0:T(128)} %bitcast.2.core_ref, bf16[128,2048]{1,0:T(8,128)(2,1)S(1)} %bitcast.28, bf16[128,2048]{1,0:T(8,128)(2,1)S(1)} %collective-permute-done.far_ref, bf16[4,512,2048]{2,1,0:T(8,128)(2,1)S(1)} %shard_map.74.scaled_ref), custom_call_target="tpu_custom_call" | custom-call | flops 1 | bytes 1 | tf_op jit(solution)/shard_map/pallas_call | solution.py:110
  82.8 1.9 %collective-permute-start.1 = (f32[4,128,512]{2,1,0:T(8,128)S(1)}, f32[4,128,512]{2,1,0:T(8,128)S(1)}, u32[]{:S(2)}, u32[]{:S(2)}) collective-permute-start(f32[4,128,512]{2,1,0:T(8,128)S(1)} %get-tuple-element.10), channel_id=1, source_target_pairs={{0,1},{1,0},{2,3},{3,2},{4,5},{5,4},{6,7},{7,6},{8,9},{9,8},{10,11... | collective-permute-start | bytes 3145736 | tf_op jit(solution)/shard_map/ppermute | solution.py:213
  84.7 0.0 collective-permute-done.4.refs_3_
  84.7 2.6 %collective-permute-done.1.refs_1_ = f32[4,128,512]{2,1,0:T(8,128)S(1)} collective-permute-done((f32[4,128,512]{2,1,0:T(8,128)S(1)}, f32[4,128,512]{2,1,0:T(8,128)S(1)}, u32[]{:S(2)}, u32[]{:S(2)}) %collective-permute-start.1) | collective-permute-done | bytes 1048608 | tf_op jit(solution)/shard_map/ppermute | solution.py:213
  87.3 1.1 shard_map.77
  88.4 5.6 %all-to-all-start.1 = ((bf16[8,2,64,512]{3,2,1,0:T(8,128)(2,1)}), bf16[8,2,64,512]{3,2,1,0:T(8,128)(2,1)S(1)}, u32[]{:S(2)}, u32[]{:S(2)}) async-start(bf16[8,2,64,512]{3,2,1,0:T(8,128)(2,1)} %shard_map.77), calls=%async_computation.1 | async-start | bytes 2097152 | tf_op jit(solution)/shard_map/all_to_all | solution.py:214
  94.0 0.1 pad_add_fusion.place_ref
  94.1 15.3 %all-to-all-done.1 = bf16[8,2,64,512]{3,2,1,0:T(8,128)(2,1)S(1)} async-done(((bf16[8,2,64,512]{3,2,1,0:T(8,128)(2,1)}), bf16[8,2,64,512]{3,2,1,0:T(8,128)(2,1)S(1)}, u32[]{:S(2)}, u32[]{:S(2)}) %all-to-all-start.1) | async-done | bytes 1048608 | tf_op jit(solution)/shard_map/all_to_all | solution.py:214
  109.4 1.7 %shard_map.78 = f32[2048,128]{1,0:T(8,128)} custom-call(s32[2]{0:T(128)S(1)} %pad_add_fusion.place_ref, bf16[4,2,2,2,4,8,512]{6,5,4,3,2,1,0:T(8,128)(2,1)S(1)} %bitcast.25), custom_call_target="tpu_custom_call" | custom-call | tf_op jit(solution)/shard_map/pallas_call | solution.py:166
  (9 shorter events, 0.0 us)
Async XLA Ops:
  3.2 47.6 %copy-start = (s32[2048]{0:T(1024)S(1)}, s32[2048]{0:T(1024)}, u32[]{:S(2)}) copy-start(s32[2048]{0:T(1024)} %param.8) | copy-start | bytes 24580
  3.3 47.7 %copy-start.3 = (f32[2000]{0:T(1024)S(1)}, f32[2000]{0:T(1024)}, u32[]{:S(2)}) copy-start(f32[2000]{0:T(1024)} %param.10) | copy-start | bytes 24004
  3.3 48.9 %copy-start.1 = (s32[2048]{0:T(1024)S(1)}, s32[2048]{0:T(1024)}, u32[]{:S(2)}) copy-start(s32[2048]{0:T(1024)} %param.9) | copy-start | bytes 24580
  3.3 48.9 %copy-start.2 = (f32[20000]{0:T(1024)S(1)}, f32[20000]{0:T(1024)}, u32[]{:S(2)}) copy-start(f32[20000]{0:T(1024)} %param.11) | copy-start | bytes 240004
  3.3 55.2 %all-to-all-start = ((bf16[4,256,2048]{2,1,0:T(8,128)(2,1)}), bf16[4,256,2048]{2,1,0:T(8,128)(2,1)}, u32[]{:S(2)}, u32[]{:S(2)}) async-start(bf16[4,256,2048]{2,1,0:T(8,128)(2,1)} %shard_map.73), calls=%async_computation | async-start | bytes 8388608 | tf_op jit(solution)/shard_map/all_to_all | solution.py:195
  8.4 49.9 %copy-start.4 = (f32[2]{0:T(128)S(1)}, f32[2]{0:T(128)}, u32[]{:S(2)}) copy-start(f32[2]{0:T(128)} %param.12) | copy-start | bytes 28
  43.4 10.4 %collective-permute-start = (bf16[128,2048]{1,0:T(8,128)(2,1)S(1)}, bf16[128,2048]{1,0:T(8,128)(2,1)S(1)}, u32[]{:S(2)}, u32[]{:S(2)}) collective-permute-start(bf16[128,2048]{1,0:T(8,128)(2,1)S(1)} %bitcast.26), channel_id=1, source_target_pairs={{0,4},{4,0},{1,5},{5,1},{2,6},{6,2},{3,7},{7,3},{8,12},{12,8},{9,1... | collective-permute-start | bytes 1572872 | tf_op jit(solution)/shard_map/ppermute | solution.py:200
  46.2 15.9 %collective-permute-start.2 = (bf16[128,2048]{1,0:T(8,128)(2,1)S(1)}, bf16[128,2048]{1,0:T(8,128)(2,1)S(1)}, u32[]{:S(2)}, u32[]{:S(2)}) collective-permute-start(bf16[128,2048]{1,0:T(8,128)(2,1)S(1)} %bitcast.27), channel_id=1, source_target_pairs={{0,64},{64,0},{1,65},{65,1},{2,66},{66,2},{3,67},{67,3},{4,68},{68... | collective-permute-start | bytes 1572872 | tf_op jit(solution)/shard_map/ppermute | solution.py:199
  53.9 17.4 %collective-permute-start.3 = (bf16[128,2048]{1,0:T(8,128)(2,1)S(1)}, bf16[128,2048]{1,0:T(8,128)(2,1)S(1)}, u32[]{:S(2)}, u32[]{:S(2)}) collective-permute-start(bf16[128,2048]{1,0:T(8,128)(2,1)S(1)} %collective-permute-done.far_ref), channel_id=1, source_target_pairs={{0,64},{64,0},{1,65},{65,1},{2,66},{66,2},{3,67},{67,3},{4,68},{68... | collective-permute-start | bytes 1572872 | tf_op jit(solution)/shard_map/ppermute | solution.py:201
  73.8 10.8 %collective-permute-start.4 = (f32[4,128,512]{2,1,0:T(8,128)S(1)}, f32[4,128,512]{2,1,0:T(8,128)S(1)}, u32[]{:S(2)}, u32[]{:S(2)}) collective-permute-start(f32[4,128,512]{2,1,0:T(8,128)S(1)} %get-tuple-element.12), channel_id=1, source_target_pairs={{0,1},{1,0},{2,3},{3,2},{4,5},{5,4},{6,7},{7,6},{8,9},{9,8},{10,11... | collective-permute-start | bytes 3145736 | tf_op jit(solution)/shard_map/ppermute | solution.py:213
  82.8 4.6 %collective-permute-start.1 = (f32[4,128,512]{2,1,0:T(8,128)S(1)}, f32[4,128,512]{2,1,0:T(8,128)S(1)}, u32[]{:S(2)}, u32[]{:S(2)}) collective-permute-start(f32[4,128,512]{2,1,0:T(8,128)S(1)} %get-tuple-element.10), channel_id=1, source_target_pairs={{0,1},{1,0},{2,3},{3,2},{4,5},{5,4},{6,7},{7,6},{8,9},{9,8},{10,11... | collective-permute-start | bytes 3145736 | tf_op jit(solution)/shard_map/ppermute | solution.py:213
  88.4 21.1 %all-to-all-start.1 = ((bf16[8,2,64,512]{3,2,1,0:T(8,128)(2,1)}), bf16[8,2,64,512]{3,2,1,0:T(8,128)(2,1)S(1)}, u32[]{:S(2)}, u32[]{:S(2)}) async-start(bf16[8,2,64,512]{3,2,1,0:T(8,128)(2,1)} %shard_map.77), calls=%async_computation.1 | async-start | bytes 2097152 | tf_op jit(solution)/shard_map/all_to_all | solution.py:214

commit v8 on v6

--- a/solution.py
+++ b/solution.py
@@ -30,6 +30,35 @@
         preferred_element_type=jnp.float32,
     )
     return jnp.sum(jnp.where(low, picked, 0.0), axis=1)
+
+
+def repeat_kernel(source_ref, out_ref, block_ref, sems):
+    fetch = pltpu.make_async_copy(source_ref, block_ref, sems.at[0])
+    fetch.start()
+    fetch.wait()
+    copies = [
+        pltpu.make_async_copy(block_ref, out_ref.at[at], sems.at[at])
+        for at in range(out_ref.shape[0])
+    ]
+    for copy in copies:
+        copy.start()
+    for copy in copies:
+        copy.wait()
+
+
+def repeat(block, times):
+    return pl.pallas_call(
+        repeat_kernel,
+        in_specs=[pl.BlockSpec(memory_space=pltpu.HBM)],
+        out_specs=pl.BlockSpec(memory_space=pltpu.HBM),
+        out_shape=jax.ShapeDtypeStruct((times,) + block.shape, block.dtype),
+        scratch_shapes=[
+            pltpu.VMEM(block.shape, block.dtype),
+            pltpu.SemaphoreType.DMA((times,)),
+        ],
+        compiler_params=pltpu.CompilerParams(vmem_limit_bytes=60 * 1024 * 1024),
+        cost_estimate=SMALL,
+    )(block)
 
 
 def scale_kernel(coeffs_ref, response_ref, out_ref):
@@ -155,7 +184,7 @@
     rows = jnp.where(core == 0, jnp.stack([second, first]), jnp.stack([first, second]))
     rows = rows.reshape(ROWS_DEV, depth)
 
-    coeffs_y = jnp.broadcast_to(coeffs[None], (n_y, aux_local, depth))
+    coeffs_y = repeat(coeffs, n_y)
     coeffs_y = lax.all_to_all(coeffs_y, "y", 0, 0, tiled=True)
 
     gathered = lax.all_gather(rows, "half_z", axis=0)

time: 107 us -> 107 us (level)
  local copies, waits for them, and re-layouts: 5.04 us -> 1.33 us
  Pallas kernels: 11.6 us -> 14.8 us
    broadcast_in_dim x1 -> x0, local copies, waits for them, and re-layouts: 3.73 us -> none  [on_device(): coeffs_y = jnp.broadcast_to(coeffs[None], (n_y, aux_local, depth))]
    pallas_call x0 -> x1, Pallas kernels: none -> 3.23 us  [repeat(): pl.pallas_call(repeat_kernel, in_specs=[pl.BlockSpec(memory_space=pltpu.H...]
where the time goes in v8:
time: 107 us; the launch traced here: 106 us
  starting transfers between devices  35.6 us (33%)
  blocking collectives  33.1 us (31%)
  waiting for transfers between devices  17.4 us (16%)
  Pallas kernels  14.8 us (14%)
  matrix products  2.87 us (3%)
  local copies, waits for them, and re-layouts  1.33 us (1%)
    all_gather x1, blocking collectives, on_device(): gathered = lax.all_gather(rows, 'half_z', axis=0)  33.1 us
    all_to_all x1, waiting for transfers between devices, on_device(): parts = lax.all_to_all(add_cores(*sides), ('y', 'x_lo'), 0, 0, tiled=True)  15.1 us
    ppermute x2, starting transfers between devices, on_device(): sides.append((kept, lax.ppermute(away, 'core', swap)))  12.8 us
    all_to_all x1, starting transfers between devices, on_device(): parts = lax.all_to_all(add_cores(*sides), ('y', 'x_lo'), 0, 0, tiled=True)  5.72 us
    pallas_call x2, Pallas kernels, products(): pl.pallas_call(product_kernel, grid=(n_y // 2,), in_specs=[rows, rows, pl...  5.2 us
    all_to_all x1, starting transfers between devices, on_device(): coeffs_y = lax.all_to_all(coeffs_y, 'y', 0, 0, tiled=True)  5.16 us
    ppermute x1, starting transfers between devices, on_device(): near_partner = lax.ppermute(near, 'x_hi', swap)  4.65 us
    ppermute x1, starting transfers between devices, on_device(): far_partner = lax.ppermute(far, 'x_hi', swap)  4.52 us
  transfers between devices with their start and end apart: 7, of which 2 were waited for; matrix products, arithmetic and copies ran while one was open for 4% of the time, Pallas kernels for 8%

profile of v8, /device:TPU:1, one launch (start us, length us, event | category | flops | bytes accessed | tf_op | source)
XLA Modules:
  0.0 106.2 jit_solution(11155111239356487229)
XLA Ops:
  0.0 3.2 %shard_map.73 = bf16[4,256,2048]{2,1,0:T(8,128)(2,1)} custom-call(bf16[256,2048]{1,0:T(8,128)(2,1)} %source_ref.1), custom_call_target="tpu_custom_call" | custom-call | flops 1 | bytes 1 | tf_op jit(solution)/shard_map/pallas_call | solution.py:50
  3.2 0.0 copy-start
  3.2 0.0 copy-start.3
  3.3 0.0 copy-start.1
  3.3 0.0 copy-start.2
  3.3 5.2 %all-to-all-start = ((bf16[4,256,2048]{2,1,0:T(8,128)(2,1)}), bf16[4,256,2048]{2,1,0:T(8,128)(2,1)}, u32[]{:S(2)}, u32[]{:S(2)}) async-start(bf16[4,256,2048]{2,1,0:T(8,128)(2,1)} %shard_map.73), calls=%async_computation | async-start | bytes 8388608 | tf_op jit(solution)/shard_map/all_to_all | solution.py:188
  9.1 0.9 constant_dynamic-slice_fusion
  10.1 0.1 maximum_select_fusion
  10.2 33.1 %all_gather.3 = bf16[8,16,2048]{2,1,0:T(8,128)(2,1)S(1)} all-gather(bf16[1,16,2048]{2,1,0:T(8,128)(2,1)S(1)} %select_n.50), channel_id=1, replica_groups=mesh['y'=4,'x_hi'=2,'half_z'=8,'parity'=2,'x_lo'=2,'core'=2] {'half_z'}, dimensions={0}, use_global_device_ids=true | all-gather | bytes 589824 | tf_op jit(solution)/shard_map/all_gather | solution.py:190
  43.3 0.3 copy.17
  43.6 2.8 %collective-permute-start = (bf16[128,2048]{1,0:T(8,128)(2,1)S(1)}, bf16[128,2048]{1,0:T(8,128)(2,1)S(1)}, u32[]{:S(2)}, u32[]{:S(2)}) collective-permute-start(bf16[128,2048]{1,0:T(8,128)(2,1)S(1)} %bitcast.29), channel_id=1, source_target_pairs={{0,4},{4,0},{1,5},{5,1},{2,6},{6,2},{3,7},{7,3},{8,12},{12,8},{9,1... | collective-permute-start | bytes 1572872 | tf_op jit(solution)/shard_map/ppermute | solution.py:193
  46.4 4.7 %collective-permute-start.2 = (bf16[128,2048]{1,0:T(8,128)(2,1)S(1)}, bf16[128,2048]{1,0:T(8,128)(2,1)S(1)}, u32[]{:S(2)}, u32[]{:S(2)}) collective-permute-start(bf16[128,2048]{1,0:T(8,128)(2,1)S(1)} %bitcast.30), channel_id=1, source_target_pairs={{0,64},{64,0},{1,65},{65,1},{2,66},{66,2},{3,67},{67,3},{4,68},{68... | collective-permute-start | bytes 1572872 | tf_op jit(solution)/shard_map/ppermute | solution.py:192
  51.1 1.2 %fusion = f32[2048]{0:T(1024)S(1)} fusion(s32[2048]{0:T(1024)S(1)} %get-tuple-element.18, s32[2048]{0:T(1024)S(1)} %get-tuple-element.17, f32[2000]{0:T(1024)S(1)} %copy-done.3), kind=kOutput, calls=%fused_computation.3 | convolution fusion | flops 51148800 | bytes 32576 | tf_op jit(solution)/shard_map/dot_general | solution.py:25
  52.3 1.7 %fusion.1 = f32[2048]{0:T(1024)S(1)} fusion(s32[2048]{0:T(1024)S(1)} %get-tuple-element.20, s32[2048]{0:T(1024)S(1)} %get-tuple-element.19, f32[20000]{0:T(1024)S(1)} %copy-done.2), kind=kOutput, calls=%fused_computation.4 | convolution fusion | flops 504428544 | bytes 104576 | tf_op jit(solution)/shard_map/dot_general | solution.py:25
  54.0 0.0 collective-permute-done.far_ref
  54.0 4.5 %collective-permute-start.3 = (bf16[128,2048]{1,0:T(8,128)(2,1)S(1)}, bf16[128,2048]{1,0:T(8,128)(2,1)S(1)}, u32[]{:S(2)}, u32[]{:S(2)}) collective-permute-start(bf16[128,2048]{1,0:T(8,128)(2,1)S(1)} %collective-permute-done.far_ref), channel_id=1, source_target_pairs={{0,64},{64,0},{1,65},{65,1},{2,66},{66,2},{3,67},{67,3},{4,68},{68... | collective-permute-start | bytes 1572872 | tf_op jit(solution)/shard_map/ppermute | solution.py:194
  58.6 0.1 add_divide_fusion.response_ref
  58.7 0.0 all-to-all-done.coeffs_ref
  58.7 3.6 %shard_map.74.scaled_ref = bf16[4,512,2048]{2,1,0:T(8,128)(2,1)S(1)} custom-call(bf16[4,256,2048]{2,1,0:T(8,128)(2,1)} %all-to-all-done.coeffs_ref, f32[2,2048]{1,0:T(2,128)S(1)} %add_divide_fusion.response_ref), custom_call_target="tpu_custom_call" | custom-call | flops 1 | bytes 1 | tf_op jit(solution)/shard_map/pallas_call | solution.py:75
  62.3 2.6 %shard_map.75 = (f32[4,128,512]{2,1,0:T(8,128)S(1)}, f32[4,128,512]{2,1,0:T(8,128)S(1)}) custom-call(bf16[128,2048]{1,0:T(8,128)(2,1)S(1)} %bitcast.31, bf16[128,2048]{1,0:T(8,128)(2,1)S(1)} %collective-permute-done.far_ref, bf16[4,512,2048]{2,1,0:T(8,128)(2,1)S(1)} %shard_map.74.scaled_ref), custom_call_target="tpu_custom_call" | custom-call | flops 1 | bytes 1 | tf_op jit(solution)/shard_map/pallas_call | solution.py:106
  64.9 8.3 %collective-permute-start.1 = (f32[4,128,512]{2,1,0:T(8,128)S(1)}, f32[4,128,512]{2,1,0:T(8,128)S(1)}, u32[]{:S(2)}, u32[]{:S(2)}) collective-permute-start(f32[4,128,512]{2,1,0:T(8,128)S(1)} %get-tuple-element.10), channel_id=1, source_target_pairs={{0,1},{1,0},{2,3},{3,2},{4,5},{5,4},{6,7},{7,6},{8,9},{9,8},{10,11... | collective-permute-start | bytes 3145736 | tf_op jit(solution)/shard_map/ppermute | solution.py:206
  73.2 0.0 collective-permute-done.2.near_ref
  73.2 0.0 collective-permute-done.3.far_ref
  73.2 2.6 %shard_map.76 = (f32[4,128,512]{2,1,0:T(8,128)S(1)}, f32[4,128,512]{2,1,0:T(8,128)S(1)}) custom-call(bf16[128,2048]{1,0:T(8,128)(2,1)S(1)} %collective-permute-done.2.near_ref, bf16[128,2048]{1,0:T(8,128)(2,1)S(1)} %collective-permute-done.3.far_ref, bf16[4,512,2048]{2,1,0:T(8,128)(2,1)S(1)} %shard_map.74.scaled_ref), custom_call_target="tpu_custom_call" | custom-call | flops 1 | bytes 1 | tf_op jit(solution)/shard_map/pallas_call | solution.py:106
  75.9 4.5 %collective-permute-start.4 = (f32[4,128,512]{2,1,0:T(8,128)S(1)}, f32[4,128,512]{2,1,0:T(8,128)S(1)}, u32[]{:S(2)}, u32[]{:S(2)}) collective-permute-start(f32[4,128,512]{2,1,0:T(8,128)S(1)} %get-tuple-element.12), channel_id=1, source_target_pairs={{0,1},{1,0},{2,3},{3,2},{4,5},{5,4},{6,7},{7,6},{8,9},{9,8},{10,11... | collective-permute-start | bytes 3145736 | tf_op jit(solution)/shard_map/ppermute | solution.py:206
  80.3 0.0 collective-permute-done.1.refs_1_
  80.3 2.3 %collective-permute-done.4.refs_3_ = f32[4,128,512]{2,1,0:T(8,128)S(1)} collective-permute-done((f32[4,128,512]{2,1,0:T(8,128)S(1)}, f32[4,128,512]{2,1,0:T(8,128)S(1)}, u32[]{:S(2)}, u32[]{:S(2)}) %collective-permute-start.4) | collective-permute-done | bytes 1048608 | tf_op jit(solution)/shard_map/ppermute | solution.py:206
  82.6 1.1 shard_map.77
  83.6 5.7 %all-to-all-start.1 = ((bf16[8,2,64,512]{3,2,1,0:T(8,128)(2,1)}), bf16[8,2,64,512]{3,2,1,0:T(8,128)(2,1)S(1)}, u32[]{:S(2)}, u32[]{:S(2)}) async-start(bf16[8,2,64,512]{3,2,1,0:T(8,128)(2,1)} %shard_map.77), calls=%async_computation.1 | async-start | bytes 2097152 | tf_op jit(solution)/shard_map/all_to_all | solution.py:207
  89.4 0.1 pad_add_fusion.place_ref
  89.4 15.1 %all-to-all-done.1 = bf16[8,2,64,512]{3,2,1,0:T(8,128)(2,1)S(1)} async-done(((bf16[8,2,64,512]{3,2,1,0:T(8,128)(2,1)}), bf16[8,2,64,512]{3,2,1,0:T(8,128)(2,1)S(1)}, u32[]{:S(2)}, u32[]{:S(2)}) %all-to-all-start.1) | async-done | bytes 1048608 | tf_op jit(solution)/shard_map/all_to_all | solution.py:207
  104.5 1.7 %shard_map.78 = f32[2048,128]{1,0:T(8,128)} custom-call(s32[2]{0:T(128)S(1)} %pad_add_fusion.place_ref, bf16[4,2,2,2,4,8,512]{6,5,4,3,2,1,0:T(8,128)(2,1)S(1)} %bitcast.28), custom_call_target="tpu_custom_call" | custom-call | tf_op jit(solution)/shard_map/pallas_call | solution.py:155
  (13 shorter events, 0.1 us)
Async XLA Ops:
  3.2 47.8 %copy-start = (s32[2048]{0:T(1024)S(1)}, s32[2048]{0:T(1024)}, u32[]{:S(2)}) copy-start(s32[2048]{0:T(1024)} %param.8) | copy-start | bytes 24580
  3.2 47.8 %copy-start.3 = (f32[2000]{0:T(1024)S(1)}, f32[2000]{0:T(1024)}, u32[]{:S(2)}) copy-start(f32[2000]{0:T(1024)} %param.10) | copy-start | bytes 24004
  3.3 49.0 %copy-start.1 = (s32[2048]{0:T(1024)S(1)}, s32[2048]{0:T(1024)}, u32[]{:S(2)}) copy-start(s32[2048]{0:T(1024)} %param.9) | copy-start | bytes 24580
  3.3 49.0 %copy-start.2 = (f32[20000]{0:T(1024)S(1)}, f32[20000]{0:T(1024)}, u32[]{:S(2)}) copy-start(f32[20000]{0:T(1024)} %param.11) | copy-start | bytes 240004
  3.3 55.4 %all-to-all-start = ((bf16[4,256,2048]{2,1,0:T(8,128)(2,1)}), bf16[4,256,2048]{2,1,0:T(8,128)(2,1)}, u32[]{:S(2)}, u32[]{:S(2)}) async-start(bf16[4,256,2048]{2,1,0:T(8,128)(2,1)} %shard_map.73), calls=%async_computation | async-start | bytes 8388608 | tf_op jit(solution)/shard_map/all_to_all | solution.py:188
  8.4 50.1 %copy-start.4 = (f32[2]{0:T(128)S(1)}, f32[2]{0:T(128)}, u32[]{:S(2)}) copy-start(f32[2]{0:T(128)} %param.12) | copy-start | bytes 28
  43.6 10.4 %collective-permute-start = (bf16[128,2048]{1,0:T(8,128)(2,1)S(1)}, bf16[128,2048]{1,0:T(8,128)(2,1)S(1)}, u32[]{:S(2)}, u32[]{:S(2)}) collective-permute-start(bf16[128,2048]{1,0:T(8,128)(2,1)S(1)} %bitcast.29), channel_id=1, source_target_pairs={{0,4},{4,0},{1,5},{5,1},{2,6},{6,2},{3,7},{7,3},{8,12},{12,8},{9,1... | collective-permute-start | bytes 1572872 | tf_op jit(solution)/shard_map/ppermute | solution.py:193
  46.4 26.8 %collective-permute-start.2 = (bf16[128,2048]{1,0:T(8,128)(2,1)S(1)}, bf16[128,2048]{1,0:T(8,128)(2,1)S(1)}, u32[]{:S(2)}, u32[]{:S(2)}) collective-permute-start(bf16[128,2048]{1,0:T(8,128)(2,1)S(1)} %bitcast.30), channel_id=1, source_target_pairs={{0,64},{64,0},{1,65},{65,1},{2,66},{66,2},{3,67},{67,3},{4,68},{68... | collective-permute-start | bytes 1572872 | tf_op jit(solution)/shard_map/ppermute | solution.py:192
  54.0 19.2 %collective-permute-start.3 = (bf16[128,2048]{1,0:T(8,128)(2,1)S(1)}, bf16[128,2048]{1,0:T(8,128)(2,1)S(1)}, u32[]{:S(2)}, u32[]{:S(2)}) collective-permute-start(bf16[128,2048]{1,0:T(8,128)(2,1)S(1)} %collective-permute-done.far_ref), channel_id=1, source_target_pairs={{0,64},{64,0},{1,65},{65,1},{2,66},{66,2},{3,67},{67,3},{4,68},{68... | collective-permute-start | bytes 1572872 | tf_op jit(solution)/shard_map/ppermute | solution.py:194
  64.9 15.4 %collective-permute-start.1 = (f32[4,128,512]{2,1,0:T(8,128)S(1)}, f32[4,128,512]{2,1,0:T(8,128)S(1)}, u32[]{:S(2)}, u32[]{:S(2)}) collective-permute-start(f32[4,128,512]{2,1,0:T(8,128)S(1)} %get-tuple-element.10), channel_id=1, source_target_pairs={{0,1},{1,0},{2,3},{3,2},{4,5},{5,4},{6,7},{7,6},{8,9},{9,8},{10,11... | collective-permute-start | bytes 3145736 | tf_op jit(solution)/shard_map/ppermute | solution.py:206
  75.9 6.7 %collective-permute-start.4 = (f32[4,128,512]{2,1,0:T(8,128)S(1)}, f32[4,128,512]{2,1,0:T(8,128)S(1)}, u32[]{:S(2)}, u32[]{:S(2)}) collective-permute-start(f32[4,128,512]{2,1,0:T(8,128)S(1)} %get-tuple-element.12), channel_id=1, source_target_pairs={{0,1},{1,0},{2,3},{3,2},{4,5},{5,4},{6,7},{7,6},{8,9},{9,8},{10,11... | collective-permute-start | bytes 3145736 | tf_op jit(solution)/shard_map/ppermute | solution.py:206
  83.6 20.9 %all-to-all-start.1 = ((bf16[8,2,64,512]{3,2,1,0:T(8,128)(2,1)}), bf16[8,2,64,512]{3,2,1,0:T(8,128)(2,1)S(1)}, u32[]{:S(2)}, u32[]{:S(2)}) async-start(bf16[8,2,64,512]{3,2,1,0:T(8,128)(2,1)} %shard_map.77), calls=%async_computation.1 | async-start | bytes 2097152 | tf_op jit(solution)/shard_map/all_to_all | solution.py:207
